TPU v7x, 512 devices: a whole 4x8x8 slice. The times are simulated.
512 devices in a mesh: section: 16 (over z, core), tensor: 16 (over x, y_lo), dp: 2 (over y_hi).
Axes of the slice: x: 4, y: 8 (y_hi: 2, y_lo: 4; y = y_hi * 4 + y_lo), z: 8, core: 2. Of those that a mesh axis runs over, the one named last changes fastest.
Arguments:
- section_input: bfloat16 [16, 256, 4096], P('section', 'dp', 'tensor'), parts along dimension 1, may hold values from -6 to 6
- stash_pool: bfloat16 [16, 2, 256, 4096], P('section', None, 'dp', 'tensor'), parts along dimension 2, may hold values from -6 to 6
- reload_slot: int32 [16], P('section'), may hold values from 0 to 1
- cotangent: bfloat16 [16, 256, 4096], P('section', 'dp', 'tensor'), parts along dimension 1, may hold values from -6 to 6
- norm_gain: float32 [16, 4096], P('section', 'tensor'), may hold values from 0.5 to 6
- query_weight: bfloat16 [16, 4096, 4096], P('section', None, 'tensor'), may hold values from -0.09375 to 0.09375
- kv_weight: bfloat16 [16, 4096, 1024], P('section', 'tensor'), may hold values from -0.09375 to 0.09375
- out_weight: bfloat16 [16, 4096, 4096], P('section', 'tensor'), may hold values from -0.09375 to 0.09375
Outputs:
- next_input: bfloat16 [16, 256, 4096], P('section', 'dp', 'tensor'), parts along dimension 1
- received_stash: bfloat16 [16, 256, 4096], P('section', 'dp', 'tensor'), parts along dimension 1
- input_grad: bfloat16 [16, 256, 4096], P('section', 'dp', 'tensor'), parts along dimension 1
There are 2 independent parts, one for each index of `dp`. A program takes and returns all parts, laid end to end along the dimension named above; an argument that names none is the same for every part. Nothing has to cross between parts.
All inputs are finite; a program needn't handle non-finite values.
Results may differ from a plain program's by a relative error of at most 0.024.
The roundings to bfloat16 on the way count: a program that leaves them out, or rounds other values in their place, can miss the bound.
Values may be sent and summed in bfloat16 or wider, within the bound.
No kernel may reach another device: no remote copies, remote signals or barrier semaphores. Data moves between devices by JAX's collectives and lax.ppermute only.
A program may use at most 64 MiB of HBM per device.

v0:
```python
import jax
import jax.numpy as jnp
from jax import lax
from jax.sharding import PartitionSpec as P

HEADS = 32
KVH = 4
HD = 128


norm_eps = 1e-05


def passed_along(block, axis, distance):
    devices = range(lax.axis_size(axis))
    route = [(i - distance, i) for i in devices if i - distance in devices]
    return lax.ppermute(block, axis, route)


def from_partner(value, axis, distance):
    mask = 2**distance
    pairs = [(source, source ^ mask) for source in range(lax.axis_size(axis))]
    return lax.ppermute(value, axis, pairs)


def rope_tables(row_total, head_width):
    half_width = head_width // 2
    inverse = 10000.0 ** (-2.0 * jnp.arange(half_width, dtype=jnp.float32) / head_width)
    angles = jnp.arange(row_total, dtype=jnp.float32)[:, None] * inverse[None, :]
    return (jnp.cos(angles)[:, None, :], jnp.sin(angles)[:, None, :])


def rotate(values, cos_table, sin_table):
    half_width = values.shape[-1] // 2
    first_half = values[..., :half_width]
    second_half = values[..., half_width:]
    return jnp.concatenate(
        [
            first_half * cos_table - second_half * sin_table,
            second_half * cos_table + first_half * sin_table,
        ],
        axis=-1,
    )


def unrotate(values, cos_table, sin_table):
    half_width = values.shape[-1] // 2
    first_half = values[..., :half_width]
    second_half = values[..., half_width:]
    return jnp.concatenate(
        [
            first_half * cos_table + second_half * sin_table,
            second_half * cos_table - first_half * sin_table,
        ],
        axis=-1,
    )


def feature_total(partial_value):
    return lax.psum(partial_value, "tensor")


def gather_features(local_cols):
    return lax.all_gather(local_cols, "tensor", axis=1, tiled=True)


def tensor_total(partial_value):
    return lax.psum(partial_value, "tensor")


def pipe(values_out, offset):
    return passed_along(values_out, "section", offset)


def contract_last(left_side, right_side):
    return lax.dot_general(
        left_side, right_side, (((1,), (1,)), ((), ())), preferred_element_type=jnp.float32
    )


def group_kv(normed_cols, kv_w, group_index):
    token_count = normed_cols.shape[0]
    partial_value = jnp.dot(normed_cols, kv_w, preferred_element_type=jnp.float32)
    kv_all = tensor_total(partial_value).reshape(token_count, 2, KVH, HD)
    key_head = lax.dynamic_index_in_dim(kv_all[:, 0], group_index, 1, keepdims=False)
    value_head = lax.dynamic_index_in_dim(kv_all[:, 1], group_index, 1, keepdims=False)
    return (key_head, value_head)


def norm_factor(rows_wide):
    full_width = rows_wide.shape[1] * lax.axis_size("tensor")
    total = feature_total(jnp.sum(rows_wide * rows_wide, axis=-1, keepdims=True))
    return lax.rsqrt(total / full_width + norm_eps)


def local_heads(normed_cols, query_w, kv_w, cos_table, sin_table, group_index):
    gathered = gather_features(normed_cols)
    token_count = gathered.shape[0]
    key_wide, value_wide = group_kv(normed_cols, kv_w, group_index)
    key_head = rotate(key_wide[:, None, :], cos_table, sin_table).astype(jnp.bfloat16)[:, 0]
    value_head = value_wide.astype(jnp.bfloat16)
    query_heads = jnp.dot(gathered, query_w, preferred_element_type=jnp.float32).reshape(
        token_count, -1, HD
    )
    query_heads = (rotate(query_heads, cos_table, sin_table) * HD ** (-0.5)).astype(jnp.bfloat16)
    scores = jnp.einsum("thd,sd->hts", query_heads, key_head, preferred_element_type=jnp.float32)
    causal = jnp.arange(token_count)[:, None] >= jnp.arange(token_count)[None, :]
    scores = jnp.where(causal[None], scores, -1e30)
    shifted = jnp.exp(scores - jnp.max(scores, axis=-1, keepdims=True))
    softmax_probs = shifted / jnp.sum(shifted, axis=-1, keepdims=True)
    prob_weights = softmax_probs.astype(jnp.bfloat16)
    attended = jnp.einsum(
        "hts,sd->thd", prob_weights, value_head, preferred_element_type=jnp.float32
    )
    attended = attended.astype(jnp.bfloat16).reshape(token_count, -1)
    return (query_heads, key_head, value_head, softmax_probs, prob_weights, attended)


def per_device(
    section_input,
    stash_pool,
    reload_slot,
    cotangent,
    norm_gain,
    query_weight,
    kv_weight,
    out_weight,
):
    token_rows = section_input[0]
    cot_rows = cotangent[0]
    gain_row = norm_gain[0]
    query_w = query_weight[0]
    kv_w = kv_weight[0]
    out_w = out_weight[0]
    section_count = lax.axis_size("section")
    section_pos = lax.axis_index("section")
    is_early = section_pos < section_count // 2
    tensor_pos = lax.axis_index("tensor")
    local_width = token_rows.shape[1]
    column_start = tensor_pos * local_width
    heads_here = query_w.shape[1] // HD
    group_index = tensor_pos * heads_here // (HEADS // KVH)
    token_count = token_rows.shape[0]
    full_width = local_width * lax.axis_size("tensor")
    cos_table, sin_table = rope_tables(token_count, HD)
    rows_wide = token_rows.astype(jnp.float32)
    normed = (rows_wide * norm_factor(rows_wide) * gain_row).astype(jnp.bfloat16)
    attended = local_heads(normed, query_w, kv_w, cos_table, sin_table, group_index)[5]
    out_term = jnp.dot(attended, out_w, preferred_element_type=jnp.float32)
    summed = lax.psum(out_term.astype(jnp.bfloat16), "tensor").astype(jnp.float32)
    own_cols = lax.dynamic_slice_in_dim(summed, column_start, local_width, 1)
    layer_out = (rows_wide + own_cols).astype(jnp.bfloat16)
    next_input = pipe(layer_out, 1)
    picked = lax.dynamic_index_in_dim(stash_pool[0], reload_slot[0], 0, keepdims=False)
    travel = jnp.where(is_early, token_rows, picked)
    bit_count = section_count.bit_length() - 1
    for bit_index in range(bit_count):
        travel = from_partner(travel, "section", bit_index)
    back_input = jnp.where(is_early, travel, token_rows)
    back_wide = back_input.astype(jnp.float32)
    factor = norm_factor(back_wide)
    back_normed = (back_wide * factor * gain_row).astype(jnp.bfloat16)
    query_heads, key_head, value_head, softmax_probs, prob_weights, _ = local_heads(
        back_normed, query_w, kv_w, cos_table, sin_table, group_index
    )
    cot_whole = gather_features(cot_rows)
    grad_out = (
        contract_last(cot_whole, out_w).astype(jnp.bfloat16).reshape(token_count, heads_here, HD)
    )
    grad_probs = jnp.einsum("thd,sd->hts", grad_out, value_head, preferred_element_type=jnp.float32)
    row_delta = jnp.sum(softmax_probs * grad_probs, axis=-1, keepdims=True)
    grad_scores = (softmax_probs * (grad_probs - row_delta)).astype(jnp.bfloat16)
    grad_query = jnp.einsum(
        "hts,sd->thd", grad_scores, key_head, preferred_element_type=jnp.float32
    )
    grad_query = (
        (unrotate(grad_query, cos_table, sin_table) * HD ** (-0.5))
        .astype(jnp.bfloat16)
        .reshape(token_count, -1)
    )
    grad_key = jnp.einsum(
        "hts,thd->sd", grad_scores, query_heads, preferred_element_type=jnp.float32
    )
    grad_key = unrotate(grad_key[:, None, :], cos_table, sin_table)[:, 0]
    grad_value = jnp.einsum(
        "hts,thd->sd", prob_weights, grad_out, preferred_element_type=jnp.float32
    )
    placed = jnp.zeros((token_count, 2, KVH, HD), jnp.float32)
    placed = lax.dynamic_update_slice(
        placed, jnp.stack([grad_key, grad_value], axis=1)[:, :, None, :], (0, 0, group_index, 0)
    )
    grad_kv = tensor_total(placed.reshape(token_count, 2 * KVH * HD)).astype(jnp.bfloat16)
    query_cols = lax.psum_scatter(
        contract_last(grad_query, query_w).astype(jnp.bfloat16),
        "tensor",
        scatter_dimension=1,
        tiled=True,
    ).astype(jnp.float32)
    grad_normed = query_cols + contract_last(grad_kv, kv_w)
    scaled = grad_normed * gain_row
    mixed_mean = feature_total(jnp.sum(scaled * back_wide, axis=-1, keepdims=True)) / full_width
    grad_rows = factor * scaled - back_wide * factor * factor * factor * mixed_mean
    grad_local = (cot_rows.astype(jnp.float32) + grad_rows).astype(jnp.bfloat16)
    input_grad = pipe(grad_local, -1)
    return (next_input[None], travel[None], input_grad[None])


def solution(mesh):
    return jax.shard_map(
        per_device,
        mesh=mesh,
        in_specs=(
            P("section", "dp", "tensor"),
            P("section", None, "dp", "tensor"),
            P("section"),
            P("section", "dp", "tensor"),
            P("section", "tensor"),
            P("section", None, "tensor"),
            P("section", "tensor", None),
            P("section", "tensor", None),
        ),
        out_specs=(
            P("section", "dp", "tensor"),
            P("section", "dp", "tensor"),
            P("section", "dp", "tensor"),
        ),
        check_vma=False,
    )
```

profile of v0, /device:TPU:1, one launch (start us, length us, event | category | flops | bytes accessed | tf_op | source)
XLA Modules:
  0.0 972.8 jit_solution(5292058022167904860)
XLA Ops:
  8.9 8.8 collective-permute-start.1
  18.6 1.9 collective-permute-start.2
  20.5 3.1 collective-permute-done.2
  23.6 1.9 collective-permute-start.3
  25.5 4.7 collective-permute-done.3
  30.2 4.5 collective-permute-start.4
  34.7 4.4 collective-permute-done.4
  41.2 33.8 %psum.52 = f32[128,1]{0,1:T(1,128)S(1)} all-reduce(f32[128,1]{0,1:T(1,128)S(1)} %bitcast.179), channel_id=1, replica_groups=mesh['section'=16,'tensor'=16,'dp'=2] {'tensor'}, use_global_device_ids=true, to_apply=%region_7.8 | all-reduce | flops 128 | bytes 1024 | tf_op jit(solution)/shard_map/psum | solution.py:60
  79.9 4.1 copy.57
  84.3 158.2 %all-reduce.10.cloned.1.call-done = f32[128,2,4,128]{3,0,2,1:T(8,128)} async-done(((f32[128,2,4,128]{3,0,2,1:T(8,128)}), f32[128,2,4,128]{3,0,2,1:T(8,128)}) %all-reduce.10.cloned.1.call-update) | async-done | bytes 524304 | tf_op jit(solution)/shard_map/psum | solution.py:68
  244.8 73.9 %all-gather.9.cloned.1.call-done = bf16[1,128,4096]{2,1,0:T(8,128)(2,1)} async-done(((bf16[1,128,256]{2,1,0:T(8,128)(2,1)}), bf16[1,128,4096]{2,1,0:T(8,128)(2,1)}) %all-gather.9.cloned.1.call-update) | async-done | bytes 1048592 | tf_op jit(solution)/shard_map/all_gather | solution.py:64
  318.7 2.1 fusion.13
  320.9 73.5 %all-gather.7.cloned.1.call-done = bf16[128,4096]{1,0:T(8,128)(2,1)} async-done(((bf16[128,256]{1,0:T(8,128)(2,1)}), bf16[128,4096]{1,0:T(8,128)(2,1)}) %all-gather.7.cloned.1.call-update) | async-done | bytes 1048592 | tf_op jit(solution)/shard_map/all_gather | solution.py:64
  394.3 2.6 fusion.17
  397.8 3.4 convolution_convert_fusion
  402.4 82.1 %all-reduce.11 = bf16[128,1024]{0,1:T(8,128)(2,1)S(1)} all-reduce(f32[128,1024]{0,1:T(8,128)S(1)} %bitcast.164), channel_id=1, replica_groups=mesh['section'=16,'tensor'=16,'dp'=2] {'tensor'}, use_global_device_ids=true, to_apply=%region_13.14 | all-reduce | flops 131072 | bytes 786432 | tf_op jit(solution)/shard_map/psum | solution.py:68
  484.6 4.5 reduce-scatter.2.cloned.1.call-done
  490.3 33.5 %all-reduce = (f32[128,1]{0,1:T(1,128)S(1)}, f32[128,1]{0,1:T(1,128)S(1)}) all-reduce(f32[128,1]{0,1:T(1,128)} %bitcast.177, f32[128,1]{0,1:T(1,128)S(1)} %bitcast.178), channel_id=1, replica_groups=mesh['section'=16,'tensor'=16,'dp'=2] {'tensor'}, use_global_device_ids=true, to_apply=%region_1.2 | all-reduce | flops 256 | bytes 2048 | tf_op jit(solution)/shard_map/psum | solution.py:60
  526.5 171.6 %all-reduce.6.cloned.1.call-done = f32[128,2,4,128]{0,3,2,1:T(8,128)} async-done(((f32[128,2,4,128]{0,3,2,1:T(8,128)}), f32[128,2,4,128]{0,3,2,1:T(8,128)}) %all-reduce.6.cloned.1.call-update) | async-done | bytes 524304 | tf_op jit(solution)/shard_map/psum | solution.py:68
  700.5 74.2 %all-gather.5.cloned.1.call-done = bf16[128,4096]{1,0:T(8,128)(2,1)} async-done(((bf16[128,256]{1,0:T(8,128)(2,1)}), bf16[128,4096]{1,0:T(8,128)(2,1)}) %all-gather.5.cloned.1.call-update) | async-done | bytes 1048592 | tf_op jit(solution)/shard_map/all_gather | solution.py:64
  774.7 2.6 fusion.19
  779.8 11.5 %collective-permute-start.5 = (bf16[128,256]{1,0:T(8,128)(2,1)S(1)}, bf16[128,256]{1,0:T(8,128)(2,1)S(1)}, u32[]{:S(2)}, u32[]{:S(2)}) collective-permute-start(bf16[128,256]{1,0:T(8,128)(2,1)S(1)} %fusion.34), channel_id=1, source_target_pairs={{32,0},{64,32},{96,64},{128,96},{160,128},{192,160},{224,192},{256... | collective-permute-start | bytes 196616 | tf_op jit(solution)/shard_map/ppermute | solution.py:17
  791.2 157.3 %all-reduce.8.cloned.1.call-done = bf16[128,4096]{1,0:T(8,128)(2,1)} async-done(((bf16[128,4096]{1,0:T(8,128)(2,1)}), bf16[128,4096]{1,0:T(8,128)(2,1)}) %all-reduce.8.cloned.1.call-update) | async-done | bytes 1048592 | tf_op jit(solution)/shard_map/psum | solution.py:150
  949.4 13.3 %collective-permute-start = (bf16[128,256]{1,0:T(8,128)(2,1)S(1)}, bf16[128,256]{1,0:T(8,128)(2,1)S(1)}, u32[]{:S(2)}, u32[]{:S(2)}) collective-permute-start(bf16[128,256]{1,0:T(8,128)(2,1)S(1)} %fusion.38), channel_id=1, source_target_pairs={{0,32},{32,64},{64,96},{96,128},{128,160},{160,192},{192,224},{224... | collective-permute-start | bytes 196616 | tf_op jit(solution)/shard_map/ppermute | solution.py:17
  (98 shorter events, 25.8 us)
Async XLA Ops:
  7.2 311.5 %copy-start = (bf16[1,256,4096]{2,1,0:T(8,128)(2,1)S(1)}, bf16[1,256,4096]{2,1,0:T(8,128)(2,1)}, u32[]{:S(2)}) copy-start(bf16[1,256,4096]{2,1,0:T(8,128)(2,1)} %param.15) | copy-start | bytes 6291460
  7.2 235.3 %all-reduce.10.cloned.1.call-start = ((), (), s32[]{:S(2)}) async-start(), calls=%async_computation.4 | async-start | bytes 1048576 | tf_op jit(solution)/shard_map/psum | solution.py:68
  8.9 9.7 collective-permute-start.1
  18.6 5.0 collective-permute-start.2
  23.6 6.6 collective-permute-start.3
  30.2 9.0 collective-permute-start.4
  78.3 240.3 %all-gather.9.cloned.1.call-start = ((), (), s32[]{:S(2)}) async-start(), calls=%async_computation.7 | async-start | bytes 1114112 | tf_op jit(solution)/shard_map/all_gather | solution.py:64
  79.1 315.2 %all-gather.7.cloned.1.call-start = ((), (), s32[]{:S(2)}) async-start(), calls=%async_computation.5 | async-start | bytes 1114112 | tf_op jit(solution)/shard_map/all_gather | solution.py:64
  79.8 409.2 %reduce-scatter.2.cloned.1.call-start = ((), (), s32[]{:S(2)}) async-start(), calls=%async_computation.6 | async-start | bytes 1114112 | tf_op jit(solution)/shard_map/reduce_scatter | solution.py:193
  84.0 317.8 %copy-start.12 = (f32[64]{0:T(128)}, f32[64]{0:T(128)S(1)}, u32[]{:S(2)}) copy-start(f32[64]{0:T(128)S(1)} %multiply_power_fusion) | copy-start | bytes 772
  84.3 313.5 %copy-start.4 = (f32[128,64]{0,1:T(8,128)}, f32[128,64]{0,1:T(8,128)S(1)}, u32[]{:S(2)}) copy-start(f32[128,64]{0,1:T(8,128)S(1)} %get-tuple-element.20) | copy-start | bytes 98308
  84.3 313.5 %copy-start.6 = (f32[128,64]{0,1:T(8,128)}, f32[128,64]{0,1:T(8,128)S(1)}, u32[]{:S(2)}) copy-start(f32[128,64]{0,1:T(8,128)S(1)} %get-tuple-element.21) | copy-start | bytes 98308
  401.2 87.9 %copy-start.1 = (bf16[1,256,1024]{2,1,0:T(8,128)(2,1)S(1)}, bf16[1,256,1024]{2,1,0:T(8,128)(2,1)}, u32[]{:S(2)}) copy-start(bf16[1,256,1024]{2,1,0:T(8,128)(2,1)} %param.14) | copy-start | bytes 1572868
  401.2 296.9 %all-reduce.6.cloned.1.call-start = ((), (), s32[]{:S(2)}) async-start(), calls=%async_computation.1 | async-start | bytes 1048576 | tf_op jit(solution)/shard_map/psum | solution.py:68
  401.4 122.4 %copy-start.2 = (bf16[1,128,256]{2,1,0:T(8,128)(2,1)S(1)}, bf16[1,128,256]{2,1,0:T(8,128)(2,1)}, u32[]{:S(2)}) copy-start(bf16[1,128,256]{2,1,0:T(8,128)(2,1)} %param.8) | copy-start | bytes 196612
  484.5 41.2 %copy-start.11 = (f32[1,256]{1,0:T(1,128)S(1)}, f32[1,256]{1,0:T(1,128)}, u32[]{:S(2)}) copy-start(f32[1,256]{1,0:T(1,128)} %param.12) | copy-start | bytes 3076
  484.5 215.7 %copy-start.13 = (f32[64]{0:T(128)S(1)}, f32[64]{0:T(128)}, u32[]{:S(2)}) copy-start(f32[64]{0:T(128)} %copy-done.12) | copy-start | bytes 772
  525.7 249.0 %all-gather.5.cloned.1.call-start = ((), (), s32[]{:S(2)}) async-start(), calls=%async_computation.2 | async-start | bytes 1114112 | tf_op jit(solution)/shard_map/all_gather | solution.py:64
  526.5 422.0 %all-reduce.8.cloned.1.call-start = ((), (), s32[]{:S(2)}) async-start(), calls=%async_computation.3 | async-start | bytes 2097152 | tf_op jit(solution)/shard_map/psum | solution.py:150
  699.1 78.3 %copy-start.5 = (f32[128,64]{0,1:T(8,128)S(1)}, f32[128,64]{0,1:T(8,128)}, u32[]{:S(2)}) copy-start(f32[128,64]{0,1:T(8,128)} %copy-done.4) | copy-start | bytes 98308
  699.1 78.3 %copy-start.7 = (f32[128,64]{0,1:T(8,128)S(1)}, f32[128,64]{0,1:T(8,128)}, u32[]{:S(2)}) copy-start(f32[128,64]{0,1:T(8,128)} %copy-done.6) | copy-start | bytes 98308
  778.1 186.6 %copy-start.10 = (bf16[128,256]{1,0:T(8,128)(2,1)S(1)}, bf16[128,256]{1,0:T(8,128)(2,1)}, u32[]{:S(2)}) copy-start(bf16[128,256]{1,0:T(8,128)(2,1)} %copy-done.9) | copy-start | bytes 196612
  779.8 183.0 %collective-permute-start.5 = (bf16[128,256]{1,0:T(8,128)(2,1)S(1)}, bf16[128,256]{1,0:T(8,128)(2,1)S(1)}, u32[]{:S(2)}, u32[]{:S(2)}) collective-permute-start(bf16[128,256]{1,0:T(8,128)(2,1)S(1)} %fusion.34), channel_id=1, source_target_pairs={{32,0},{64,32},{96,64},{128,96},{160,128},{192,160},{224,192},{256... | collective-permute-start | bytes 196616 | tf_op jit(solution)/shard_map/ppermute | solution.py:17
  949.4 14.6 %collective-permute-start = (bf16[128,256]{1,0:T(8,128)(2,1)S(1)}, bf16[128,256]{1,0:T(8,128)(2,1)S(1)}, u32[]{:S(2)}, u32[]{:S(2)}) collective-permute-start(bf16[128,256]{1,0:T(8,128)(2,1)S(1)} %fusion.38), channel_id=1, source_target_pairs={{0,32},{32,64},{64,96},{96,128},{128,160},{160,192},{192,224},{224... | collective-permute-start | bytes 196616 | tf_op jit(solution)/shard_map/ppermute | solution.py:17
  (5 other events, 16.0 us)
Sparse Core Ops, SparseCore 0:
  78.5 163.9 all-reduce.9
  244.7 73.9 all-gather.8
  321.4 72.8 all-gather.6
  401.4 87.6 reduce-scatter.1
  525.8 172.2 all-reduce.5
  700.7 73.9 all-gather.4
  779.7 168.7 all-reduce.7
where the time goes:
time: 974 us; the launch traced here: 973 us
  waiting for transfers between devices  729 us (75%)
  blocking collectives  149 us (15%)
  starting transfers between devices  42.2 us (4%)
  matrix products  18.5 us (2%)
  between operations  15.4 us (2%)
  local copies, waits for them, and re-layouts  12.1 us (1%)
    psum x2, waiting for transfers between devices, tensor_total(): return lax.psum(partial_value, 'tensor')  330 us
    all_gather x3, waiting for transfers between devices, gather_features(): return lax.all_gather(local_cols, 'tensor', axis=1, tiled=True)  222 us
    psum x1, waiting for transfers between devices, per_device(): lax.psum(out_term.astype(jnp.bfloat16), 'tensor').astype(jnp.float32)  157 us
    psum x1, blocking collectives, tensor_total(): return lax.psum(partial_value, 'tensor')  82.1 us
    psum x2, blocking collectives, feature_total(): return lax.psum(partial_value, 'tensor')  67.3 us
    ppermute x2, starting transfers between devices, passed_along(): return lax.ppermute(block, axis, route)  24.8 us
  transfers between devices with their start and end apart: 13, of which 12 were waited for; matrix products, arithmetic and copies ran while one was open for 1% of the time, Pallas kernels for 0%

commit v1 on v0

v1 whole, which is shorter than its diff:
```python
import functools

import jax
import jax.numpy as jnp
import numpy as np
from jax import lax
from jax.experimental import pallas as pl
from jax.experimental.pallas import tpu as pltpu
from jax.sharding import PartitionSpec as P

HEADS = 32
KVH = 4
HD = 128
TOK = 128
WIDTH = 4096
COLS = 256
SIDE = 4
norm_eps = 1e-05
MIB = 1024 * 1024

ALONG_Y = [[x * SIDE + y for y in range(SIDE)] for x in range(SIDE)]
ALONG_X = [[x * SIDE + y for x in range(SIDE)] for y in range(SIDE)]

NN = (((1,), (0,)), ((), ()))
NT = (((1,), (1,)), ((), ()))
TN = (((0,), (0,)), ((), ()))


def rope_angles():
    inverse = 10000.0 ** (-2.0 * np.arange(HD // 2, dtype=np.float64) / HD)
    angles = np.arange(TOK, dtype=np.float64)[:, None] * inverse[None, :]
    return np.cos(angles).astype(np.float32), np.sin(angles).astype(np.float32)


def matmul(left, right, dims):
    return lax.dot_general(left, right, dims, preferred_element_type=jnp.float32)


def exchange(blocks, groups):
    return lax.all_to_all(blocks, "tensor", 0, 0, axis_index_groups=groups)


def call(kernel, outs, *operands, vmem=32, flops=0):
    nbytes = sum(int(np.prod(a.shape)) * a.dtype.itemsize for a in (*operands, *outs))
    return pl.pallas_call(
        kernel,
        out_shape=outs,
        compiler_params=pltpu.CompilerParams(vmem_limit_bytes=vmem * MIB),
        cost_estimate=pl.CostEstimate(flops=flops, bytes_accessed=nbytes, transcendentals=0),
    )(*operands)


def shape(dims, dtype=jnp.bfloat16):
    return jax.ShapeDtypeStruct(dims, dtype)


def pack_kv_weight(w_ref, out_ref):
    for x in range(SIDE):
        keys = w_ref[:, x * HD : (x + 1) * HD].T
        values = w_ref[:, (KVH + x) * HD : (KVH + x + 1) * HD].T
        for y in range(SIDE):
            out_ref[x * SIDE + y, 0:16] = keys[16 * y : 16 * y + 16]
            out_ref[x * SIDE + y, 16:32] = keys[64 + 16 * y : 80 + 16 * y]
            out_ref[x * SIDE + y, 32:64] = values[32 * y : 32 * y + 32]


def norm_and_kv(rows_ref, kvw_ref, cos_ref, sin_ref, normed_ref, kv_ref, raw_ref, factor_ref):
    total = jnp.zeros((2 * TOK, 1), jnp.float32)
    for x in range(SIDE):
        for y in range(SIDE):
            block = rows_ref[x, y * 384 : y * 384 + 256].astype(jnp.float32)
            total = total + jnp.sum(block * block, axis=1, keepdims=True)
    factor = lax.rsqrt(total / WIDTH + norm_eps)
    factor_ref[...] = jnp.broadcast_to(factor[TOK:], (TOK, HD))
    kv = jnp.zeros((64, 2 * TOK), jnp.float32)
    for x in range(SIDE):
        gains = rows_ref[x, 1536:1552].astype(jnp.float32)
        for y in range(SIDE):
            gain = gains[3 * y : 3 * y + 1] + gains[3 * y + 1 : 3 * y + 2] + gains[3 * y + 2 : 3 * y + 3]
            block = rows_ref[x, y * 384 : y * 384 + 256].astype(jnp.float32)
            normed = (block * factor * gain).astype(jnp.bfloat16)
            normed_ref[x * SIDE + y] = normed
            kv = kv + matmul(kvw_ref[x * SIDE + y], normed, NT)
    raw_ref[...] = kv[:, TOK:]
    first, second = kv[0:16], kv[16:32]
    cos, sin = cos_ref[...], sin_ref[...]
    out = jnp.concatenate([first * cos - second * sin, second * cos + first * sin, kv[32:64]], axis=0)
    out = out.astype(jnp.bfloat16)
    for y in range(SIDE):
        kv_ref[y] = out


def attention(
    rows_ref, normed_ref, kv_ref, qw_ref, ow_ref, cos_ref, sin_ref, cost_ref, sint_ref,
    attended_ref, grad_query_ref, grad_kv_ref, mixed_ref,
):
    query = jnp.zeros((2 * TOK, COLS), jnp.float32)
    grad_out = jnp.zeros((TOK, COLS), jnp.float32)
    for x in range(SIDE):
        for y in range(SIDE):
            t = x * SIDE + y
            query = query + matmul(normed_ref[t], qw_ref[t * COLS : (t + 1) * COLS], NN)
            cot = rows_ref[x, y * 384 + 256 : y * 384 + 384]
            grad_out = grad_out + matmul(cot, ow_ref[:, t * COLS : (t + 1) * COLS], NT)
    grad_out = grad_out.astype(jnp.bfloat16)
    kv = [kv_ref[y] for y in range(SIDE)]
    cos, sin = cos_ref[...], sin_ref[...]
    scale = HD ** (-0.5)
    causal = lax.broadcasted_iota(jnp.int32, (TOK, TOK), 0) >= lax.broadcasted_iota(
        jnp.int32, (TOK, TOK), 1
    )

    def softmax(scores):
        scores = jnp.where(causal, scores, -1e30)
        shifted = jnp.exp(scores - jnp.max(scores, axis=-1, keepdims=True))
        return shifted / jnp.sum(shifted, axis=-1, keepdims=True)

    def keys_values(start):
        part = [k[:, start : start + TOK] for k in kv]
        keys = jnp.concatenate([p[0:16] for p in part] + [p[16:32] for p in part], axis=0)
        return keys, jnp.concatenate([p[32:64] for p in part], axis=0)

    def heads(start, h):
        raw = query[start : start + TOK, h * HD : (h + 1) * HD]
        turned = raw * cos + pltpu.roll(raw, HD // 2, 1) * sin
        return raw, (turned * scale).astype(jnp.bfloat16)

    keys, values = keys_values(0)
    for h in range(2):
        _, query_head = heads(0, h)
        weights = softmax(matmul(query_head, keys, NN)).astype(jnp.bfloat16)
        attended_ref[:, h * HD : (h + 1) * HD] = matmul(weights, values, NT).astype(jnp.bfloat16)

    keys, values = keys_values(TOK)
    grad_key = jnp.zeros((HD, TOK), jnp.float32)
    grad_value = jnp.zeros((HD, TOK), jnp.float32)
    mixed = jnp.zeros((TOK, HD), jnp.float32)
    for h in range(2):
        raw, query_head = heads(TOK, h)
        probs = softmax(matmul(query_head, keys, NN))
        grad_head = grad_out[:, h * HD : (h + 1) * HD]
        grad_probs = matmul(grad_head, values, NN)
        delta = jnp.sum(probs * grad_probs, axis=-1, keepdims=True)
        grad_scores = (probs * (grad_probs - delta)).astype(jnp.bfloat16)
        turned = matmul(grad_scores, keys, NT)
        grad_query = (turned * cos - pltpu.roll(turned, HD // 2, 1) * sin) * scale
        grad_query = grad_query.astype(jnp.bfloat16)
        grad_query_ref[:, h * HD : (h + 1) * HD] = grad_query
        mixed = mixed + grad_query.astype(jnp.float32) * raw
        grad_key = grad_key + matmul(query_head, grad_scores, TN)
        grad_value = grad_value + matmul(grad_head, probs.astype(jnp.bfloat16), TN)
    cost, sint = cost_ref[...], sint_ref[...]
    first, second = grad_key[:64], grad_key[64:]
    key_first = first * cost + second * sint
    key_second = second * cost - first * sint
    for y in range(SIDE):
        grad_kv_ref[y, 0:16] = key_first[16 * y : 16 * y + 16]
        grad_kv_ref[y, 16:32] = key_second[16 * y : 16 * y + 16]
        grad_kv_ref[y, 32:64] = grad_value[32 * y : 32 * y + 32]
    mixed_ref[...] = jnp.broadcast_to(jnp.sum(mixed.T, axis=0, keepdims=True), (8, TOK))


def split_rows(total):
    high = total.astype(jnp.bfloat16)
    low = (total - high.astype(jnp.float32)).astype(jnp.bfloat16)
    row = lax.broadcasted_iota(jnp.int32, (16, TOK), 0)
    both = jnp.where(row == 0, high.astype(jnp.float32), low.astype(jnp.float32))
    both = jnp.where(row < 2, both, 0.0)
    return jnp.concatenate([both, jnp.zeros((16, COLS - TOK), jnp.float32)], axis=1).astype(jnp.bfloat16)


def project(attended_ref, grad_query_ref, grad_kv_ref, raw_ref, mixed_ref, qw_ref, ow_ref, kvw_ref, out_ref):
    attended = attended_ref[...]
    grad_query = grad_query_ref[...]
    grad_kv = grad_kv_ref[0] + grad_kv_ref[1] + grad_kv_ref[2] + grad_kv_ref[3]
    grad_kv = grad_kv.astype(jnp.bfloat16)
    mixed = mixed_ref[0:1] + jnp.sum(grad_kv.astype(jnp.float32) * raw_ref[...], axis=0, keepdims=True)
    rows = split_rows(mixed)
    for x in range(SIDE):
        for y in range(SIDE):
            t = x * SIDE + y
            term = matmul(attended, ow_ref[:, t * COLS : (t + 1) * COLS], NN)
            out_ref[x, y * 256 : y * 256 + TOK] = term.astype(jnp.bfloat16)
            term = matmul(grad_query, qw_ref[t * COLS : (t + 1) * COLS], NT)
            term = term + matmul(grad_kv, kvw_ref[t], TN)
            out_ref[x, y * 256 + TOK : y * 256 + 256] = term.astype(jnp.bfloat16)
        out_ref[x, 1024:1040] = rows


def sum_x(parts_ref, out_ref):
    rows = parts_ref[0, 1024:1040].astype(jnp.float32)
    for x in range(1, SIDE):
        rows = rows + parts_ref[x, 1024:1040].astype(jnp.float32)
    mixed = split_rows(rows[0:1, :TOK] + rows[1:2, :TOK])
    for y in range(SIDE):
        total = parts_ref[0, y * 256 : y * 256 + 256].astype(jnp.float32)
        for x in range(1, SIDE):
            total = total + parts_ref[x, y * 256 : y * 256 + 256].astype(jnp.float32)
        out_ref[y, 0:256] = total.astype(jnp.bfloat16)
        out_ref[y, 256:272] = mixed


def finish(parts_ref, rows_ref, back_ref, cot_ref, gain_ref, factor_ref, out_ref, grad_ref):
    total = parts_ref[0].astype(jnp.float32)
    for y in range(1, SIDE):
        total = total + parts_ref[y].astype(jnp.float32)
    out_ref[...] = (rows_ref[...].astype(jnp.float32) + total[0:TOK]).astype(jnp.bfloat16)
    mixed = jnp.broadcast_to(total[256:257, :TOK] + total[257:258, :TOK], (TOK, TOK)).T[:, 0:1]
    factor = factor_ref[:, 0:1]
    scaled = total[TOK : 2 * TOK] * gain_ref[...]
    grad_rows = factor * scaled - back_ref[...].astype(jnp.float32) * (factor * factor * mixed / WIDTH)
    grad_ref[...] = (cot_ref[...].astype(jnp.float32) + grad_rows).astype(jnp.bfloat16)


def per_device(
    section_input,
    stash_pool,
    reload_slot,
    cotangent,
    norm_gain,
    query_weight,
    kv_weight,
    out_weight,
):
    token_rows = section_input[0]
    cot_rows = cotangent[0]
    query_w = query_weight[0]
    kv_w = kv_weight[0]
    out_w = out_weight[0]
    section_count = lax.axis_size("section")
    section_pos = lax.axis_index("section")
    is_early = section_pos < section_count // 2
    y_pos = lax.axis_index("tensor") % SIDE

    picked = lax.dynamic_index_in_dim(stash_pool[0], reload_slot[0], 0, keepdims=False)
    sending = jnp.where(is_early, token_rows, picked)
    mirrored = [(s, section_count - 1 - s) for s in range(section_count)]
    received = lax.ppermute(sending, "section", mirrored)
    back_rows = jnp.where(is_early, received, token_rows)

    packed = call(pack_kv_weight, (shape((16, 64, COLS)),), kv_w)[0]
    kv_rows = lax.all_to_all(packed, "tensor", 0, 0)

    gain_row = norm_gain
    high = lax.reduce_precision(gain_row, 8, 7)
    middle = lax.reduce_precision(gain_row - high, 8, 7)
    low = gain_row - high - middle
    gains = jnp.concatenate([high, middle, low, jnp.zeros((13, COLS), jnp.float32)], axis=0)
    own = jnp.concatenate([token_rows, back_rows, cot_rows, gains.astype(jnp.bfloat16)], axis=0)
    column = exchange(jnp.broadcast_to(own[None], (SIDE,) + own.shape), ALONG_Y)
    gains = jnp.concatenate(
        [column[:, 384:387].reshape(12, COLS), jnp.zeros((4, COLS), jnp.bfloat16)], axis=0
    )
    column = jnp.concatenate([column[:, :384].reshape(1536, COLS), gains], axis=0)
    rows = exchange(jnp.broadcast_to(column[None], (SIDE,) + column.shape), ALONG_X)

    cos, sin = rope_angles()
    cos_cols, sin_cols = jnp.asarray(cos.T.copy()), jnp.asarray(sin.T.copy())
    wide = np.concatenate([cos, cos], axis=1), np.concatenate([-sin, sin], axis=1)
    cos_wide, sin_wide = jnp.asarray(wide[0]), jnp.asarray(wide[1])
    cos_own = jnp.tile(lax.dynamic_slice_in_dim(cos_cols, 16 * y_pos, 16, 0), (1, 2))
    sin_own = jnp.tile(lax.dynamic_slice_in_dim(sin_cols, 16 * y_pos, 16, 0), (1, 2))
    normed, kv_own, kv_raw, factor = call(
        norm_and_kv,
        (
            shape((16, 2 * TOK, COLS)),
            shape((SIDE, 64, 2 * TOK)),
            shape((64, TOK), jnp.float32),
            shape((TOK, HD), jnp.float32),
        ),
        rows, kv_rows, cos_own, sin_own,
        flops=2 * 64 * 256 * 4096,
    )
    kv_all = exchange(kv_own, ALONG_Y)
    attended, grad_query, grad_kv, mixed = call(
        attention,
        (
            shape((TOK, COLS)),
            shape((TOK, COLS)),
            shape((SIDE, 64, TOK), jnp.float32),
            shape((8, TOK), jnp.float32),
        ),
        rows, normed, kv_all, query_w, out_w, cos_wide, sin_wide, cos_cols, sin_cols,
        flops=2 * 384 * 256 * 4096,
    )
    grad_kv = exchange(grad_kv, ALONG_Y)
    terms = call(
        project,
        (shape((SIDE, 1040, COLS)),),
        attended, grad_query, grad_kv, kv_raw, mixed, query_w, out_w, kv_rows,
        flops=2 * 256 * 256 * 4096,
    )[0]
    terms = exchange(terms, ALONG_X)
    terms = call(sum_x, (shape((SIDE, 272, COLS)),), terms)[0]
    terms = exchange(terms, ALONG_Y)
    layer_out, grad_local = call(
        finish,
        (shape((TOK, COLS)), shape((TOK, COLS))),
        terms, token_rows, back_rows, cot_rows, gain_row, factor,
    )
    next_input = lax.ppermute(layer_out, "section", [(s, s + 1) for s in range(section_count - 1)])
    input_grad = lax.ppermute(grad_local, "section", [(s + 1, s) for s in range(section_count - 1)])
    return (next_input[None], received[None], input_grad[None])


def solution(mesh):
    return jax.shard_map(
        per_device,
        mesh=mesh,
        in_specs=(
            P("section", "dp", "tensor"),
            P("section", None, "dp", "tensor"),
            P("section"),
            P("section", "dp", "tensor"),
            P("section", "tensor"),
            P("section", None, "tensor"),
            P("section", "tensor", None),
            P("section", "tensor", None),
        ),
        out_specs=(
            P("section", "dp", "tensor"),
            P("section", "dp", "tensor"),
            P("section", "dp", "tensor"),
        ),
        check_vma=False,
    )
```

time: 974 us -> 185 us (0.19)
  waiting for transfers between devices: 729 us -> 77 us
  blocking collectives: 149 us -> 50.5 us
  matrix products: 18.5 us -> 0 us
  between operations: 15.4 us -> 1.58 us
    psum x3 -> x0, waiting for transfers between devices: 487 us -> none  [the longest x2 330 us: tensor_total(): return lax.psum(partial_value, 'tensor')]
    all_gather x3 -> x0, waiting for transfers between devices: 222 us -> none  [gather_features(): return lax.all_gather(local_cols, 'tensor', axis=1, tiled=True)]
    psum x3 -> x0, blocking collectives: 149 us -> none  [the longest x1 82.1 us: tensor_total(): return lax.psum(partial_value, 'tensor')]
    all_to_all x0 -> x3, waiting for transfers between devices: none -> 70.7 us  [the longest x2 55.4 us: exchange(): return lax.all_to_all(blocks, 'tensor', 0, 0, axis_index_groups=groups)]
    all_to_all x0 -> x4, blocking collectives: none -> 50.5 us  [exchange(): return lax.all_to_all(blocks, 'tensor', 0, 0, axis_index_groups=groups)]
    ppermute x6 -> x3, starting transfers between devices: 42 us -> 22.9 us  [the longest x1 12.1 us: per_device(): received = lax.ppermute(sending, 'section', mirrored)]
    dot_general x13 -> x0, matrix products: 16.1 us -> none  [the longest x3 6.72 us: contract_last(): lax.dot_general(left_side, right_side, (((1,), (1,)), ((), ())), preferre...]
    all_to_all x0 -> x3, starting transfers between devices: none -> 13.3 us  [the longest x2 8.42 us: exchange(): return lax.all_to_all(blocks, 'tensor', 0, 0, axis_index_groups=groups)]
  transfers between devices with their start and end apart: 13 -> 6, of which waited for: 12 -> 5; matrix products, arithmetic and copies ran while one was open for 1% -> 1% of each run, Pallas kernels for 0% -> 1%
where the time goes in v1:
time: 185 us; the launch traced here: 184 us
  waiting for transfers between devices  77 us (42%)
  blocking collectives  50.5 us (27%)
  starting transfers between devices  36.2 us (20%)
  local copies, waits for them, and re-layouts  9.71 us (5%)
  Pallas kernels  6.32 us (3%)
  other arithmetic  2.42 us (1%)
    all_to_all x2, waiting for transfers between devices, exchange(): return lax.all_to_all(blocks, 'tensor', 0, 0, axis_index_groups=groups)  55.4 us
    all_to_all x4, blocking collectives, exchange(): return lax.all_to_all(blocks, 'tensor', 0, 0, axis_index_groups=groups)  50.5 us
    all_to_all x1, waiting for transfers between devices, per_device(): kv_rows = lax.all_to_all(packed, 'tensor', 0, 0)  15.4 us
    ppermute x1, starting transfers between devices, per_device(): received = lax.ppermute(sending, 'section', mirrored)  12.1 us
    ppermute x1, starting transfers between devices, per_device(): lax.ppermute(layer_out, 'section', [(s, s + 1) for s in range(section_cou...  8.9 us
    all_to_all x2, starting transfers between devices, exchange(): return lax.all_to_all(blocks, 'tensor', 0, 0, axis_index_groups=groups)  8.42 us
    pallas_call x6, Pallas kernels, call(): pl.pallas_call(kernel, out_shape=outs, compiler_params=pltpu.CompilerPara...  6.32 us
    all_to_all x1, starting transfers between devices, per_device(): kv_rows = lax.all_to_all(packed, 'tensor', 0, 0)  4.87 us
  transfers between devices with their start and end apart: 6, of which 5 were waited for; matrix products, arithmetic and copies ran while one was open for 1% of the time, Pallas kernels for 1%

profile of v1, /device:TPU:1, one launch (start us, length us, event | category | flops | bytes accessed | tf_op | source)
XLA Modules:
  0.0 183.7 jit_solution(12712441244117074934)
XLA Ops:
  2.2 12.1 %collective-permute-start = (bf16[128,256]{1,0:T(8,128)(2,1)S(1)}, bf16[128,256]{1,0:T(8,128)(2,1)S(1)}, u32[]{:S(2)}, u32[]{:S(2)}) collective-permute-start(bf16[128,256]{1,0:T(8,128)(2,1)S(1)} %bitcast_select_fusion), channel_id=1, source_target_pairs={{0,480},{32,448},{64,416},{96,384},{128,352},{160,320},{192,288},{... | collective-permute-start | bytes 196616 | tf_op jit(solution)/shard_map/ppermute | solution.py:238
  15.0 2.6 %collective-permute-done = bf16[128,256]{1,0:T(8,128)(2,1)S(1)} collective-permute-done((bf16[128,256]{1,0:T(8,128)(2,1)S(1)}, bf16[128,256]{1,0:T(8,128)(2,1)S(1)}, u32[]{:S(2)}, u32[]{:S(2)}) %collective-permute-start) | collective-permute-done | bytes 65568 | tf_op jit(solution)/shard_map/ppermute | solution.py:238
  18.5 1.8 %concatenate.9 = bf16[400,256]{1,0:T(8,128)(2,1)S(1)} concatenate(bf16[128,256]{1,0:T(8,128)(2,1)} %bitcast.29, bf16[128,256]{1,0:T(8,128)(2,1)S(1)} %broadcast_select_fusion.back_ref, bf16[128,256]{1,0:T(8,128)(2,1)} %bitcast.32, bf16[1,256]{1,0:T(2,128)(2,1)S(1)} %get-tuple-element.24, bf16[1,256]{1,0:T(2,128)(2,1)S(1)} %get-tuple-element.25, ...), dimensions={0} | concatenate | bytes 409600 | tf_op jit(solution)/shard_map/concatenate | solution.py:249
  20.3 1.0 broadcast_in_dim.28
  21.3 4.6 %all-to-all-start = ((bf16[4,400,256]{2,1,0:T(8,128)(2,1)}), bf16[4,400,256]{2,1,0:T(8,128)(2,1)S(1)}, u32[]{:S(2)}, u32[]{:S(2)}) async-start(bf16[4,400,256]{2,1,0:T(8,128)(2,1)} %broadcast_in_dim.28), calls=%async_computation | async-start | bytes 1638400 | tf_op jit(solution)/shard_map/all_to_all | solution.py:40
  25.9 1.0 shard_map.139
  26.9 19.3 %all-to-all-done = bf16[4,400,256]{2,1,0:T(8,128)(2,1)S(1)} async-done(((bf16[4,400,256]{2,1,0:T(8,128)(2,1)}), bf16[4,400,256]{2,1,0:T(8,128)(2,1)S(1)}, u32[]{:S(2)}, u32[]{:S(2)}) %all-to-all-start) | async-done | bytes 819232 | tf_op jit(solution)/shard_map/all_to_all | solution.py:40
  46.2 4.9 %all-to-all-start.2 = ((bf16[16,64,256]{2,1,0:T(8,128)(2,1)}), bf16[16,64,256]{2,1,0:T(8,128)(2,1)S(1)}, u32[]{:S(2)}, u32[]{:S(2)}) async-start(bf16[16,64,256]{2,1,0:T(8,128)(2,1)} %shard_map.139), calls=%async_computation.2 | async-start | bytes 1048576 | tf_op jit(solution)/shard_map/all_to_all | solution.py:242
  51.5 15.4 %all-to-all-done.2.kvw_ref = bf16[16,64,256]{2,1,0:T(8,128)(2,1)S(1)} async-done(((bf16[16,64,256]{2,1,0:T(8,128)(2,1)}), bf16[16,64,256]{2,1,0:T(8,128)(2,1)S(1)}, u32[]{:S(2)}, u32[]{:S(2)}) %all-to-all-start.2) | async-done | bytes 524320 | tf_op jit(solution)/shard_map/all_to_all | solution.py:242
  66.8 1.8 %broadcast_in_dim.30 = bf16[4,1552,256]{2,1,0:T(8,128)(2,1)} broadcast(bf16[1552,256]{1,0:T(8,128)(2,1)S(1)} %concatenate.10), dimensions={1,2} | broadcast | bytes 3973120 | tf_op jit(solution)/shard_map/broadcast_in_dim | solution.py:255
  68.7 3.8 %all-to-all-start.1 = ((bf16[4,1552,256]{2,1,0:T(8,128)(2,1)}), bf16[4,1552,256]{2,1,0:T(8,128)(2,1)S(1)}, u32[]{:S(2)}, u32[]{:S(2)}) async-start(bf16[4,1552,256]{2,1,0:T(8,128)(2,1)} %broadcast_in_dim.30), calls=%async_computation.1 | async-start | bytes 6356992 | tf_op jit(solution)/shard_map/all_to_all | solution.py:40
  72.6 36.0 %all-to-all-done.1.rows_ref = bf16[4,1552,256]{2,1,0:T(8,128)(2,1)S(1)} async-done(((bf16[4,1552,256]{2,1,0:T(8,128)(2,1)}), bf16[4,1552,256]{2,1,0:T(8,128)(2,1)S(1)}, u32[]{:S(2)}, u32[]{:S(2)}) %all-to-all-start.1) | async-done | bytes 3178528 | tf_op jit(solution)/shard_map/all_to_all | solution.py:40
  108.7 1.2 copy-done.4
  109.9 1.4 shard_map.140
  111.2 7.2 %all_to_all.35.kv_ref = bf16[4,64,256]{2,1,0:T(8,128)(2,1)S(1)} all-to-all(bf16[4,64,256]{2,1,0:T(8,128)(2,1)S(1)} %get-tuple-element.14), channel_id=1, replica_groups={{0,2,4,6},{8,10,12,14},{16,18,20,22},{24,26,28,30},{1,3,5,7},{9,11,13,1..., dimensions={0} | all-to-all | bytes 262144 | tf_op jit(solution)/shard_map/all_to_all | solution.py:40
  118.4 1.6 copy-done.1
  120.0 2.1 %shard_map.141 = (bf16[128,256]{1,0:T(8,128)(2,1)S(1)}, bf16[128,256]{1,0:T(8,128)(2,1)S(1)}, f32[4,64,128]{2,1,0:T(8,128)S(1)}, f32[8,128]{1,0:T(8,128)S(1)}) custom-call(bf16[4,1552,256]{2,1,0:T(8,128)(2,1)S(1)} %all-to-all-done.1.rows_ref, bf16[16,256,256]{2,1,0:T(8,128)(2,1)S(1)} %get-tuple-element.13.normed_ref, ...), custom_call_target="tpu_custom_call" | custom-call | flops 805306368 | bytes 10063872 | tf_op jit(solution)/shard_map/pallas_call | solution.py:45
  122.1 7.2 %all_to_all.36.grad_kv_ref = f32[4,64,128]{2,1,0:T(8,128)S(1)} all-to-all(f32[4,64,128]{2,1,0:T(8,128)S(1)} %get-tuple-element.17), channel_id=1, replica_groups={{0,2,4,6},{8,10,12,14},{16,18,20,22},{24,26,28,30},{1,3,5,7},{9,11,13,1..., dimensions={0} | all-to-all | bytes 262144 | tf_op jit(solution)/shard_map/all_to_all | solution.py:40
  129.2 1.4 shard_map.142
  130.7 23.8 %all_to_all.37.parts_ref = bf16[4,1040,256]{2,1,0:T(8,128)(2,1)S(1)} all-to-all(bf16[4,1040,256]{2,1,0:T(8,128)(2,1)S(1)} %shard_map.142), channel_id=1, replica_groups={{0,8,16,24},{2,10,18,26},{4,12,20,28},{6,14,22,30},{1,9,17,25},{3,11,19..., dimensions={0} | all-to-all | bytes 4259840 | tf_op jit(solution)/shard_map/all_to_all | solution.py:40
  154.7 12.4 %all_to_all.38.parts_ref = bf16[4,272,256]{2,1,0:T(8,128)(2,1)S(1)} all-to-all(bf16[4,272,256]{2,1,0:T(8,128)(2,1)S(1)} %shard_map.143), channel_id=1, replica_groups={{0,2,4,6},{8,10,12,14},{16,18,20,22},{24,26,28,30},{1,3,5,7},{9,11,13,1..., dimensions={0} | all-to-all | bytes 1114112 | tf_op jit(solution)/shard_map/all_to_all | solution.py:40
  167.3 8.9 %collective-permute-start.1 = (bf16[128,256]{1,0:T(8,128)(2,1)S(1)}, bf16[128,256]{1,0:T(8,128)(2,1)S(1)}, u32[]{:S(2)}, u32[]{:S(2)}) collective-permute-start(bf16[128,256]{1,0:T(8,128)(2,1)S(1)} %get-tuple-element.21), channel_id=1, source_target_pairs={{0,32},{32,64},{64,96},{96,128},{128,160},{160,192},{192,224},{224... | collective-permute-start | bytes 196616 | tf_op jit(solution)/shard_map/ppermute | solution.py:301
  176.3 1.9 %collective-permute-start.2 = (bf16[128,256]{1,0:T(8,128)(2,1)S(1)}, bf16[128,256]{1,0:T(8,128)(2,1)S(1)}, u32[]{:S(2)}, u32[]{:S(2)}) collective-permute-start(bf16[128,256]{1,0:T(8,128)(2,1)S(1)} %get-tuple-element.22), channel_id=1, source_target_pairs={{32,0},{64,32},{96,64},{128,96},{160,128},{192,160},{224,192},{256... | collective-permute-start | bytes 196616 | tf_op jit(solution)/shard_map/ppermute | solution.py:302
  178.2 3.6 %collective-permute-done.2 = bf16[128,256]{1,0:T(8,128)(2,1)S(1)} collective-permute-done((bf16[128,256]{1,0:T(8,128)(2,1)S(1)}, bf16[128,256]{1,0:T(8,128)(2,1)S(1)}, u32[]{:S(2)}, u32[]{:S(2)}) %collective-permute-start.2) | collective-permute-done | bytes 65568 | tf_op jit(solution)/shard_map/ppermute | solution.py:302
  (46 shorter events, 5.2 us)
Async XLA Ops:
  0.6 25.2 %copy-start.7 = (bf16[1,256,1024]{2,1,0:T(8,128)(2,1)S(1)}, bf16[1,256,1024]{2,1,0:T(8,128)(2,1)}, u32[]{:S(2)}) copy-start(bf16[1,256,1024]{2,1,0:T(8,128)(2,1)} %param.18) | copy-start | bytes 1572868
  2.2 15.4 %collective-permute-start = (bf16[128,256]{1,0:T(8,128)(2,1)S(1)}, bf16[128,256]{1,0:T(8,128)(2,1)S(1)}, u32[]{:S(2)}, u32[]{:S(2)}) collective-permute-start(bf16[128,256]{1,0:T(8,128)(2,1)S(1)} %bitcast_select_fusion), channel_id=1, source_target_pairs={{0,480},{32,448},{64,416},{96,384},{128,352},{160,320},{192,288},{... | collective-permute-start | bytes 196616 | tf_op jit(solution)/shard_map/ppermute | solution.py:238
  21.3 24.9 %all-to-all-start = ((bf16[4,400,256]{2,1,0:T(8,128)(2,1)}), bf16[4,400,256]{2,1,0:T(8,128)(2,1)S(1)}, u32[]{:S(2)}, u32[]{:S(2)}) async-start(bf16[4,400,256]{2,1,0:T(8,128)(2,1)} %broadcast_in_dim.28), calls=%async_computation | async-start | bytes 1638400 | tf_op jit(solution)/shard_map/all_to_all | solution.py:40
  46.2 20.6 %all-to-all-start.2 = ((bf16[16,64,256]{2,1,0:T(8,128)(2,1)}), bf16[16,64,256]{2,1,0:T(8,128)(2,1)S(1)}, u32[]{:S(2)}, u32[]{:S(2)}) async-start(bf16[16,64,256]{2,1,0:T(8,128)(2,1)} %shard_map.139), calls=%async_computation.2 | async-start | bytes 1048576 | tf_op jit(solution)/shard_map/all_to_all | solution.py:242
  66.8 1.9 %copy-start.3 = (bf16[16,64,256]{2,1,0:T(8,128)(2,1)}, bf16[16,64,256]{2,1,0:T(8,128)(2,1)S(1)}, u32[]{:S(2)}) copy-start(bf16[16,64,256]{2,1,0:T(8,128)(2,1)S(1)} %all-to-all-done.2.kvw_ref) | copy-start | bytes 1572868
  68.7 3.9 %copy-start.11 = (f32[64,128]{1,0:T(8,128)S(1)}, f32[64,128]{1,0:T(8,128)}, u32[]{:S(2)}) copy-start(f32[64,128]{1,0:T(8,128)} %constant.49.clone.sint_ref) | copy-start | bytes 98308
  68.7 3.9 %copy-start.12 = (f32[64,128]{1,0:T(8,128)S(1)}, f32[64,128]{1,0:T(8,128)}, u32[]{:S(2)}) copy-start(f32[64,128]{1,0:T(8,128)} %constant.48.clone.cost_ref) | copy-start | bytes 98308
  68.7 40.0 %all-to-all-start.1 = ((bf16[4,1552,256]{2,1,0:T(8,128)(2,1)}), bf16[4,1552,256]{2,1,0:T(8,128)(2,1)S(1)}, u32[]{:S(2)}, u32[]{:S(2)}) async-start(bf16[4,1552,256]{2,1,0:T(8,128)(2,1)} %broadcast_in_dim.30), calls=%async_computation.1 | async-start | bytes 6356992 | tf_op jit(solution)/shard_map/all_to_all | solution.py:40
  72.5 45.9 %copy-start.9 = (f32[128,128]{1,0:T(8,128)S(1)}, f32[128,128]{1,0:T(8,128)}, u32[]{:S(2)}) copy-start(f32[128,128]{1,0:T(8,128)} %constant.50.clone.cos_ref) | copy-start | bytes 196612
  72.5 45.9 %copy-start.10 = (f32[128,128]{1,0:T(8,128)S(1)}, f32[128,128]{1,0:T(8,128)}, u32[]{:S(2)}) copy-start(f32[128,128]{1,0:T(8,128)} %constant.51.clone.sin_ref) | copy-start | bytes 196612
  108.7 9.7 %copy-start = (bf16[1,4096,256]{2,1,0:T(8,128)(2,1)S(1)}, bf16[1,4096,256]{2,1,0:T(8,128)(2,1)}, u32[]{:S(2)}) copy-start(bf16[1,4096,256]{2,1,0:T(8,128)(2,1)} %param.17) | copy-start | bytes 6291460
  108.7 1.2 copy-start.4
  118.4 1.6 copy-start.1
  120.0 9.2 %copy-start.2 = (bf16[1,256,4096]{2,1,0:T(8,128)(2,1)S(1)}, bf16[1,256,4096]{2,1,0:T(8,128)(2,1)}, u32[]{:S(2)}) copy-start(bf16[1,256,4096]{2,1,0:T(8,128)(2,1)} %param.19) | copy-start | bytes 6291460
  120.0 9.2 %copy-start.5 = (bf16[16,64,256]{2,1,0:T(8,128)(2,1)S(1)}, bf16[16,64,256]{2,1,0:T(8,128)(2,1)}, u32[]{:S(2)}) copy-start(bf16[16,64,256]{2,1,0:T(8,128)(2,1)} %copy-done.3) | copy-start | bytes 1572868
  154.5 12.7 %copy-start.6 = (bf16[1,128,256]{2,1,0:T(8,128)(2,1)S(1)}, bf16[1,128,256]{2,1,0:T(8,128)(2,1)}, u32[]{:S(2)}) copy-start(bf16[1,128,256]{2,1,0:T(8,128)(2,1)} %param.12) | copy-start | bytes 196612
  154.5 12.7 %copy-start.8 = (bf16[1,128,256]{2,1,0:T(8,128)(2,1)S(1)}, bf16[1,128,256]{2,1,0:T(8,128)(2,1)}, u32[]{:S(2)}) copy-start(bf16[1,128,256]{2,1,0:T(8,128)(2,1)} %param.15) | copy-start | bytes 196612
  154.5 12.7 %copy-start.13 = (f32[1,256]{1,0:T(1,128)S(1)}, f32[1,256]{1,0:T(1,128)}, u32[]{:S(2)}) copy-start(f32[1,256]{1,0:T(1,128)} %gain_ref.1) | copy-start | bytes 3076
  167.3 10.8 %collective-permute-start.1 = (bf16[128,256]{1,0:T(8,128)(2,1)S(1)}, bf16[128,256]{1,0:T(8,128)(2,1)S(1)}, u32[]{:S(2)}, u32[]{:S(2)}) collective-permute-start(bf16[128,256]{1,0:T(8,128)(2,1)S(1)} %get-tuple-element.21), channel_id=1, source_target_pairs={{0,32},{32,64},{64,96},{96,128},{128,160},{160,192},{192,224},{224... | collective-permute-start | bytes 196616 | tf_op jit(solution)/shard_map/ppermute | solution.py:301
  176.3 5.6 %collective-permute-start.2 = (bf16[128,256]{1,0:T(8,128)(2,1)S(1)}, bf16[128,256]{1,0:T(8,128)(2,1)S(1)}, u32[]{:S(2)}, u32[]{:S(2)}) collective-permute-start(bf16[128,256]{1,0:T(8,128)(2,1)S(1)} %get-tuple-element.22), channel_id=1, source_target_pairs={{32,0},{64,32},{96,64},{128,96},{160,128},{192,160},{224,192},{256... | collective-permute-start | bytes 196616 | tf_op jit(solution)/shard_map/ppermute | solution.py:302

commit v2 on v1

--- a/solution.py
+++ b/solution.py
@@ -19,7 +19,6 @@
 MIB = 1024 * 1024
 
 ALONG_Y = [[x * SIDE + y for y in range(SIDE)] for x in range(SIDE)]
-ALONG_X = [[x * SIDE + y for x in range(SIDE)] for y in range(SIDE)]
 
 NN = (((1,), (0,)), ((), ()))
 NT = (((1,), (1,)), ((), ()))
@@ -40,11 +39,27 @@
     return lax.all_to_all(blocks, "tensor", 0, 0, axis_index_groups=groups)
 
 
+def around_x(t, k):
+    return (t // SIDE + k) % SIDE * SIDE + t % SIDE
+
+
+def from_ahead(block, k):
+    return lax.ppermute(block, "tensor", [(around_x(t, k), t) for t in range(16)])
+
+
+def to_ahead(block, k):
+    return lax.ppermute(block, "tensor", [(t, around_x(t, k)) for t in range(16)])
+
+
 def call(kernel, outs, *operands, vmem=32, flops=0):
     nbytes = sum(int(np.prod(a.shape)) * a.dtype.itemsize for a in (*operands, *outs))
+    specs = [
+        pl.BlockSpec(memory_space=pltpu.SMEM if a.shape == (1,) else pltpu.VMEM) for a in operands
+    ]
     return pl.pallas_call(
         kernel,
         out_shape=outs,
+        in_specs=specs,
         compiler_params=pltpu.CompilerParams(vmem_limit_bytes=vmem * MIB),
         cost_estimate=pl.CostEstimate(flops=flops, bytes_accessed=nbytes, transcendentals=0),
     )(*operands)
@@ -64,23 +79,38 @@
             out_ref[x * SIDE + y, 32:64] = values[32 * y : 32 * y + 32]
 
 
-def norm_and_kv(rows_ref, kvw_ref, cos_ref, sin_ref, normed_ref, kv_ref, raw_ref, factor_ref):
-    total = jnp.zeros((2 * TOK, 1), jnp.float32)
-    for x in range(SIDE):
-        for y in range(SIDE):
-            block = rows_ref[x, y * 384 : y * 384 + 256].astype(jnp.float32)
-            total = total + jnp.sum(block * block, axis=1, keepdims=True)
-    factor = lax.rsqrt(total / WIDTH + norm_eps)
-    factor_ref[...] = jnp.broadcast_to(factor[TOK:], (TOK, HD))
+def source_block(x_ref, k):
+    return lax.rem(x_ref[0] + k, SIDE)
+
+
+def norm_and_kv(
+    x_ref, f0, f1, f2, f3, b0, b1, b2, b3, kvw_ref, cos_ref, sin_ref, normed_ref, kv_ref, raw_ref, factor_ref
+):
+    ahead, back = (f0, f1, f2, f3), (b0, b1, b2, b3)
+    total = jnp.zeros((TOK, COLS), jnp.float32)
+    back_total = jnp.zeros((TOK, COLS), jnp.float32)
+    for k in range(SIDE):
+        for y in range(SIDE):
+            block = ahead[k][y * 256 : y * 256 + TOK].astype(jnp.float32)
+            total = total + block * block
+            block = back[k][y * TOK : (y + 1) * TOK].astype(jnp.float32)
+            back_total = back_total + block * block
+    factor = lax.rsqrt(jnp.sum(total, axis=1, keepdims=True) / WIDTH + norm_eps)
+    back_factor = lax.rsqrt(jnp.sum(back_total, axis=1, keepdims=True) / WIDTH + norm_eps)
+    factor_ref[...] = jnp.broadcast_to(back_factor, (TOK, HD))
     kv = jnp.zeros((64, 2 * TOK), jnp.float32)
-    for x in range(SIDE):
-        gains = rows_ref[x, 1536:1552].astype(jnp.float32)
-        for y in range(SIDE):
+    for k in range(SIDE):
+        gains = ahead[k][1024:1040].astype(jnp.float32)
+        for y in range(SIDE):
+            t = source_block(x_ref, k) * SIDE + y
             gain = gains[3 * y : 3 * y + 1] + gains[3 * y + 1 : 3 * y + 2] + gains[3 * y + 2 : 3 * y + 3]
-            block = rows_ref[x, y * 384 : y * 384 + 256].astype(jnp.float32)
+            block = ahead[k][y * 256 : y * 256 + TOK].astype(jnp.float32)
             normed = (block * factor * gain).astype(jnp.bfloat16)
-            normed_ref[x * SIDE + y] = normed
-            kv = kv + matmul(kvw_ref[x * SIDE + y], normed, NT)
+            block = back[k][y * TOK : (y + 1) * TOK].astype(jnp.float32)
+            back_normed = (block * back_factor * gain).astype(jnp.bfloat16)
+            normed = jnp.concatenate([normed, back_normed], axis=0)
+            normed_ref[k * SIDE + y] = normed
+            kv = kv + matmul(kvw_ref[t], normed, NT)
     raw_ref[...] = kv[:, TOK:]
     first, second = kv[0:16], kv[16:32]
     cos, sin = cos_ref[...], sin_ref[...]
@@ -90,19 +120,30 @@
         kv_ref[y] = out
 
 
+def weight_rows(t):
+    return pl.ds(pl.multiple_of(t * COLS, COLS), COLS)
+
+
+def queries(x_ref, normed_ref, f0, f1, f2, f3, qw_ref, ow_ref, query_ref, grad_out_ref):
+    ahead = (f0, f1, f2, f3)
+    query = jnp.zeros((2 * TOK, COLS), jnp.float32)
+    grad_out = jnp.zeros((TOK, COLS), jnp.float32)
+    for k in range(SIDE):
+        for y in range(SIDE):
+            block = weight_rows(source_block(x_ref, k) * SIDE + y)
+            query = query + matmul(normed_ref[k * SIDE + y], qw_ref[block, :], NN)
+            cot = ahead[k][y * 256 + TOK : y * 256 + 256]
+            grad_out = grad_out + matmul(cot, ow_ref[:, block], NT)
+    query_ref[...] = query
+    grad_out_ref[...] = grad_out.astype(jnp.bfloat16)
+
+
 def attention(
-    rows_ref, normed_ref, kv_ref, qw_ref, ow_ref, cos_ref, sin_ref, cost_ref, sint_ref,
+    query_ref, grad_out_ref, kv_ref, cos_ref, sin_ref, cost_ref, sint_ref,
     attended_ref, grad_query_ref, grad_kv_ref, mixed_ref,
 ):
-    query = jnp.zeros((2 * TOK, COLS), jnp.float32)
-    grad_out = jnp.zeros((TOK, COLS), jnp.float32)
-    for x in range(SIDE):
-        for y in range(SIDE):
-            t = x * SIDE + y
-            query = query + matmul(normed_ref[t], qw_ref[t * COLS : (t + 1) * COLS], NN)
-            cot = rows_ref[x, y * 384 + 256 : y * 384 + 384]
-            grad_out = grad_out + matmul(cot, ow_ref[:, t * COLS : (t + 1) * COLS], NT)
-    grad_out = grad_out.astype(jnp.bfloat16)
+    query = query_ref[...]
+    grad_out = grad_out_ref[...]
     kv = [kv_ref[y] for y in range(SIDE)]
     cos, sin = cos_ref[...], sin_ref[...]
     scale = HD ** (-0.5)
@@ -169,45 +210,65 @@
     return jnp.concatenate([both, jnp.zeros((16, COLS - TOK), jnp.float32)], axis=1).astype(jnp.bfloat16)
 
 
-def project(attended_ref, grad_query_ref, grad_kv_ref, raw_ref, mixed_ref, qw_ref, ow_ref, kvw_ref, out_ref):
+def project_out(x_ref, attended_ref, ow_ref, o0, o1, o2, o3):
     attended = attended_ref[...]
+    for k, out_ref in enumerate((o0, o1, o2, o3)):
+        for y in range(SIDE):
+            block = weight_rows(source_block(x_ref, k) * SIDE + y)
+            term = matmul(attended, ow_ref[:, block], NN)
+            out_ref[y * TOK : (y + 1) * TOK] = term.astype(jnp.bfloat16)
+
+
+def project_grad(
+    x_ref, grad_query_ref, grad_kv_ref, raw_ref, mixed_ref, qw_ref, kvw_ref, o0, o1, o2, o3
+):
     grad_query = grad_query_ref[...]
     grad_kv = grad_kv_ref[0] + grad_kv_ref[1] + grad_kv_ref[2] + grad_kv_ref[3]
     grad_kv = grad_kv.astype(jnp.bfloat16)
     mixed = mixed_ref[0:1] + jnp.sum(grad_kv.astype(jnp.float32) * raw_ref[...], axis=0, keepdims=True)
     rows = split_rows(mixed)
-    for x in range(SIDE):
-        for y in range(SIDE):
-            t = x * SIDE + y
-            term = matmul(attended, ow_ref[:, t * COLS : (t + 1) * COLS], NN)
-            out_ref[x, y * 256 : y * 256 + TOK] = term.astype(jnp.bfloat16)
-            term = matmul(grad_query, qw_ref[t * COLS : (t + 1) * COLS], NT)
+    for k, out_ref in enumerate((o0, o1, o2, o3)):
+        for y in range(SIDE):
+            t = source_block(x_ref, k) * SIDE + y
+            term = matmul(grad_query, qw_ref[weight_rows(t), :], NT)
             term = term + matmul(grad_kv, kvw_ref[t], TN)
-            out_ref[x, y * 256 + TOK : y * 256 + 256] = term.astype(jnp.bfloat16)
-        out_ref[x, 1024:1040] = rows
-
-
-def sum_x(parts_ref, out_ref):
-    rows = parts_ref[0, 1024:1040].astype(jnp.float32)
-    for x in range(1, SIDE):
-        rows = rows + parts_ref[x, 1024:1040].astype(jnp.float32)
+            out_ref[y * TOK : (y + 1) * TOK] = term.astype(jnp.bfloat16)
+        out_ref[512:528] = rows
+
+
+def sum_out(p0, p1, p2, p3, out_ref):
+    for y in range(SIDE):
+        total = jnp.zeros((TOK, COLS), jnp.float32)
+        for part in (p0, p1, p2, p3):
+            total = total + part[y * TOK : (y + 1) * TOK].astype(jnp.float32)
+        out_ref[y, 0:TOK] = total.astype(jnp.bfloat16)
+
+
+def sum_grad(p0, p1, p2, p3, out_ref):
+    sum_out(p0, p1, p2, p3, out_ref)
+    rows = jnp.zeros((16, COLS), jnp.float32)
+    for part in (p0, p1, p2, p3):
+        rows = rows + part[512:528].astype(jnp.float32)
     mixed = split_rows(rows[0:1, :TOK] + rows[1:2, :TOK])
     for y in range(SIDE):
-        total = parts_ref[0, y * 256 : y * 256 + 256].astype(jnp.float32)
-        for x in range(1, SIDE):
-            total = total + parts_ref[x, y * 256 : y * 256 + 256].astype(jnp.float32)
-        out_ref[y, 0:256] = total.astype(jnp.bfloat16)
-        out_ref[y, 256:272] = mixed
-
-
-def finish(parts_ref, rows_ref, back_ref, cot_ref, gain_ref, factor_ref, out_ref, grad_ref):
+        out_ref[y, TOK : TOK + 16] = mixed
+
+
+def finish_out(parts_ref, rows_ref, out_ref):
+    total = rows_ref[...].astype(jnp.float32)
+    for y in range(SIDE):
+        total = total + parts_ref[y].astype(jnp.float32)
+    out_ref[...] = total.astype(jnp.bfloat16)
+
+
+def finish_grad(parts_ref, back_ref, cot_ref, gain_ref, factor_ref, grad_ref):
     total = parts_ref[0].astype(jnp.float32)
     for y in range(1, SIDE):
         total = total + parts_ref[y].astype(jnp.float32)
-    out_ref[...] = (rows_ref[...].astype(jnp.float32) + total[0:TOK]).astype(jnp.bfloat16)
-    mixed = jnp.broadcast_to(total[256:257, :TOK] + total[257:258, :TOK], (TOK, TOK)).T[:, 0:1]
+    mixed = jnp.broadcast_to(total[TOK : TOK + 1, :TOK] + total[TOK + 1 : TOK + 2, :TOK], (TOK, TOK))
+    mixed = mixed.T[:, 0:1]
     factor = factor_ref[:, 0:1]
-    scaled = total[TOK : 2 * TOK] * gain_ref[...]
+    scaled = total[0:TOK] * gain_ref[...]
     grad_rows = factor * scaled - back_ref[...].astype(jnp.float32) * (factor * factor * mixed / WIDTH)
     grad_ref[...] = (cot_ref[...].astype(jnp.float32) + grad_rows).astype(jnp.bfloat16)
 
@@ -238,21 +299,27 @@
     received = lax.ppermute(sending, "section", mirrored)
     back_rows = jnp.where(is_early, received, token_rows)
 
-    packed = call(pack_kv_weight, (shape((16, 64, COLS)),), kv_w)[0]
-    kv_rows = lax.all_to_all(packed, "tensor", 0, 0)
-
+    x_pos = (lax.axis_index("tensor") // SIDE).astype(jnp.int32).reshape(1)
     gain_row = norm_gain
     high = lax.reduce_precision(gain_row, 8, 7)
     middle = lax.reduce_precision(gain_row - high, 8, 7)
     low = gain_row - high - middle
     gains = jnp.concatenate([high, middle, low, jnp.zeros((13, COLS), jnp.float32)], axis=0)
-    own = jnp.concatenate([token_rows, back_rows, cot_rows, gains.astype(jnp.bfloat16)], axis=0)
+    own = jnp.concatenate([token_rows, cot_rows, gains.astype(jnp.bfloat16)], axis=0)
     column = exchange(jnp.broadcast_to(own[None], (SIDE,) + own.shape), ALONG_Y)
+    back_rows, _ = lax.optimization_barrier((back_rows, column))
+    back_column = exchange(jnp.broadcast_to(back_rows[None], (SIDE,) + back_rows.shape), ALONG_Y)
     gains = jnp.concatenate(
-        [column[:, 384:387].reshape(12, COLS), jnp.zeros((4, COLS), jnp.bfloat16)], axis=0
-    )
-    column = jnp.concatenate([column[:, :384].reshape(1536, COLS), gains], axis=0)
-    rows = exchange(jnp.broadcast_to(column[None], (SIDE,) + column.shape), ALONG_X)
+        [column[:, 256:259].reshape(12, COLS), jnp.zeros((4, COLS), jnp.bfloat16)], axis=0
+    )
+    column = jnp.concatenate([column[:, :256].reshape(1024, COLS), gains], axis=0)
+    ahead = [column] + [from_ahead(column, k) for k in range(1, SIDE)]
+    kv_w, _ = lax.optimization_barrier((kv_w, back_column))
+    back_column = back_column.reshape(4 * TOK, COLS)
+    back = [back_column] + [from_ahead(back_column, k) for k in range(1, SIDE)]
+
+    packed = call(pack_kv_weight, (shape((16, 64, COLS)),), kv_w)[0]
+    kv_rows = lax.all_to_all(packed, "tensor", 0, 0)
 
     cos, sin = rope_angles()
     cos_cols, sin_cols = jnp.asarray(cos.T.copy()), jnp.asarray(sin.T.copy())
@@ -268,10 +335,16 @@
             shape((64, TOK), jnp.float32),
             shape((TOK, HD), jnp.float32),
         ),
-        rows, kv_rows, cos_own, sin_own,
+        x_pos, *ahead, *back, kv_rows, cos_own, sin_own,
         flops=2 * 64 * 256 * 4096,
     )
     kv_all = exchange(kv_own, ALONG_Y)
+    query, grad_out = call(
+        queries,
+        (shape((2 * TOK, COLS), jnp.float32), shape((TOK, COLS))),
+        x_pos, normed, *ahead, query_w, out_w,
+        flops=2 * 384 * 256 * 4096,
+    )
     attended, grad_query, grad_kv, mixed = call(
         attention,
         (
@@ -280,25 +353,37 @@
             shape((SIDE, 64, TOK), jnp.float32),
             shape((8, TOK), jnp.float32),
         ),
-        rows, normed, kv_all, query_w, out_w, cos_wide, sin_wide, cos_cols, sin_cols,
-        flops=2 * 384 * 256 * 4096,
+        query, grad_out, kv_all, cos_wide, sin_wide, cos_cols, sin_cols,
     )
     grad_kv = exchange(grad_kv, ALONG_Y)
+    out_terms = call(
+        project_out,
+        (shape((4 * TOK, COLS)),) * SIDE,
+        x_pos, attended, out_w,
+        flops=2 * 128 * 256 * 4096,
+    )
+    out_terms = [out_terms[0]] + [to_ahead(out_terms[k], k) for k in range(1, SIDE)]
+    out_terms = call(sum_out, (shape((SIDE, TOK, COLS)),), *out_terms)[0]
+    out_terms, _ = lax.optimization_barrier((out_terms, grad_kv))
+    out_terms = exchange(out_terms, ALONG_Y)
+    layer_out = call(finish_out, (shape((TOK, COLS)),), out_terms, token_rows)[0]
+    next_input = lax.ppermute(layer_out, "section", [(s, s + 1) for s in range(section_count - 1)])
+
     terms = call(
-        project,
-        (shape((SIDE, 1040, COLS)),),
-        attended, grad_query, grad_kv, kv_raw, mixed, query_w, out_w, kv_rows,
-        flops=2 * 256 * 256 * 4096,
+        project_grad,
+        (shape((4 * TOK + 16, COLS)),) * SIDE,
+        x_pos, grad_query, grad_kv, kv_raw, mixed, query_w, kv_rows,
+        flops=2 * 128 * 256 * 4096,
+    )
+    terms = [terms[0]] + [to_ahead(terms[k], k) for k in range(1, SIDE)]
+    terms = call(sum_grad, (shape((SIDE, TOK + 16, COLS)),), *terms)[0]
+    terms, _ = lax.optimization_barrier((terms, out_terms))
+    terms = exchange(terms, ALONG_Y)
+    grad_local = call(
+        finish_grad,
+        (shape((TOK, COLS)),),
+        terms, back_rows, cot_rows, gain_row, factor,
     )[0]
-    terms = exchange(terms, ALONG_X)
-    terms = call(sum_x, (shape((SIDE, 272, COLS)),), terms)[0]
-    terms = exchange(terms, ALONG_Y)
-    layer_out, grad_local = call(
-        finish,
-        (shape((TOK, COLS)), shape((TOK, COLS))),
-        terms, token_rows, back_rows, cot_rows, gain_row, factor,
-    )
-    next_input = lax.ppermute(layer_out, "section", [(s, s + 1) for s in range(section_count - 1)])
     input_grad = lax.ppermute(grad_local, "section", [(s + 1, s) for s in range(section_count - 1)])
     return (next_input[None], received[None], input_grad[None])
 

time: 185 us -> 186 us (level)
  the two profiles are of different devices: /device:TPU:1 before, /device:TPU:3 now
where the time goes in v2:
time: 186 us; the launch traced here: 184 us
  starting transfers between devices  84.2 us (45%)
  waiting for transfers between devices  48 us (26%)
  local copies, waits for them, and re-layouts  23 us (12%)
  blocking collectives  13.5 us (7%)
  Pallas kernels  13.2 us (7%)
    all_to_all x5, starting transfers between devices, exchange(): return lax.all_to_all(blocks, 'tensor', 0, 0, axis_index_groups=groups)  22.1 us
    ppermute x6, waiting for transfers between devices, from_ahead(): lax.ppermute(block, 'tensor', [(around_x(t, k), t) for t in range(16)])  21 us
    ppermute x6, starting transfers between devices, from_ahead(): lax.ppermute(block, 'tensor', [(around_x(t, k), t) for t in range(16)])  20.5 us
    unnamed x65, local copies, waits for them, and re-layouts  19.2 us
    ppermute x6, starting transfers between devices, to_ahead(): lax.ppermute(block, 'tensor', [(t, around_x(t, k)) for t in range(16)])  17.7 us
    ppermute x6, waiting for transfers between devices, to_ahead(): lax.ppermute(block, 'tensor', [(t, around_x(t, k)) for t in range(16)])  17.2 us
    all_to_all x1, blocking collectives, exchange(): return lax.all_to_all(blocks, 'tensor', 0, 0, axis_index_groups=groups)  13.5 us
    pallas_call x10, Pallas kernels, call(): pl.pallas_call(kernel, out_shape=outs, in_specs=specs, compiler_params=pl...  13.2 us
  transfers between devices with their start and end apart: 21, of which 12 were waited for; matrix products, arithmetic and copies ran while one was open for 1% of the time, Pallas kernels for 4%

profile of v2, /device:TPU:3, one launch (start us, length us, event | category | flops | bytes accessed | tf_op | source)
XLA Modules:
  0.0 184.4 jit_solution(8324154467820742586)
XLA Ops:
  4.1 4.6 %all-to-all-start = ((bf16[4,272,256]{2,1,0:T(8,128)(2,1)}), bf16[4,272,256]{2,1,0:T(8,128)(2,1)S(1)}, u32[]{:S(2)}, u32[]{:S(2)}) async-start(bf16[4,272,256]{2,1,0:T(8,128)(2,1)} %broadcast_in_dim.28), calls=%async_computation | async-start | bytes 1114112 | tf_op jit(solution)/shard_map/all_to_all | solution.py:39
  9.4 11.5 %collective-permute-start.3 = (bf16[128,256]{1,0:T(8,128)(2,1)S(1)}, bf16[128,256]{1,0:T(8,128)(2,1)S(1)}, u32[]{:S(2)}, u32[]{:S(2)}) collective-permute-start(bf16[128,256]{1,0:T(8,128)(2,1)S(1)} %bitcast_select_fusion), channel_id=1, source_target_pairs={{0,480},{32,448},{64,416},{96,384},{128,352},{160,320},{192,288},{... | collective-permute-start | bytes 196616 | tf_op jit(solution)/shard_map/ppermute | solution.py:299
  20.9 3.0 %collective-permute-done.3 = bf16[128,256]{1,0:T(8,128)(2,1)S(1)} collective-permute-done((bf16[128,256]{1,0:T(8,128)(2,1)S(1)}, bf16[128,256]{1,0:T(8,128)(2,1)S(1)}, u32[]{:S(2)}, u32[]{:S(2)}) %collective-permute-start.3) | collective-permute-done | bytes 65568 | tf_op jit(solution)/shard_map/ppermute | solution.py:299
  24.6 13.5 %all_to_all.35 = bf16[4,128,256]{2,1,0:T(8,128)(2,1)S(1)} all-to-all(bf16[4,128,256]{2,1,0:T(8,128)(2,1)S(1)} %broadcast_in_dim.30), channel_id=1, replica_groups={{0,2,4,6},{8,10,12,14},{16,18,20,22},{24,26,28,30},{1,3,5,7},{9,11,13,1..., dimensions={0} | all-to-all | bytes 524288 | tf_op jit(solution)/shard_map/all_to_all | solution.py:39
  39.2 5.2 %all-to-all-start.2 = ((bf16[16,64,256]{2,1,0:T(8,128)(2,1)}), bf16[16,64,256]{2,1,0:T(8,128)(2,1)S(1)}, u32[]{:S(2)}, u32[]{:S(2)}) async-start(bf16[16,64,256]{2,1,0:T(8,128)(2,1)} %shard_map.139), calls=%async_computation.2 | async-start | bytes 1048576 | tf_op jit(solution)/shard_map/all_to_all | solution.py:322
  44.6 3.1 %collective-permute-start.2 = (bf16[1040,256]{1,0:T(8,128)(2,1)S(1)}, bf16[1040,256]{1,0:T(8,128)(2,1)S(1)}, u32[]{:S(2)}, u32[]{:S(2)}) collective-permute-start(bf16[1040,256]{1,0:T(8,128)(2,1)S(1)} %concatenate.10.f0), channel_id=1, source_target_pairs={{24,0},{26,2},{28,4},{30,6},{0,8},{2,10},{4,12},{6,14},{8,16},{10,... | collective-permute-start | bytes 1597448 | tf_op jit(solution)/shard_map/ppermute | solution.py:47
  50.3 3.9 %collective-permute-start = (bf16[1040,256]{1,0:T(8,128)(2,1)S(1)}, bf16[1040,256]{1,0:T(8,128)(2,1)}, u32[]{:S(2)}, u32[]{:S(2)}) collective-permute-start(bf16[1040,256]{1,0:T(8,128)(2,1)S(1)} %concatenate.10.f0), channel_id=1, source_target_pairs={{8,0},{10,2},{12,4},{14,6},{16,8},{18,10},{20,12},{22,14},{24,16},... | collective-permute-start | bytes 1597448 | tf_op jit(solution)/shard_map/ppermute | solution.py:47
  56.1 4.9 %collective-permute-start.5 = (bf16[512,256]{1,0:T(8,128)(2,1)S(1)}, bf16[512,256]{1,0:T(8,128)(2,1)}, u32[]{:S(2)}, u32[]{:S(2)}) collective-permute-start(bf16[512,256]{1,0:T(8,128)(2,1)S(1)} %bitcast.32), channel_id=1, source_target_pairs={{16,0},{18,2},{20,4},{22,6},{24,8},{26,10},{28,12},{30,14},{0,16},... | collective-permute-start | bytes 786440 | tf_op jit(solution)/shard_map/ppermute | solution.py:47
  64.0 4.1 %collective-permute-start.4 = (bf16[512,256]{1,0:T(8,128)(2,1)S(1)}, bf16[512,256]{1,0:T(8,128)(2,1)}, u32[]{:S(2)}, u32[]{:S(2)}) collective-permute-start(bf16[512,256]{1,0:T(8,128)(2,1)S(1)} %bitcast.33), channel_id=1, source_target_pairs={{8,0},{10,2},{12,4},{14,6},{16,8},{18,10},{20,12},{22,14},{24,16},... | collective-permute-start | bytes 786440 | tf_op jit(solution)/shard_map/ppermute | solution.py:47
  70.3 8.1 %collective-permute-done.f1 = bf16[1040,256]{1,0:T(8,128)(2,1)} collective-permute-done((bf16[1040,256]{1,0:T(8,128)(2,1)S(1)}, bf16[1040,256]{1,0:T(8,128)(2,1)}, u32[]{:S(2)}, u32[]{:S(2)}) %collective-permute-start) | collective-permute-done | bytes 532512 | tf_op jit(solution)/shard_map/ppermute | solution.py:47
  80.3 2.9 %collective-permute-done.5.b2 = bf16[512,256]{1,0:T(8,128)(2,1)} collective-permute-done((bf16[512,256]{1,0:T(8,128)(2,1)S(1)}, bf16[512,256]{1,0:T(8,128)(2,1)}, u32[]{:S(2)}, u32[]{:S(2)}) %collective-permute-start.5) | collective-permute-done | bytes 262176 | tf_op jit(solution)/shard_map/ppermute | solution.py:47
  83.2 5.8 %collective-permute-done.4.b1 = bf16[512,256]{1,0:T(8,128)(2,1)} collective-permute-done((bf16[512,256]{1,0:T(8,128)(2,1)S(1)}, bf16[512,256]{1,0:T(8,128)(2,1)}, u32[]{:S(2)}, u32[]{:S(2)}) %collective-permute-start.4) | collective-permute-done | bytes 262176 | tf_op jit(solution)/shard_map/ppermute | solution.py:47
  97.4 4.4 %all-to-all-start.3 = ((bf16[4,64,256]{2,1,0:T(8,128)(2,1)}), bf16[4,64,256]{2,1,0:T(8,128)(2,1)S(1)}, u32[]{:S(2)}, u32[]{:S(2)}) async-start(bf16[4,64,256]{2,1,0:T(8,128)(2,1)} %copy-done.13), calls=%async_computation.3 | async-start | bytes 262144 | tf_op jit(solution)/shard_map/all_to_all | solution.py:39
  118.4 3.1 %collective-permute-start.8 = (bf16[512,256]{1,0:T(8,128)(2,1)}, bf16[512,256]{1,0:T(8,128)(2,1)}, u32[]{:S(2)}, u32[]{:S(2)}) collective-permute-start(bf16[512,256]{1,0:T(8,128)(2,1)} %get-tuple-element.34), channel_id=1, source_target_pairs={{0,16},{2,18},{4,20},{6,22},{8,24},{10,26},{12,28},{14,30},{16,0},... | collective-permute-start | bytes 786440 | tf_op jit(solution)/shard_map/ppermute | solution.py:51
  121.5 3.8 %collective-permute-start.9 = (bf16[512,256]{1,0:T(8,128)(2,1)}, bf16[512,256]{1,0:T(8,128)(2,1)}, u32[]{:S(2)}, u32[]{:S(2)}) collective-permute-start(bf16[512,256]{1,0:T(8,128)(2,1)} %get-tuple-element.35), channel_id=1, source_target_pairs={{0,24},{2,26},{4,28},{6,30},{8,0},{10,2},{12,4},{14,6},{16,8},{18,... | collective-permute-start | bytes 786440 | tf_op jit(solution)/shard_map/ppermute | solution.py:51
  125.4 4.5 %all-to-all-start.4 = ((f32[4,64,128]{2,1,0:T(8,128)}), f32[4,64,128]{2,1,0:T(8,128)S(1)}, u32[]{:S(2)}, u32[]{:S(2)}) async-start(f32[4,64,128]{2,1,0:T(8,128)} %get-tuple-element.36), calls=%async_computation.4 | async-start | bytes 262144 | tf_op jit(solution)/shard_map/all_to_all | solution.py:39
  129.9 6.0 %collective-permute-done.9.p3 = bf16[512,256]{1,0:T(8,128)(2,1)} collective-permute-done((bf16[512,256]{1,0:T(8,128)(2,1)}, bf16[512,256]{1,0:T(8,128)(2,1)}, u32[]{:S(2)}, u32[]{:S(2)}) %collective-permute-start.9) | collective-permute-done | bytes 262176 | tf_op jit(solution)/shard_map/ppermute | solution.py:51
  137.8 4.4 %all-to-all-start.5 = ((bf16[4,128,256]{2,1,0:T(8,128)(2,1)}), bf16[4,128,256]{2,1,0:T(8,128)(2,1)S(1)}, u32[]{:S(2)}, u32[]{:S(2)}) async-start(bf16[4,128,256]{2,1,0:T(8,128)(2,1)} %shard_map.144), calls=%async_computation.5 | async-start | bytes 524288 | tf_op jit(solution)/shard_map/all_to_all | solution.py:39
  147.9 4.0 %collective-permute-start.13 = (bf16[528,256]{1,0:T(8,128)(2,1)S(1)}, bf16[528,256]{1,0:T(8,128)(2,1)S(1)}, u32[]{:S(2)}, u32[]{:S(2)}) collective-permute-start(bf16[528,256]{1,0:T(8,128)(2,1)S(1)} %get-tuple-element.44), channel_id=1, source_target_pairs={{0,24},{2,26},{4,28},{6,30},{8,0},{10,2},{12,4},{14,6},{16,8},{18,... | collective-permute-start | bytes 811016 | tf_op jit(solution)/shard_map/ppermute | solution.py:51
  152.5 2.9 %collective-permute-done.12.p2 = bf16[528,256]{1,0:T(8,128)(2,1)S(1)} collective-permute-done((bf16[528,256]{1,0:T(8,128)(2,1)S(1)}, bf16[528,256]{1,0:T(8,128)(2,1)S(1)}, u32[]{:S(2)}, u32[]{:S(2)}) %collective-permute-start.12) | collective-permute-done | bytes 270368 | tf_op jit(solution)/shard_map/ppermute | solution.py:51
  155.4 7.7 %collective-permute-done.13.p3 = bf16[528,256]{1,0:T(8,128)(2,1)S(1)} collective-permute-done((bf16[528,256]{1,0:T(8,128)(2,1)S(1)}, bf16[528,256]{1,0:T(8,128)(2,1)S(1)}, u32[]{:S(2)}, u32[]{:S(2)}) %collective-permute-start.13) | collective-permute-done | bytes 270368 | tf_op jit(solution)/shard_map/ppermute | solution.py:51
  164.0 4.2 %all-to-all-start.6 = ((bf16[4,144,256]{2,1,0:T(8,128)(2,1)}), bf16[4,144,256]{2,1,0:T(8,128)(2,1)S(1)}, u32[]{:S(2)}, u32[]{:S(2)}) async-start(bf16[4,144,256]{2,1,0:T(8,128)(2,1)} %shard_map.147), calls=%async_computation.6 | async-start | bytes 589824 | tf_op jit(solution)/shard_map/all_to_all | solution.py:39
  171.0 5.1 %all-to-all-done.6.parts_ref = bf16[4,144,256]{2,1,0:T(8,128)(2,1)S(1)} async-done(((bf16[4,144,256]{2,1,0:T(8,128)(2,1)}), bf16[4,144,256]{2,1,0:T(8,128)(2,1)S(1)}, u32[]{:S(2)}, u32[]{:S(2)}) %all-to-all-start.6) | async-done | bytes 294944 | tf_op jit(solution)/shard_map/all_to_all | solution.py:39
  176.4 4.5 %collective-permute-start.14 = (bf16[128,256]{1,0:T(8,128)(2,1)S(1)}, bf16[128,256]{1,0:T(8,128)(2,1)S(1)}, u32[]{:S(2)}, u32[]{:S(2)}) collective-permute-start(bf16[128,256]{1,0:T(8,128)(2,1)S(1)} %shard_map.148), channel_id=1, source_target_pairs={{32,0},{64,32},{96,64},{128,96},{160,128},{192,160},{224,192},{256... | collective-permute-start | bytes 196616 | tf_op jit(solution)/shard_map/ppermute | solution.py:387
  (109 shorter events, 57.6 us)
Async XLA Ops:
  0.7 37.5 %copy-start.9 = (bf16[1,256,1024]{2,1,0:T(8,128)(2,1)S(1)}, bf16[1,256,1024]{2,1,0:T(8,128)(2,1)}, u32[]{:S(2)}) copy-start(bf16[1,256,1024]{2,1,0:T(8,128)(2,1)} %param.18) | copy-start | bytes 1572868
  4.1 20.5 %all-to-all-start = ((bf16[4,272,256]{2,1,0:T(8,128)(2,1)}), bf16[4,272,256]{2,1,0:T(8,128)(2,1)S(1)}, u32[]{:S(2)}, u32[]{:S(2)}) async-start(bf16[4,272,256]{2,1,0:T(8,128)(2,1)} %broadcast_in_dim.28), calls=%async_computation | async-start | bytes 1114112 | tf_op jit(solution)/shard_map/all_to_all | solution.py:39
  9.4 14.6 %collective-permute-start.3 = (bf16[128,256]{1,0:T(8,128)(2,1)S(1)}, bf16[128,256]{1,0:T(8,128)(2,1)S(1)}, u32[]{:S(2)}, u32[]{:S(2)}) collective-permute-start(bf16[128,256]{1,0:T(8,128)(2,1)S(1)} %bitcast_select_fusion), channel_id=1, source_target_pairs={{0,480},{32,448},{64,416},{96,384},{128,352},{160,320},{192,288},{... | collective-permute-start | bytes 196616 | tf_op jit(solution)/shard_map/ppermute | solution.py:299
  39.2 49.9 %all-to-all-start.2 = ((bf16[16,64,256]{2,1,0:T(8,128)(2,1)}), bf16[16,64,256]{2,1,0:T(8,128)(2,1)S(1)}, u32[]{:S(2)}, u32[]{:S(2)}) async-start(bf16[16,64,256]{2,1,0:T(8,128)(2,1)} %shard_map.139), calls=%async_computation.2 | async-start | bytes 1048576 | tf_op jit(solution)/shard_map/all_to_all | solution.py:322
  44.6 18.6 %collective-permute-start.2 = (bf16[1040,256]{1,0:T(8,128)(2,1)S(1)}, bf16[1040,256]{1,0:T(8,128)(2,1)S(1)}, u32[]{:S(2)}, u32[]{:S(2)}) collective-permute-start(bf16[1040,256]{1,0:T(8,128)(2,1)S(1)} %concatenate.10.f0), channel_id=1, source_target_pairs={{24,0},{26,2},{28,4},{30,6},{0,8},{2,10},{4,12},{6,14},{8,16},{10,... | collective-permute-start | bytes 1597448 | tf_op jit(solution)/shard_map/ppermute | solution.py:47
  47.7 22.6 %collective-permute-start.1 = (bf16[1040,256]{1,0:T(8,128)(2,1)S(1)}, bf16[1040,256]{1,0:T(8,128)(2,1)}, u32[]{:S(2)}, u32[]{:S(2)}) collective-permute-start(bf16[1040,256]{1,0:T(8,128)(2,1)S(1)} %concatenate.10.f0), channel_id=1, source_target_pairs={{16,0},{18,2},{20,4},{22,6},{24,8},{26,10},{28,12},{30,14},{0,16},... | collective-permute-start | bytes 1597448 | tf_op jit(solution)/shard_map/ppermute | solution.py:47
  50.3 28.1 %collective-permute-start = (bf16[1040,256]{1,0:T(8,128)(2,1)S(1)}, bf16[1040,256]{1,0:T(8,128)(2,1)}, u32[]{:S(2)}, u32[]{:S(2)}) collective-permute-start(bf16[1040,256]{1,0:T(8,128)(2,1)S(1)} %concatenate.10.f0), channel_id=1, source_target_pairs={{8,0},{10,2},{12,4},{14,6},{16,8},{18,10},{20,12},{22,14},{24,16},... | collective-permute-start | bytes 1597448 | tf_op jit(solution)/shard_map/ppermute | solution.py:47
  54.2 26.1 %collective-permute-start.6 = (bf16[512,256]{1,0:T(8,128)(2,1)S(1)}, bf16[512,256]{1,0:T(8,128)(2,1)}, u32[]{:S(2)}, u32[]{:S(2)}) collective-permute-start(bf16[512,256]{1,0:T(8,128)(2,1)S(1)} %bitcast.31), channel_id=1, source_target_pairs={{24,0},{26,2},{28,4},{30,6},{0,8},{2,10},{4,12},{6,14},{8,16},{10,... | collective-permute-start | bytes 786440 | tf_op jit(solution)/shard_map/ppermute | solution.py:47
  56.1 27.1 %collective-permute-start.5 = (bf16[512,256]{1,0:T(8,128)(2,1)S(1)}, bf16[512,256]{1,0:T(8,128)(2,1)}, u32[]{:S(2)}, u32[]{:S(2)}) collective-permute-start(bf16[512,256]{1,0:T(8,128)(2,1)S(1)} %bitcast.32), channel_id=1, source_target_pairs={{16,0},{18,2},{20,4},{22,6},{24,8},{26,10},{28,12},{30,14},{0,16},... | collective-permute-start | bytes 786440 | tf_op jit(solution)/shard_map/ppermute | solution.py:47
  64.0 25.0 %collective-permute-start.4 = (bf16[512,256]{1,0:T(8,128)(2,1)S(1)}, bf16[512,256]{1,0:T(8,128)(2,1)}, u32[]{:S(2)}, u32[]{:S(2)}) collective-permute-start(bf16[512,256]{1,0:T(8,128)(2,1)S(1)} %bitcast.33), channel_id=1, source_target_pairs={{8,0},{10,2},{12,4},{14,6},{16,8},{18,10},{20,12},{22,14},{24,16},... | collective-permute-start | bytes 786440 | tf_op jit(solution)/shard_map/ppermute | solution.py:47
  97.4 12.5 %all-to-all-start.3 = ((bf16[4,64,256]{2,1,0:T(8,128)(2,1)}), bf16[4,64,256]{2,1,0:T(8,128)(2,1)S(1)}, u32[]{:S(2)}, u32[]{:S(2)}) async-start(bf16[4,64,256]{2,1,0:T(8,128)(2,1)} %copy-done.13), calls=%async_computation.3 | async-start | bytes 262144 | tf_op jit(solution)/shard_map/all_to_all | solution.py:39
  116.2 13.8 %collective-permute-start.7 = (bf16[512,256]{1,0:T(8,128)(2,1)}, bf16[512,256]{1,0:T(8,128)(2,1)S(1)}, u32[]{:S(2)}, u32[]{:S(2)}) collective-permute-start(bf16[512,256]{1,0:T(8,128)(2,1)} %get-tuple-element.33), channel_id=1, source_target_pairs={{0,8},{2,10},{4,12},{6,14},{8,16},{10,18},{12,20},{14,22},{16,24},... | collective-permute-start | bytes 786440 | tf_op jit(solution)/shard_map/ppermute | solution.py:51
  118.4 11.5 %collective-permute-start.8 = (bf16[512,256]{1,0:T(8,128)(2,1)}, bf16[512,256]{1,0:T(8,128)(2,1)}, u32[]{:S(2)}, u32[]{:S(2)}) collective-permute-start(bf16[512,256]{1,0:T(8,128)(2,1)} %get-tuple-element.34), channel_id=1, source_target_pairs={{0,16},{2,18},{4,20},{6,22},{8,24},{10,26},{12,28},{14,30},{16,0},... | collective-permute-start | bytes 786440 | tf_op jit(solution)/shard_map/ppermute | solution.py:51
  121.5 14.4 %collective-permute-start.9 = (bf16[512,256]{1,0:T(8,128)(2,1)}, bf16[512,256]{1,0:T(8,128)(2,1)}, u32[]{:S(2)}, u32[]{:S(2)}) collective-permute-start(bf16[512,256]{1,0:T(8,128)(2,1)} %get-tuple-element.35), channel_id=1, source_target_pairs={{0,24},{2,26},{4,28},{6,30},{8,0},{10,2},{12,4},{14,6},{16,8},{18,... | collective-permute-start | bytes 786440 | tf_op jit(solution)/shard_map/ppermute | solution.py:51
  125.4 12.4 %all-to-all-start.4 = ((f32[4,64,128]{2,1,0:T(8,128)}), f32[4,64,128]{2,1,0:T(8,128)S(1)}, u32[]{:S(2)}, u32[]{:S(2)}) async-start(f32[4,64,128]{2,1,0:T(8,128)} %get-tuple-element.36), calls=%async_computation.4 | async-start | bytes 262144 | tf_op jit(solution)/shard_map/all_to_all | solution.py:39
  137.8 26.1 %all-to-all-start.5 = ((bf16[4,128,256]{2,1,0:T(8,128)(2,1)}), bf16[4,128,256]{2,1,0:T(8,128)(2,1)S(1)}, u32[]{:S(2)}, u32[]{:S(2)}) async-start(bf16[4,128,256]{2,1,0:T(8,128)(2,1)} %shard_map.144), calls=%async_computation.5 | async-start | bytes 524288 | tf_op jit(solution)/shard_map/all_to_all | solution.py:39
  142.2 34.0 %copy-start.10 = (bf16[1,128,256]{2,1,0:T(8,128)(2,1)S(1)}, bf16[1,128,256]{2,1,0:T(8,128)(2,1)}, u32[]{:S(2)}) copy-start(bf16[1,128,256]{2,1,0:T(8,128)(2,1)} %param.15) | copy-start | bytes 196612
  143.4 39.8 %copy-start.28 = (bf16[128,256]{1,0:T(8,128)(2,1)S(1)}, bf16[128,256]{1,0:T(8,128)(2,1)}, u32[]{:S(2)}) copy-start(bf16[128,256]{1,0:T(8,128)(2,1)} %copy-done.27) | copy-start | bytes 196612
  143.4 9.1 %collective-permute-start.11 = (bf16[528,256]{1,0:T(8,128)(2,1)S(1)}, bf16[528,256]{1,0:T(8,128)(2,1)S(1)}, u32[]{:S(2)}, u32[]{:S(2)}) collective-permute-start(bf16[528,256]{1,0:T(8,128)(2,1)S(1)} %get-tuple-element.42), channel_id=1, source_target_pairs={{0,8},{2,10},{4,12},{6,14},{8,16},{10,18},{12,20},{14,22},{16,24},... | collective-permute-start | bytes 811016 | tf_op jit(solution)/shard_map/ppermute | solution.py:51
  145.5 9.9 %collective-permute-start.12 = (bf16[528,256]{1,0:T(8,128)(2,1)S(1)}, bf16[528,256]{1,0:T(8,128)(2,1)S(1)}, u32[]{:S(2)}, u32[]{:S(2)}) collective-permute-start(bf16[528,256]{1,0:T(8,128)(2,1)S(1)} %get-tuple-element.43), channel_id=1, source_target_pairs={{0,16},{2,18},{4,20},{6,22},{8,24},{10,26},{12,28},{14,30},{16,0},... | collective-permute-start | bytes 811016 | tf_op jit(solution)/shard_map/ppermute | solution.py:51
  147.9 15.2 %collective-permute-start.13 = (bf16[528,256]{1,0:T(8,128)(2,1)S(1)}, bf16[528,256]{1,0:T(8,128)(2,1)S(1)}, u32[]{:S(2)}, u32[]{:S(2)}) collective-permute-start(bf16[528,256]{1,0:T(8,128)(2,1)S(1)} %get-tuple-element.44), channel_id=1, source_target_pairs={{0,24},{2,26},{4,28},{6,30},{8,0},{10,2},{12,4},{14,6},{16,8},{18,... | collective-permute-start | bytes 811016 | tf_op jit(solution)/shard_map/ppermute | solution.py:51
  164.0 12.2 %all-to-all-start.6 = ((bf16[4,144,256]{2,1,0:T(8,128)(2,1)}), bf16[4,144,256]{2,1,0:T(8,128)(2,1)S(1)}, u32[]{:S(2)}, u32[]{:S(2)}) async-start(bf16[4,144,256]{2,1,0:T(8,128)(2,1)} %shard_map.147), calls=%async_computation.6 | async-start | bytes 589824 | tf_op jit(solution)/shard_map/all_to_all | solution.py:39
  168.2 12.6 %collective-permute-start.10 = (bf16[128,256]{1,0:T(8,128)(2,1)S(1)}, bf16[128,256]{1,0:T(8,128)(2,1)S(1)}, u32[]{:S(2)}, u32[]{:S(2)}) collective-permute-start(bf16[128,256]{1,0:T(8,128)(2,1)S(1)} %shard_map.145), channel_id=1, source_target_pairs={{0,32},{32,64},{64,96},{96,128},{128,160},{160,192},{192,224},{224... | collective-permute-start | bytes 196616 | tf_op jit(solution)/shard_map/ppermute | solution.py:370
  176.4 6.2 %collective-permute-start.14 = (bf16[128,256]{1,0:T(8,128)(2,1)S(1)}, bf16[128,256]{1,0:T(8,128)(2,1)S(1)}, u32[]{:S(2)}, u32[]{:S(2)}) collective-permute-start(bf16[128,256]{1,0:T(8,128)(2,1)S(1)} %shard_map.148), channel_id=1, source_target_pairs={{32,0},{64,32},{96,64},{128,96},{160,128},{192,160},{224,192},{256... | collective-permute-start | bytes 196616 | tf_op jit(solution)/shard_map/ppermute | solution.py:387
  (27 other events, 196.2 us)

commit v3 on v1

v3 whole, which is shorter than its diff:
```python
import functools

import jax
import jax.numpy as jnp
import numpy as np
from jax import lax
from jax.experimental import pallas as pl
from jax.experimental.pallas import tpu as pltpu
from jax.sharding import PartitionSpec as P

HEADS = 32
KVH = 4
HD = 128
TOK = 128
WIDTH = 4096
COLS = 256
SIDE = 4
norm_eps = 1e-05
MIB = 1024 * 1024

FIRST, SECOND = 0, 1


def tensor_rows(section, order):
    if (section + order) % 2 == 0:
        return [[x * SIDE + y for y in range(SIDE)] for x in range(SIDE)]
    return [[x * SIDE + y for x in range(SIDE)] for y in range(SIDE)]


NN = (((1,), (0,)), ((), ()))
NT = (((1,), (1,)), ((), ()))
TN = (((0,), (0,)), ((), ()))


def rope_angles():
    inverse = 10000.0 ** (-2.0 * np.arange(HD // 2, dtype=np.float64) / HD)
    angles = np.arange(TOK, dtype=np.float64)[:, None] * inverse[None, :]
    return np.cos(angles).astype(np.float32), np.sin(angles).astype(np.float32)


def matmul(left, right, dims):
    return lax.dot_general(left, right, dims, preferred_element_type=jnp.float32)


def exchange(blocks, order):
    sections = range(lax.axis_size("section"))
    groups = [[s * 16 + t for t in row] for s in sections for row in tensor_rows(s, order)]
    return lax.all_to_all(blocks, ("section", "tensor"), 0, 0, axis_index_groups=groups)


def exchange_heads(blocks):
    return lax.all_to_all(blocks, "tensor", 0, 0, axis_index_groups=tensor_rows(0, FIRST))


def call(kernel, outs, *operands, vmem=32, flops=0):
    nbytes = sum(int(np.prod(a.shape)) * a.dtype.itemsize for a in (*operands, *outs))
    specs = [
        pl.BlockSpec(memory_space=pltpu.SMEM if a.shape == (3,) else pltpu.VMEM) for a in operands
    ]
    return pl.pallas_call(
        kernel,
        out_shape=outs,
        in_specs=specs,
        compiler_params=pltpu.CompilerParams(vmem_limit_bytes=vmem * MIB),
        cost_estimate=pl.CostEstimate(flops=flops, bytes_accessed=nbytes, transcendentals=0),
    )(*operands)


def shape(dims, dtype=jnp.bfloat16):
    return jax.ShapeDtypeStruct(dims, dtype)


def block_index(pos_ref, k, j):
    return k * pos_ref[0] + j * pos_ref[1]


def weight_rows(t):
    return pl.ds(pl.multiple_of(t * COLS, COLS), COLS)


def pack_kv_weight(pos_ref, w_ref, out_ref):
    swapped = pos_ref[1] > 1
    for x in range(SIDE):
        keys = w_ref[:, x * HD : (x + 1) * HD].T
        values = w_ref[:, (KVH + x) * HD : (KVH + x + 1) * HD].T
        for y in range(SIDE):
            k, j = jnp.where(swapped, y, x), jnp.where(swapped, x, y)
            out_ref[k, j, 0:16] = keys[16 * y : 16 * y + 16]
            out_ref[k, j, 16:32] = keys[64 + 16 * y : 80 + 16 * y]
            out_ref[k, j, 32:64] = values[32 * y : 32 * y + 32]


def first_blocks(rows_ref, back_ref, cot_ref, gain_ref, kvw_ref, out_ref):
    gain = gain_ref[...]
    row = lax.broadcasted_iota(jnp.int32, (16, COLS), 0)
    high = gain.astype(jnp.bfloat16).astype(jnp.float32)
    middle = (gain - high).astype(jnp.bfloat16).astype(jnp.float32)
    low = gain - high - middle
    gains = jnp.where(row == 0, high, jnp.where(row == 1, middle, jnp.where(row == 2, low, 0.0)))
    for j in range(SIDE):
        out_ref[j, 0:TOK] = rows_ref[...]
        out_ref[j, TOK : 2 * TOK] = back_ref[...]
        out_ref[j, 2 * TOK : 3 * TOK] = cot_ref[...]
        out_ref[j, 384:400] = gains.astype(jnp.bfloat16)
        for k in range(SIDE):
            out_ref[j, 400 + 64 * k : 464 + 64 * k] = kvw_ref[k, j]


def second_blocks(parts_ref, out_ref):
    row = lax.broadcasted_iota(jnp.int32, (16, COLS), 0)
    gains = jnp.zeros((16, COLS), jnp.float32)
    for j in range(SIDE):
        part = parts_ref[j, 384:400].astype(jnp.float32)
        for i in range(3):
            gains = jnp.where(row == 3 * j + i, part[i : i + 1], gains)
    gains = gains.astype(jnp.bfloat16)
    for k in range(SIDE):
        for j in range(SIDE):
            out_ref[k, j * 384 : (j + 1) * 384] = parts_ref[j, 0:384]
        out_ref[k, 1536:1552] = gains


def norm_and_kv(pos_ref, rows_ref, first_ref, table_ref, normed_ref, kv_ref, raw_ref, factor_ref):
    total = jnp.zeros((2 * TOK, COLS), jnp.float32)
    for k in range(SIDE):
        for j in range(SIDE):
            block = rows_ref[k, j * 384 : j * 384 + 256].astype(jnp.float32)
            total = total + block * block
    factor = lax.rsqrt(jnp.sum(total, axis=1, keepdims=True) / WIDTH + norm_eps)
    factor_ref[...] = jnp.broadcast_to(factor[TOK:], (TOK, HD))
    kv = jnp.zeros((64, 2 * TOK), jnp.float32)
    for k in range(SIDE):
        gains = rows_ref[k, 1536:1552].astype(jnp.float32)
        for j in range(SIDE):
            gain = gains[3 * j : 3 * j + 1] + gains[3 * j + 1 : 3 * j + 2] + gains[3 * j + 2 : 3 * j + 3]
            block = rows_ref[k, j * 384 : j * 384 + 256].astype(jnp.float32)
            normed = (block * factor * gain).astype(jnp.bfloat16)
            normed_ref[k * SIDE + j] = normed
            kv = kv + matmul(first_ref[j, 400 + 64 * k : 464 + 64 * k], normed, NT)
    raw_ref[...] = kv[:, TOK:]
    first, second = kv[0:16], kv[16:32]
    start = pl.multiple_of(pos_ref[2] * 16, 16)
    cos, sin = table_ref[pl.ds(256 + start, 16)], table_ref[pl.ds(320 + start, 16)]
    cos, sin = jnp.concatenate([cos, cos], axis=1), jnp.concatenate([sin, sin], axis=1)
    out = jnp.concatenate([first * cos - second * sin, second * cos + first * sin, kv[32:64]], axis=0)
    out = out.astype(jnp.bfloat16)
    for y in range(SIDE):
        kv_ref[y] = out


def attention(
    pos_ref, rows_ref, normed_ref, kv_ref, qw_ref, ow_ref, table_ref,
    attended_ref, grad_query_ref, grad_kv_ref, mixed_ref,
):
    query = jnp.zeros((2 * TOK, COLS), jnp.float32)
    grad_out = jnp.zeros((TOK, COLS), jnp.float32)
    for k in range(SIDE):
        for j in range(SIDE):
            block = weight_rows(block_index(pos_ref, k, j))
            query = query + matmul(normed_ref[k * SIDE + j], qw_ref[block, :], NN)
            cot = rows_ref[k, j * 384 + 256 : j * 384 + 384]
            grad_out = grad_out + matmul(cot, ow_ref[:, block], NT)
    grad_out = grad_out.astype(jnp.bfloat16)
    kv = [kv_ref[y] for y in range(SIDE)]
    cos, sin = table_ref[0:128], table_ref[128:256]
    scale = HD ** (-0.5)
    causal = lax.broadcasted_iota(jnp.int32, (TOK, TOK), 0) >= lax.broadcasted_iota(
        jnp.int32, (TOK, TOK), 1
    )

    def softmax(scores):
        scores = jnp.where(causal, scores, -1e30)
        shifted = jnp.exp(scores - jnp.max(scores, axis=-1, keepdims=True))
        return shifted / jnp.sum(shifted, axis=-1, keepdims=True)

    def keys_values(start):
        part = [k[:, start : start + TOK] for k in kv]
        keys = jnp.concatenate([p[0:16] for p in part] + [p[16:32] for p in part], axis=0)
        return keys, jnp.concatenate([p[32:64] for p in part], axis=0)

    def heads(start, h):
        raw = query[start : start + TOK, h * HD : (h + 1) * HD]
        turned = raw * cos + pltpu.roll(raw, HD // 2, 1) * sin
        return raw, (turned * scale).astype(jnp.bfloat16)

    keys, values = keys_values(0)
    for h in range(2):
        _, query_head = heads(0, h)
        weights = softmax(matmul(query_head, keys, NN)).astype(jnp.bfloat16)
        attended_ref[:, h * HD : (h + 1) * HD] = matmul(weights, values, NT).astype(jnp.bfloat16)

    keys, values = keys_values(TOK)
    grad_key = jnp.zeros((HD, TOK), jnp.float32)
    grad_value = jnp.zeros((HD, TOK), jnp.float32)
    mixed = jnp.zeros((TOK, HD), jnp.float32)
    for h in range(2):
        raw, query_head = heads(TOK, h)
        probs = softmax(matmul(query_head, keys, NN))
        grad_head = grad_out[:, h * HD : (h + 1) * HD]
        grad_probs = matmul(grad_head, values, NN)
        delta = jnp.sum(probs * grad_probs, axis=-1, keepdims=True)
        grad_scores = (probs * (grad_probs - delta)).astype(jnp.bfloat16)
        turned = matmul(grad_scores, keys, NT)
        grad_query = (turned * cos - pltpu.roll(turned, HD // 2, 1) * sin) * scale
        grad_query = grad_query.astype(jnp.bfloat16)
        grad_query_ref[:, h * HD : (h + 1) * HD] = grad_query
        mixed = mixed + grad_query.astype(jnp.float32) * raw
        grad_key = grad_key + matmul(query_head, grad_scores, TN)
        grad_value = grad_value + matmul(grad_head, probs.astype(jnp.bfloat16), TN)
    cost, sint = table_ref[256:320], table_ref[320:384]
    first, second = grad_key[:64], grad_key[64:]
    key_first = first * cost + second * sint
    key_second = second * cost - first * sint
    for y in range(SIDE):
        grad_kv_ref[y, 0:16] = key_first[16 * y : 16 * y + 16]
        grad_kv_ref[y, 16:32] = key_second[16 * y : 16 * y + 16]
        grad_kv_ref[y, 32:64] = grad_value[32 * y : 32 * y + 32]
    mixed_ref[...] = jnp.broadcast_to(jnp.sum(mixed.T, axis=0, keepdims=True), (8, TOK))


def split_rows(total):
    high = total.astype(jnp.bfloat16)
    low = (total - high.astype(jnp.float32)).astype(jnp.bfloat16)
    row = lax.broadcasted_iota(jnp.int32, (16, TOK), 0)
    both = jnp.where(row == 0, high.astype(jnp.float32), low.astype(jnp.float32))
    both = jnp.where(row < 2, both, 0.0)
    return jnp.concatenate([both, jnp.zeros((16, COLS - TOK), jnp.float32)], axis=1).astype(jnp.bfloat16)


def project(
    pos_ref, attended_ref, grad_query_ref, grad_kv_ref, raw_ref, mixed_ref, qw_ref, ow_ref, first_ref, out_ref
):
    attended = attended_ref[...]
    grad_query = grad_query_ref[...]
    grad_kv = grad_kv_ref[0] + grad_kv_ref[1] + grad_kv_ref[2] + grad_kv_ref[3]
    grad_kv = grad_kv.astype(jnp.bfloat16)
    mixed = mixed_ref[0:1] + jnp.sum(grad_kv.astype(jnp.float32) * raw_ref[...], axis=0, keepdims=True)
    rows = split_rows(mixed)
    for k in range(SIDE):
        for j in range(SIDE):
            block = weight_rows(block_index(pos_ref, k, j))
            term = matmul(attended, ow_ref[:, block], NN)
            out_ref[k, j * 256 : j * 256 + TOK] = term.astype(jnp.bfloat16)
            term = matmul(grad_query, qw_ref[block, :], NT)
            term = term + matmul(grad_kv, first_ref[j, 400 + 64 * k : 464 + 64 * k], TN)
            out_ref[k, j * 256 + TOK : j * 256 + 256] = term.astype(jnp.bfloat16)
        out_ref[k, 1024:1040] = rows


def sum_second(parts_ref, out_ref):
    rows = jnp.zeros((16, COLS), jnp.float32)
    for k in range(SIDE):
        rows = rows + parts_ref[k, 1024:1040].astype(jnp.float32)
    mixed = split_rows(rows[0:1, :TOK] + rows[1:2, :TOK])
    for j in range(SIDE):
        total = jnp.zeros((256, COLS), jnp.float32)
        for k in range(SIDE):
            total = total + parts_ref[k, j * 256 : j * 256 + 256].astype(jnp.float32)
        out_ref[j, 0:256] = total.astype(jnp.bfloat16)
        out_ref[j, 256:272] = mixed


def finish(parts_ref, rows_ref, back_ref, cot_ref, gain_ref, factor_ref, out_ref, grad_ref):
    total = parts_ref[0].astype(jnp.float32)
    for j in range(1, SIDE):
        total = total + parts_ref[j].astype(jnp.float32)
    out_ref[...] = (rows_ref[...].astype(jnp.float32) + total[0:TOK]).astype(jnp.bfloat16)
    mixed = jnp.broadcast_to(total[256:257, :TOK] + total[257:258, :TOK], (TOK, TOK)).T[:, 0:1]
    factor = factor_ref[:, 0:1]
    scaled = total[TOK : 2 * TOK] * gain_ref[...]
    grad_rows = factor * scaled - back_ref[...].astype(jnp.float32) * (factor * factor * mixed / WIDTH)
    grad_ref[...] = (cot_ref[...].astype(jnp.float32) + grad_rows).astype(jnp.bfloat16)


def per_device(
    section_input,
    stash_pool,
    reload_slot,
    cotangent,
    norm_gain,
    query_weight,
    kv_weight,
    out_weight,
):
    token_rows = section_input[0]
    cot_rows = cotangent[0]
    query_w = query_weight[0]
    kv_w = kv_weight[0]
    out_w = out_weight[0]
    section_count = lax.axis_size("section")
    section_pos = lax.axis_index("section")
    is_early = section_pos < section_count // 2

    picked = lax.dynamic_index_in_dim(stash_pool[0], reload_slot[0], 0, keepdims=False)
    sending = jnp.where(is_early, token_rows, picked)
    mirrored = [(s, section_count - 1 - s) for s in range(section_count)]
    received = lax.ppermute(sending, "section", mirrored)
    back_rows = jnp.where(is_early, received, token_rows)

    tensor_pos = lax.axis_index("tensor").astype(jnp.int32)
    odd = (section_pos % 2).astype(jnp.int32)
    pos = jnp.stack([SIDE - 3 * odd, 1 + 3 * odd, tensor_pos % SIDE])
    cos, sin = rope_angles()
    wide = np.concatenate([cos, cos], axis=1), np.concatenate([-sin, sin], axis=1)
    table = jnp.asarray(np.concatenate([*wide, cos.T, sin.T], axis=0))

    packed = call(pack_kv_weight, (shape((SIDE, SIDE, 64, COLS)),), pos, kv_w)[0]
    packed = exchange(packed, SECOND)
    gain_row = norm_gain
    blocks = call(
        first_blocks, (shape((SIDE, 656, COLS)),), token_rows, back_rows, cot_rows, gain_row, packed
    )[0]
    first = exchange(blocks, FIRST)
    blocks = call(second_blocks, (shape((SIDE, 1552, COLS)),), first)[0]
    rows = exchange(blocks, SECOND)

    normed, kv_own, kv_raw, factor = call(
        norm_and_kv,
        (
            shape((16, 2 * TOK, COLS)),
            shape((SIDE, 64, 2 * TOK)),
            shape((64, TOK), jnp.float32),
            shape((TOK, HD), jnp.float32),
        ),
        pos, rows, first, table,
        flops=2 * 64 * 256 * 4096,
    )
    kv_all = exchange_heads(kv_own)
    attended, grad_query, grad_kv, mixed = call(
        attention,
        (
            shape((TOK, COLS)),
            shape((TOK, COLS)),
            shape((SIDE, 64, TOK), jnp.float32),
            shape((8, TOK), jnp.float32),
        ),
        pos, rows, normed, kv_all, query_w, out_w, table,
        flops=2 * 384 * 256 * 4096,
    )
    grad_kv = exchange_heads(grad_kv)
    terms = call(
        project,
        (shape((SIDE, 1040, COLS)),),
        pos, attended, grad_query, grad_kv, kv_raw, mixed, query_w, out_w, first,
        flops=2 * 256 * 256 * 4096,
    )[0]
    terms = exchange(terms, SECOND)
    terms = call(sum_second, (shape((SIDE, 272, COLS)),), terms)[0]
    terms = exchange(terms, FIRST)
    layer_out, grad_local = call(
        finish,
        (shape((TOK, COLS)), shape((TOK, COLS))),
        terms, token_rows, back_rows, cot_rows, gain_row, factor,
    )
    next_input = lax.ppermute(layer_out, "section", [(s, s + 1) for s in range(section_count - 1)])
    input_grad = lax.ppermute(grad_local, "section", [(s + 1, s) for s in range(section_count - 1)])
    return (next_input[None], received[None], input_grad[None])


def solution(mesh):
    return jax.shard_map(
        per_device,
        mesh=mesh,
        in_specs=(
            P("section", "dp", "tensor"),
            P("section", None, "dp", "tensor"),
            P("section"),
            P("section", "dp", "tensor"),
            P("section", "tensor"),
            P("section", None, "tensor"),
            P("section", "tensor", None),
            P("section", "tensor", None),
        ),
        out_specs=(
            P("section", "dp", "tensor"),
            P("section", "dp", "tensor"),
            P("section", "dp", "tensor"),
        ),
        check_vma=False,
    )
```

time: 185 us -> 158 us (0.85)
  waiting for transfers between devices: 77 us -> 6.88 us
  blocking collectives: 50.5 us -> 117 us
  starting transfers between devices: 36.2 us -> 20.7 us
  local copies, waits for them, and re-layouts: 9.71 us -> 2.96 us
  other arithmetic: 2.42 us -> 0.1 us
  Pallas kernels: 6.32 us -> 8.58 us
    all_to_all x3 -> x1, waiting for transfers between devices: 70.7 us -> 0.01 us  [exchange(): lax.all_to_all(blocks, ('section', 'tensor'), 0, 0, axis_index_groups=gro...]
    all_to_all x4 -> x6, blocking collectives: 50.5 us -> 117 us  [the longest x4 101 us: exchange(): lax.all_to_all(blocks, ('section', 'tensor'), 0, 0, axis_index_groups=gro...]
    all_to_all x3 -> x1, starting transfers between devices: 13.3 us -> 5.42 us  [exchange(): lax.all_to_all(blocks, ('section', 'tensor'), 0, 0, axis_index_groups=gro...]
    ppermute x1, starting transfers between devices: 8.9 us -> 1.92 us  [per_device(): lax.ppermute(layer_out, 'section', [(s, s + 1) for s in range(section_cou...]
    broadcast_in_dim x4 -> x0, local copies, waits for them, and re-layouts: 2.81 us -> none  [the longest x1 1.85 us: per_device(): jnp.broadcast_to(column[None], (SIDE,) + column.shape)]
    pallas_call x6 -> x8, Pallas kernels: 6.32 us -> 8.58 us  [call(): pl.pallas_call(kernel, out_shape=outs, in_specs=specs, compiler_params=pl...]
    concatenate x2 -> x0, local copies, waits for them, and re-layouts: 2.08 us -> none  [the longest x1 1.84 us: per_device(): jnp.concatenate([token_rows, back_rows, cot_rows, gains.astype(jnp.bfloat...]
    unnamed x33 -> x19, local copies, waits for them, and re-layouts: 4.72 us -> 2.96 us
  transfers between devices with their start and end apart: 6 -> 4, of which waited for: 5 -> 2; matrix products, arithmetic and copies ran while one was open for 1% -> 0% of each run, Pallas kernels for 1% -> 0%
where the time goes in v3:
time: 158 us; the launch traced here: 157 us
  blocking collectives  117 us (74%)
  starting transfers between devices  20.7 us (13%)
  Pallas kernels  8.58 us (5%)
  waiting for transfers between devices  6.88 us (4%)
  local copies, waits for them, and re-layouts  2.96 us (2%)
    all_to_all x4, blocking collectives, exchange(): lax.all_to_all(blocks, ('section', 'tensor'), 0, 0, axis_index_groups=gro...  101 us
    all_to_all x2, blocking collectives, exchange_heads(): lax.all_to_all(blocks, 'tensor', 0, 0, axis_index_groups=tensor_rows(0, F...  15.2 us
    ppermute x1, starting transfers between devices, per_device(): received = lax.ppermute(sending, 'section', mirrored)  10.9 us
    pallas_call x8, Pallas kernels, call(): pl.pallas_call(kernel, out_shape=outs, in_specs=specs, compiler_params=pl...  8.58 us
    all_to_all x1, starting transfers between devices, exchange(): lax.all_to_all(blocks, ('section', 'tensor'), 0, 0, axis_index_groups=gro...  5.42 us
    ppermute x1, waiting for transfers between devices, per_device(): received = lax.ppermute(sending, 'section', mirrored)  3.71 us
    ppermute x1, waiting for transfers between devices, per_device(): lax.ppermute(grad_local, 'section', [(s + 1, s) for s in range(section_co...  3.16 us
  transfers between devices with their start and end apart: 4, of which 2 were waited for; matrix products, arithmetic and copies ran while one was open for 0% of the time, Pallas kernels for 0%

profile of v3, /device:TPU:1, one launch (start us, length us, event | category | flops | bytes accessed | tf_op | source)
XLA Modules:
  0.0 157.2 jit_solution(18380453271803318288)
XLA Ops:
  0.8 1.0 copy-done.4
  1.8 1.5 shard_map.112
  3.3 5.4 %all-to-all-start = ((bf16[4,4,64,256]{3,2,1,0:T(8,128)(2,1)}), bf16[4,4,64,256]{3,2,1,0:T(8,128)(2,1)S(1)}, u32[]{:S(2)}, u32[]{:S(2)}) async-start(bf16[4,4,64,256]{3,2,1,0:T(8,128)(2,1)} %shard_map.112), calls=%async_computation | async-start | bytes 1048576 | tf_op jit(solution)/shard_map/all_to_all | solution.py:48
  9.4 10.9 %collective-permute-start = (bf16[128,256]{1,0:T(8,128)(2,1)S(1)}, bf16[128,256]{1,0:T(8,128)(2,1)S(1)}, u32[]{:S(2)}, u32[]{:S(2)}) collective-permute-start(bf16[128,256]{1,0:T(8,128)(2,1)S(1)} %bitcast_select_fusion), channel_id=1, source_target_pairs={{0,480},{32,448},{64,416},{96,384},{128,352},{160,320},{192,288},{... | collective-permute-start | bytes 196616 | tf_op jit(solution)/shard_map/ppermute | solution.py:297
  20.4 3.7 %collective-permute-done = bf16[128,256]{1,0:T(8,128)(2,1)S(1)} collective-permute-done((bf16[128,256]{1,0:T(8,128)(2,1)S(1)}, bf16[128,256]{1,0:T(8,128)(2,1)S(1)}, u32[]{:S(2)}, u32[]{:S(2)}) %collective-permute-start) | collective-permute-done | bytes 65568 | tf_op jit(solution)/shard_map/ppermute | solution.py:297
  24.1 0.1 shard_map.113
  24.2 15.1 %all_to_all.35.parts_ref.first_ref = bf16[4,656,256]{2,1,0:T(8,128)(2,1)S(1)} all-to-all(bf16[4,656,256]{2,1,0:T(8,128)(2,1)S(1)} %shard_map.113), channel_id=1, replica_groups={{0,2,4,6},{8,10,12,14},{16,18,20,22},{24,26,28,30},{32,40,48,56},{34,42..., dimensions={0} | all-to-all | bytes 2686976 | tf_op jit(solution)/shard_map/all_to_all | solution.py:48
  39.3 0.2 shard_map.114
  39.5 42.1 %all_to_all.36.rows_ref = bf16[4,1552,256]{2,1,0:T(8,128)(2,1)S(1)} all-to-all(bf16[4,1552,256]{2,1,0:T(8,128)(2,1)S(1)} %shard_map.114), channel_id=1, replica_groups={{0,8,16,24},{2,10,18,26},{4,12,20,28},{6,14,22,30},{32,34,36,38},{40,42..., dimensions={0} | all-to-all | bytes 6356992 | tf_op jit(solution)/shard_map/all_to_all | solution.py:48
  81.7 1.7 %shard_map.115 = (bf16[16,256,256]{2,1,0:T(8,128)(2,1)S(1)}, bf16[4,64,256]{2,1,0:T(8,128)(2,1)S(1)}, f32[64,128]{1,0:T(8,128)S(1)}, f32[128,128]{1,0:T(8,128)S(1)}) custom-call(s32[3]{0:T(128)S(1)} %pad_add_fusion.pos_ref, bf16[4,1552,256]{2,1,0:T(8,128)(2,1)S(1)} %all_to_all.36.rows_ref, bf16[4,656,256]{2,1,0:T(8,128)(2,1)S(1)} %all_to_all.35.parts_ref.first_ref, ...), custom_call_target="tpu_custom_call" | custom-call | flops 134217728 | bytes 7045132 | tf_op jit(solution)/shard_map/pallas_call | solution.py:60
  83.4 7.7 %all_to_all.37.kv_ref = bf16[4,64,256]{2,1,0:T(8,128)(2,1)S(1)} all-to-all(bf16[4,64,256]{2,1,0:T(8,128)(2,1)S(1)} %get-tuple-element.14), channel_id=1, replica_groups={{0,2,4,6},{8,10,12,14},{16,18,20,22},{24,26,28,30},{1,3,5,7},{9,11,13,1..., dimensions={0} | all-to-all | bytes 262144 | tf_op jit(solution)/shard_map/all_to_all | solution.py:52
  91.1 2.6 %shard_map.116 = (bf16[128,256]{1,0:T(8,128)(2,1)S(1)}, bf16[128,256]{1,0:T(8,128)(2,1)S(1)}, f32[4,64,128]{2,1,0:T(8,128)S(1)}, f32[8,128]{1,0:T(8,128)S(1)}) custom-call(s32[3]{0:T(128)S(1)} %pad_add_fusion.pos_ref, bf16[4,1552,256]{2,1,0:T(8,128)(2,1)S(1)} %all_to_all.36.rows_ref, bf16[16,256,256]{2,1,0:T(8,128)(2,1)S(1)} %get-tuple-element.13.normed_ref, ...), custom_call_target="tpu_custom_call" | custom-call | flops 805306368 | bytes 10063884 | tf_op jit(solution)/shard_map/pallas_call | solution.py:60
  93.8 7.4 %all_to_all.38.grad_kv_ref = f32[4,64,128]{2,1,0:T(8,128)S(1)} all-to-all(f32[4,64,128]{2,1,0:T(8,128)S(1)} %get-tuple-element.17), channel_id=1, replica_groups={{0,2,4,6},{8,10,12,14},{16,18,20,22},{24,26,28,30},{1,3,5,7},{9,11,13,1..., dimensions={0} | all-to-all | bytes 262144 | tf_op jit(solution)/shard_map/all_to_all | solution.py:52
  101.2 2.0 %shard_map.117 = bf16[4,1040,256]{2,1,0:T(8,128)(2,1)S(1)} custom-call(s32[3]{0:T(128)S(1)} %pad_add_fusion.pos_ref, bf16[128,256]{1,0:T(8,128)(2,1)S(1)} %get-tuple-element.15.attended_ref, bf16[128,256]{1,0:T(8,128)(2,1)S(1)} %get-tuple-element.16.grad_query_ref, f32[4,64,128]{2,1,0:T(8,128)S(1)} %all_to_all.38.grad_kv_ref, ...), custom_call_target="tpu_custom_call" | custom-call | flops 536870912 | bytes 7966732 | tf_op jit(solution)/shard_map/pallas_call | solution.py:60
  103.2 34.3 %all_to_all.39.parts_ref = bf16[4,1040,256]{2,1,0:T(8,128)(2,1)S(1)} all-to-all(bf16[4,1040,256]{2,1,0:T(8,128)(2,1)S(1)} %shard_map.117), channel_id=1, replica_groups={{0,8,16,24},{2,10,18,26},{4,12,20,28},{6,14,22,30},{32,34,36,38},{40,42..., dimensions={0} | all-to-all | bytes 4259840 | tf_op jit(solution)/shard_map/all_to_all | solution.py:48
  137.4 0.3 shard_map.118
  137.7 9.9 %all_to_all.40.parts_ref = bf16[4,272,256]{2,1,0:T(8,128)(2,1)S(1)} all-to-all(bf16[4,272,256]{2,1,0:T(8,128)(2,1)S(1)} %shard_map.118), channel_id=1, replica_groups={{0,2,4,6},{8,10,12,14},{16,18,20,22},{24,26,28,30},{32,40,48,56},{34,42..., dimensions={0} | all-to-all | bytes 1114112 | tf_op jit(solution)/shard_map/all_to_all | solution.py:48
  147.6 0.2 shard_map.119
  147.7 1.9 %collective-permute-start.1 = (bf16[128,256]{1,0:T(8,128)(2,1)S(1)}, bf16[128,256]{1,0:T(8,128)(2,1)S(1)}, u32[]{:S(2)}, u32[]{:S(2)}) collective-permute-start(bf16[128,256]{1,0:T(8,128)(2,1)S(1)} %get-tuple-element.21), channel_id=1, source_target_pairs={{0,32},{32,64},{64,96},{96,128},{128,160},{160,192},{192,224},{224... | collective-permute-start | bytes 196616 | tf_op jit(solution)/shard_map/ppermute | solution.py:355
  149.7 2.4 %collective-permute-start.2 = (bf16[128,256]{1,0:T(8,128)(2,1)S(1)}, bf16[128,256]{1,0:T(8,128)(2,1)S(1)}, u32[]{:S(2)}, u32[]{:S(2)}) collective-permute-start(bf16[128,256]{1,0:T(8,128)(2,1)S(1)} %get-tuple-element.22), channel_id=1, source_target_pairs={{32,0},{64,32},{96,64},{128,96},{160,128},{192,160},{224,192},{256... | collective-permute-start | bytes 196616 | tf_op jit(solution)/shard_map/ppermute | solution.py:356
  152.1 3.2 %collective-permute-done.2 = bf16[128,256]{1,0:T(8,128)(2,1)S(1)} collective-permute-done((bf16[128,256]{1,0:T(8,128)(2,1)S(1)}, bf16[128,256]{1,0:T(8,128)(2,1)S(1)}, u32[]{:S(2)}, u32[]{:S(2)}) %collective-permute-start.2) | collective-permute-done | bytes 65568 | tf_op jit(solution)/shard_map/ppermute | solution.py:356
  155.3 0.6 copy.16
  155.9 0.6 copy.17
  156.5 0.6 copy.18
  (20 shorter events, 0.1 us)
Async XLA Ops:
  0.6 8.8 %copy-start.2 = (bf16[1,128,256]{2,1,0:T(8,128)(2,1)S(1)}, bf16[1,128,256]{2,1,0:T(8,128)(2,1)}, u32[]{:S(2)}) copy-start(bf16[1,128,256]{2,1,0:T(8,128)(2,1)} %param.9) | copy-start | bytes 196612
  0.6 23.5 %copy-start.6 = (f32[1,256]{1,0:T(1,128)S(1)}, f32[1,256]{1,0:T(1,128)}, u32[]{:S(2)}) copy-start(f32[1,256]{1,0:T(1,128)} %gain_ref.3) | copy-start | bytes 3076
  0.7 1.0 copy-start.4
  1.8 7.6 %copy-start.7 = (bf16[1,2,128,256]{3,2,1,0:T(8,128)(2,1)S(1)}, bf16[1,2,128,256]{3,2,1,0:T(8,128)(2,1)}, u32[]{:S(2)}) copy-start(bf16[1,2,128,256]{3,2,1,0:T(8,128)(2,1)} %param.10) | copy-start | bytes 393220
  1.8 22.3 %copy-start.5 = (bf16[1,128,256]{2,1,0:T(8,128)(2,1)S(1)}, bf16[1,128,256]{2,1,0:T(8,128)(2,1)}, u32[]{:S(2)}) copy-start(bf16[1,128,256]{2,1,0:T(8,128)(2,1)} %param.12) | copy-start | bytes 196612
  3.3 20.8 %all-to-all-start = ((bf16[4,4,64,256]{3,2,1,0:T(8,128)(2,1)}), bf16[4,4,64,256]{3,2,1,0:T(8,128)(2,1)S(1)}, u32[]{:S(2)}, u32[]{:S(2)}) async-start(bf16[4,4,64,256]{3,2,1,0:T(8,128)(2,1)} %shard_map.112), calls=%async_computation | async-start | bytes 1048576 | tf_op jit(solution)/shard_map/all_to_all | solution.py:48
  9.4 14.7 %collective-permute-start = (bf16[128,256]{1,0:T(8,128)(2,1)S(1)}, bf16[128,256]{1,0:T(8,128)(2,1)S(1)}, u32[]{:S(2)}, u32[]{:S(2)}) collective-permute-start(bf16[128,256]{1,0:T(8,128)(2,1)S(1)} %bitcast_select_fusion), channel_id=1, source_target_pairs={{0,480},{32,448},{64,416},{96,384},{128,352},{160,320},{192,288},{... | collective-permute-start | bytes 196616 | tf_op jit(solution)/shard_map/ppermute | solution.py:297
  39.5 42.2 %copy-start.3 = (f32[384,128]{1,0:T(8,128)S(1)}, f32[384,128]{1,0:T(8,128)}, u32[]{:S(2)}) copy-start(f32[384,128]{1,0:T(8,128)} %constant.44.clone.table_ref) | copy-start | bytes 589828
  81.7 9.5 %copy-start = (bf16[1,4096,256]{2,1,0:T(8,128)(2,1)S(1)}, bf16[1,4096,256]{2,1,0:T(8,128)(2,1)}, u32[]{:S(2)}) copy-start(bf16[1,4096,256]{2,1,0:T(8,128)(2,1)} %param.14) | copy-start | bytes 6291460
  81.7 9.5 %copy-start.1 = (bf16[1,256,4096]{2,1,0:T(8,128)(2,1)S(1)}, bf16[1,256,4096]{2,1,0:T(8,128)(2,1)}, u32[]{:S(2)}) copy-start(bf16[1,256,4096]{2,1,0:T(8,128)(2,1)} %param.16) | copy-start | bytes 6291460
  147.7 4.3 %collective-permute-start.1 = (bf16[128,256]{1,0:T(8,128)(2,1)S(1)}, bf16[128,256]{1,0:T(8,128)(2,1)S(1)}, u32[]{:S(2)}, u32[]{:S(2)}) collective-permute-start(bf16[128,256]{1,0:T(8,128)(2,1)S(1)} %get-tuple-element.21), channel_id=1, source_target_pairs={{0,32},{32,64},{64,96},{96,128},{128,160},{160,192},{192,224},{224... | collective-permute-start | bytes 196616 | tf_op jit(solution)/shard_map/ppermute | solution.py:355
  149.7 5.6 %collective-permute-start.2 = (bf16[128,256]{1,0:T(8,128)(2,1)S(1)}, bf16[128,256]{1,0:T(8,128)(2,1)S(1)}, u32[]{:S(2)}, u32[]{:S(2)}) collective-permute-start(bf16[128,256]{1,0:T(8,128)(2,1)S(1)} %get-tuple-element.22), channel_id=1, source_target_pairs={{32,0},{64,32},{96,64},{128,96},{160,128},{192,160},{224,192},{256... | collective-permute-start | bytes 196616 | tf_op jit(solution)/shard_map/ppermute | solution.py:356

commit v4 on v3

--- a/solution.py
+++ b/solution.py
@@ -48,19 +48,20 @@
     return lax.all_to_all(blocks, ("section", "tensor"), 0, 0, axis_index_groups=groups)
 
 
-def exchange_heads(blocks):
-    return lax.all_to_all(blocks, "tensor", 0, 0, axis_index_groups=tensor_rows(0, FIRST))
-
-
-def call(kernel, outs, *operands, vmem=32, flops=0):
+def exchange_row(blocks, axis):
+    return lax.all_to_all(blocks, "tensor", 0, 0, axis_index_groups=tensor_rows(1 - axis, FIRST))
+
+
+def call(kernel, outs, *operands, vmem=32, flops=0, scratch=(), in_place=False):
     nbytes = sum(int(np.prod(a.shape)) * a.dtype.itemsize for a in (*operands, *outs))
-    specs = [
-        pl.BlockSpec(memory_space=pltpu.SMEM if a.shape == (3,) else pltpu.VMEM) for a in operands
+    spaces = [
+        pltpu.SMEM if a.shape == (3,) else pltpu.HBM if in_place else pltpu.VMEM for a in operands
     ]
     return pl.pallas_call(
         kernel,
         out_shape=outs,
-        in_specs=specs,
+        in_specs=[pl.BlockSpec(memory_space=space) for space in spaces],
+        scratch_shapes=scratch,
         compiler_params=pltpu.CompilerParams(vmem_limit_bytes=vmem * MIB),
         cost_estimate=pl.CostEstimate(flops=flops, bytes_accessed=nbytes, transcendentals=0),
     )(*operands)
@@ -78,19 +79,14 @@
     return pl.ds(pl.multiple_of(t * COLS, COLS), COLS)
 
 
-def pack_kv_weight(pos_ref, w_ref, out_ref):
-    swapped = pos_ref[1] > 1
-    for x in range(SIDE):
-        keys = w_ref[:, x * HD : (x + 1) * HD].T
-        values = w_ref[:, (KVH + x) * HD : (KVH + x + 1) * HD].T
-        for y in range(SIDE):
-            k, j = jnp.where(swapped, y, x), jnp.where(swapped, x, y)
-            out_ref[k, j, 0:16] = keys[16 * y : 16 * y + 16]
-            out_ref[k, j, 16:32] = keys[64 + 16 * y : 80 + 16 * y]
-            out_ref[k, j, 32:64] = values[32 * y : 32 * y + 32]
-
-
-def first_blocks(rows_ref, back_ref, cot_ref, gain_ref, kvw_ref, out_ref):
+def first_blocks(pos_ref, *refs):
+    sources, out_ref, (rows_ref, cot_ref, gain_ref, kvw_ref), sems = refs[:4], refs[4], refs[5:9], refs[9]
+    held = (rows_ref, cot_ref, gain_ref, kvw_ref)
+    copies = [pltpu.make_async_copy(a, b, sems.at[n]) for n, (a, b) in enumerate(zip(sources, held))]
+    for copy in copies:
+        copy.start()
+    for copy in copies[:3]:
+        copy.wait()
     gain = gain_ref[...]
     row = lax.broadcasted_iota(jnp.int32, (16, COLS), 0)
     high = gain.astype(jnp.bfloat16).astype(jnp.float32)
@@ -99,44 +95,74 @@
     gains = jnp.where(row == 0, high, jnp.where(row == 1, middle, jnp.where(row == 2, low, 0.0)))
     for j in range(SIDE):
         out_ref[j, 0:TOK] = rows_ref[...]
-        out_ref[j, TOK : 2 * TOK] = back_ref[...]
-        out_ref[j, 2 * TOK : 3 * TOK] = cot_ref[...]
-        out_ref[j, 384:400] = gains.astype(jnp.bfloat16)
-        for k in range(SIDE):
-            out_ref[j, 400 + 64 * k : 464 + 64 * k] = kvw_ref[k, j]
-
-
-def second_blocks(parts_ref, out_ref):
+        out_ref[j, TOK : 2 * TOK] = cot_ref[...]
+        out_ref[j, 256:272] = gains.astype(jnp.bfloat16)
+    copies[3].wait()
+    swapped = pos_ref[1] > 1
+    for x in range(SIDE):
+        keys = kvw_ref[:, x * HD : (x + 1) * HD].T
+        values = kvw_ref[:, (KVH + x) * HD : (KVH + x + 1) * HD].T
+        for y in range(SIDE):
+            k, j = jnp.where(swapped, y, x), jnp.where(swapped, x, y)
+            start = pl.multiple_of(272 + 64 * k, 16)
+            out_ref[j, pl.ds(start, 16)] = keys[16 * y : 16 * y + 16]
+            out_ref[j, pl.ds(start + 16, 16)] = keys[64 + 16 * y : 80 + 16 * y]
+            out_ref[j, pl.ds(start + 32, 32)] = values[32 * y : 32 * y + 32]
+
+
+def second_blocks(parts_ref, back_ref, out_ref):
     row = lax.broadcasted_iota(jnp.int32, (16, COLS), 0)
     gains = jnp.zeros((16, COLS), jnp.float32)
     for j in range(SIDE):
-        part = parts_ref[j, 384:400].astype(jnp.float32)
+        part = parts_ref[j, 256:272].astype(jnp.float32)
         for i in range(3):
             gains = jnp.where(row == 3 * j + i, part[i : i + 1], gains)
     gains = gains.astype(jnp.bfloat16)
     for k in range(SIDE):
         for j in range(SIDE):
-            out_ref[k, j * 384 : (j + 1) * 384] = parts_ref[j, 0:384]
-        out_ref[k, 1536:1552] = gains
-
-
-def norm_and_kv(pos_ref, rows_ref, first_ref, table_ref, normed_ref, kv_ref, raw_ref, factor_ref):
-    total = jnp.zeros((2 * TOK, COLS), jnp.float32)
+            out_ref[k, j * 256 : (j + 1) * 256] = parts_ref[j, 0:256]
+            out_ref[k, 1040 + 64 * j : 1104 + 64 * j] = parts_ref[j, 272 + 64 * k : 336 + 64 * k]
+        out_ref[k, 1024:1040] = gains
+        out_ref[k, 1296:1424] = back_ref[...]
+
+
+def third_blocks(parts_ref, out_ref):
+    for j in range(SIDE):
+        for k in range(SIDE):
+            out_ref[j, k * TOK : (k + 1) * TOK] = parts_ref[k, 1296:1424]
+
+
+def deliver(out_ref, grad_ref, received_ref, next_ref, before_ref, copy_ref):
+    next_ref[...] = out_ref[...]
+    before_ref[...] = grad_ref[...]
+    copy_ref[...] = received_ref[...]
+
+
+def norm_and_kv(pos_ref, rows_ref, back_ref, table_ref, normed_ref, kv_ref, raw_ref, factor_ref):
+    def blocks(k, j):
+        block = rows_ref[k, j * 256 : j * 256 + TOK].astype(jnp.float32)
+        return block, back_ref[j, k * TOK : (k + 1) * TOK].astype(jnp.float32)
+
+    total = jnp.zeros((TOK, COLS), jnp.float32)
+    back_total = jnp.zeros((TOK, COLS), jnp.float32)
     for k in range(SIDE):
         for j in range(SIDE):
-            block = rows_ref[k, j * 384 : j * 384 + 256].astype(jnp.float32)
+            block, back_block = blocks(k, j)
             total = total + block * block
+            back_total = back_total + back_block * back_block
     factor = lax.rsqrt(jnp.sum(total, axis=1, keepdims=True) / WIDTH + norm_eps)
-    factor_ref[...] = jnp.broadcast_to(factor[TOK:], (TOK, HD))
+    back_factor = lax.rsqrt(jnp.sum(back_total, axis=1, keepdims=True) / WIDTH + norm_eps)
+    factor_ref[...] = jnp.broadcast_to(back_factor, (TOK, HD))
     kv = jnp.zeros((64, 2 * TOK), jnp.float32)
     for k in range(SIDE):
-        gains = rows_ref[k, 1536:1552].astype(jnp.float32)
+        gains = rows_ref[k, 1024:1040].astype(jnp.float32)
         for j in range(SIDE):
             gain = gains[3 * j : 3 * j + 1] + gains[3 * j + 1 : 3 * j + 2] + gains[3 * j + 2 : 3 * j + 3]
-            block = rows_ref[k, j * 384 : j * 384 + 256].astype(jnp.float32)
-            normed = (block * factor * gain).astype(jnp.bfloat16)
-            normed_ref[k * SIDE + j] = normed
-            kv = kv + matmul(first_ref[j, 400 + 64 * k : 464 + 64 * k], normed, NT)
+            block, back_block = blocks(k, j)
+            normed_ref[k * SIDE + j, 0:TOK] = (block * factor * gain).astype(jnp.bfloat16)
+            normed_ref[k * SIDE + j, TOK:] = (back_block * back_factor * gain).astype(jnp.bfloat16)
+            weight = rows_ref[k, 1040 + 64 * j : 1104 + 64 * j]
+            kv = kv + matmul(weight, normed_ref[k * SIDE + j], NT)
     raw_ref[...] = kv[:, TOK:]
     first, second = kv[0:16], kv[16:32]
     start = pl.multiple_of(pos_ref[2] * 16, 16)
@@ -158,7 +184,7 @@
         for j in range(SIDE):
             block = weight_rows(block_index(pos_ref, k, j))
             query = query + matmul(normed_ref[k * SIDE + j], qw_ref[block, :], NN)
-            cot = rows_ref[k, j * 384 + 256 : j * 384 + 384]
+            cot = rows_ref[k, j * 256 + TOK : (j + 1) * 256]
             grad_out = grad_out + matmul(cot, ow_ref[:, block], NT)
     grad_out = grad_out.astype(jnp.bfloat16)
     kv = [kv_ref[y] for y in range(SIDE)]
@@ -228,7 +254,7 @@
 
 
 def project(
-    pos_ref, attended_ref, grad_query_ref, grad_kv_ref, raw_ref, mixed_ref, qw_ref, ow_ref, first_ref, out_ref
+    pos_ref, attended_ref, grad_query_ref, grad_kv_ref, raw_ref, mixed_ref, qw_ref, ow_ref, rows_ref, out_ref
 ):
     attended = attended_ref[...]
     grad_query = grad_query_ref[...]
@@ -238,16 +264,19 @@
     rows = split_rows(mixed)
     for k in range(SIDE):
         for j in range(SIDE):
-            block = weight_rows(block_index(pos_ref, k, j))
+            t = block_index(pos_ref, k, j)
+            block = weight_rows(t)
+            start = pl.multiple_of(lax.rem(t, SIDE) * 256, 256)
             term = matmul(attended, ow_ref[:, block], NN)
-            out_ref[k, j * 256 : j * 256 + TOK] = term.astype(jnp.bfloat16)
+            out_ref[lax.div(t, SIDE), pl.ds(start, TOK)] = term.astype(jnp.bfloat16)
             term = matmul(grad_query, qw_ref[block, :], NT)
-            term = term + matmul(grad_kv, first_ref[j, 400 + 64 * k : 464 + 64 * k], TN)
-            out_ref[k, j * 256 + TOK : j * 256 + 256] = term.astype(jnp.bfloat16)
-        out_ref[k, 1024:1040] = rows
-
-
-def sum_second(parts_ref, out_ref):
+            term = term + matmul(grad_kv, rows_ref[k, 1040 + 64 * j : 1104 + 64 * j], TN)
+            out_ref[lax.div(t, SIDE), pl.ds(start + TOK, TOK)] = term.astype(jnp.bfloat16)
+    for x in range(SIDE):
+        out_ref[x, 1024:1040] = rows
+
+
+def sum_first(parts_ref, out_ref):
     rows = jnp.zeros((16, COLS), jnp.float32)
     for k in range(SIDE):
         rows = rows + parts_ref[k, 1024:1040].astype(jnp.float32)
@@ -303,16 +332,22 @@
     cos, sin = rope_angles()
     wide = np.concatenate([cos, cos], axis=1), np.concatenate([-sin, sin], axis=1)
     table = jnp.asarray(np.concatenate([*wide, cos.T, sin.T], axis=0))
-
-    packed = call(pack_kv_weight, (shape((SIDE, SIDE, 64, COLS)),), pos, kv_w)[0]
-    packed = exchange(packed, SECOND)
     gain_row = norm_gain
+
+    held = [pltpu.VMEM(a.shape, a.dtype) for a in (token_rows, cot_rows, gain_row, kv_w)]
     blocks = call(
-        first_blocks, (shape((SIDE, 656, COLS)),), token_rows, back_rows, cot_rows, gain_row, packed
+        first_blocks,
+        (shape((SIDE, 528, COLS)),),
+        pos, token_rows, cot_rows, gain_row, kv_w,
+        scratch=(*held, pltpu.SemaphoreType.DMA((4,))),
+        in_place=True,
+        vmem=58,
     )[0]
-    first = exchange(blocks, FIRST)
-    blocks = call(second_blocks, (shape((SIDE, 1552, COLS)),), first)[0]
+    blocks = exchange(blocks, FIRST)
+    blocks = call(second_blocks, (shape((SIDE, 1424, COLS)),), blocks, back_rows)[0]
     rows = exchange(blocks, SECOND)
+    blocks = call(third_blocks, (shape((SIDE, 4 * TOK, COLS)),), rows)[0]
+    back = exchange(blocks, FIRST)
 
     normed, kv_own, kv_raw, factor = call(
         norm_and_kv,
@@ -322,10 +357,10 @@
             shape((64, TOK), jnp.float32),
             shape((TOK, HD), jnp.float32),
         ),
-        pos, rows, first, table,
+        pos, rows, back, table,
         flops=2 * 64 * 256 * 4096,
     )
-    kv_all = exchange_heads(kv_own)
+    kv_all = exchange_row(kv_own, 1)
     attended, grad_query, grad_kv, mixed = call(
         attention,
         (
@@ -337,16 +372,16 @@
         pos, rows, normed, kv_all, query_w, out_w, table,
         flops=2 * 384 * 256 * 4096,
     )
-    grad_kv = exchange_heads(grad_kv)
+    grad_kv = exchange_row(grad_kv, 1)
     terms = call(
         project,
         (shape((SIDE, 1040, COLS)),),
-        pos, attended, grad_query, grad_kv, kv_raw, mixed, query_w, out_w, first,
+        pos, attended, grad_query, grad_kv, kv_raw, mixed, query_w, out_w, rows,
         flops=2 * 256 * 256 * 4096,
     )[0]
-    terms = exchange(terms, SECOND)
-    terms = call(sum_second, (shape((SIDE, 272, COLS)),), terms)[0]
-    terms = exchange(terms, FIRST)
+    terms = exchange_row(terms, 0)
+    terms = call(sum_first, (shape((SIDE, 272, COLS)),), terms)[0]
+    terms = exchange_row(terms, 1)
     layer_out, grad_local = call(
         finish,
         (shape((TOK, COLS)), shape((TOK, COLS))),
@@ -354,6 +389,9 @@
     )
     next_input = lax.ppermute(layer_out, "section", [(s, s + 1) for s in range(section_count - 1)])
     input_grad = lax.ppermute(grad_local, "section", [(s + 1, s) for s in range(section_count - 1)])
+    next_input, input_grad, received = call(
+        deliver, (shape((TOK, COLS)),) * 3, next_input, input_grad, received
+    )
     return (next_input[None], received[None], input_grad[None])
 
 

time: 158 us -> 152 us (0.962)
  blocking collectives: 117 us -> 112 us
  local copies, waits for them, and re-layouts: 2.96 us -> 0.03 us
  Pallas kernels: 8.58 us -> 10.7 us
    all_to_all x4 -> x2, blocking collectives: 101 us -> 63.8 us  [exchange(): lax.all_to_all(blocks, ('section', 'tensor'), 0, 0, axis_index_groups=gro...]
    all_to_all x2 -> x4, blocking collectives: 15.2 us -> 48.2 us  [exchange_row(): lax.all_to_all(blocks, 'tensor', 0, 0, axis_index_groups=tensor_rows(1 -...]
    unnamed x19 -> x16, local copies, waits for them, and re-layouts: 2.96 us -> 0.03 us
    pallas_call x8 -> x9, Pallas kernels: 8.58 us -> 10.7 us  [call(): pl.pallas_call(kernel, out_shape=outs, in_specs=[pl.BlockSpec(memory_spac...]
where the time goes in v4:
time: 152 us
  blocking collectives  112 us (74%)
  starting transfers between devices  21.3 us (14%)
  Pallas kernels  10.7 us (7%)
  waiting for transfers between devices  5.79 us (4%)
    all_to_all x2, blocking collectives, exchange(): lax.all_to_all(blocks, ('section', 'tensor'), 0, 0, axis_index_groups=gro...  63.8 us
    all_to_all x4, blocking collectives, exchange_row(): lax.all_to_all(blocks, 'tensor', 0, 0, axis_index_groups=tensor_rows(1 -...  48.2 us
    ppermute x1, starting transfers between devices, per_device(): received = lax.ppermute(sending, 'section', mirrored)  12.1 us
    pallas_call x9, Pallas kernels, call(): pl.pallas_call(kernel, out_shape=outs, in_specs=[pl.BlockSpec(memory_spac...  10.7 us
    all_to_all x1, starting transfers between devices, exchange(): lax.all_to_all(blocks, ('section', 'tensor'), 0, 0, axis_index_groups=gro...  4.85 us
    ppermute x1, waiting for transfers between devices, per_device(): lax.ppermute(grad_local, 'section', [(s + 1, s) for s in range(section_co...  3.16 us
  transfers between devices with their start and end apart: 4, of which 2 were waited for; matrix products, arithmetic and copies ran while one was open for 0% of the time, Pallas kernels for 0%

profile of v4, /device:TPU:1, one launch (start us, length us, event | category | flops | bytes accessed | tf_op | source)
XLA Modules:
  0.0 151.8 jit_solution(15057438393709344211)
XLA Ops:
  0.6 0.0 copy-start.2
  0.7 0.6 pad_add_fusion.pos_ref
  1.3 3.0 %shard_map.112 = bf16[4,528,256]{2,1,0:T(8,128)(2,1)} custom-call(s32[3]{0:T(128)} %pad_add_fusion.pos_ref, bf16[128,256]{1,0:T(8,128)(2,1)} %bitcast.23, bf16[128,256]{1,0:T(8,128)(2,1)} %bitcast.25, f32[1,256]{1,0:T(1,128)} %gain_ref.1, bf16[256,1024]{1,0:T(8,128)(2,1)} %bitcast.27), custom_call_target="tpu_custom_call" | custom-call | bytes 1737740 | tf_op jit(solution)/shard_map/pallas_call | solution.py:60
  4.3 4.9 %all-to-all-start = ((bf16[4,528,256]{2,1,0:T(8,128)(2,1)}), bf16[4,528,256]{2,1,0:T(8,128)(2,1)S(1)}, u32[]{:S(2)}, u32[]{:S(2)}) async-start(bf16[4,528,256]{2,1,0:T(8,128)(2,1)} %shard_map.112), calls=%async_computation | async-start | bytes 2162688 | tf_op jit(solution)/shard_map/all_to_all | solution.py:48
  9.8 12.1 %collective-permute-start = (bf16[128,256]{1,0:T(8,128)(2,1)S(1)}, bf16[128,256]{1,0:T(8,128)(2,1)S(1)}, u32[]{:S(2)}, u32[]{:S(2)}) collective-permute-start(bf16[128,256]{1,0:T(8,128)(2,1)S(1)} %bitcast_select_fusion), channel_id=1, source_target_pairs={{0,480},{32,448},{64,416},{96,384},{128,352},{160,320},{192,288},{... | collective-permute-start | bytes 196616 | tf_op jit(solution)/shard_map/ppermute | solution.py:326
  21.9 2.6 %collective-permute-done.received_ref = bf16[128,256]{1,0:T(8,128)(2,1)S(1)} collective-permute-done((bf16[128,256]{1,0:T(8,128)(2,1)S(1)}, bf16[128,256]{1,0:T(8,128)(2,1)S(1)}, u32[]{:S(2)}, u32[]{:S(2)}) %collective-permute-start) | collective-permute-done | bytes 65568 | tf_op jit(solution)/shard_map/ppermute | solution.py:326
  24.6 0.0 all-to-all-done.parts_ref
  24.6 0.2 shard_map.113
  24.8 48.0 %all_to_all.35.parts_ref.rows_ref = bf16[4,1424,256]{2,1,0:T(8,128)(2,1)S(1)} all-to-all(bf16[4,1424,256]{2,1,0:T(8,128)(2,1)S(1)} %shard_map.113), channel_id=1, replica_groups={{0,8,16,24},{2,10,18,26},{4,12,20,28},{6,14,22,30},{32,34,36,38},{40,42..., dimensions={0} | all-to-all | bytes 5832704 | tf_op jit(solution)/shard_map/all_to_all | solution.py:48
  72.8 0.1 shard_map.114
  72.9 15.8 %all_to_all.36.back_ref = bf16[4,512,256]{2,1,0:T(8,128)(2,1)S(1)} all-to-all(bf16[4,512,256]{2,1,0:T(8,128)(2,1)S(1)} %shard_map.114), channel_id=1, replica_groups={{0,2,4,6},{8,10,12,14},{16,18,20,22},{24,26,28,30},{32,40,48,56},{34,42..., dimensions={0} | all-to-all | bytes 2097152 | tf_op jit(solution)/shard_map/all_to_all | solution.py:48
  88.7 1.7 %shard_map.115 = (bf16[16,256,256]{2,1,0:T(8,128)(2,1)S(1)}, bf16[4,64,256]{2,1,0:T(8,128)(2,1)S(1)}, f32[64,128]{1,0:T(8,128)S(1)}, f32[128,128]{1,0:T(8,128)S(1)}) custom-call(s32[3]{0:T(128)S(1)} %copy-done.5, bf16[4,1424,256]{2,1,0:T(8,128)(2,1)S(1)} %all_to_all.35.parts_ref.rows_ref, bf16[4,512,256]{2,1,0:T(8,128)(2,1)S(1)} %all_to_all.36.back_ref, ...), custom_call_target="tpu_custom_call" | custom-call | flops 134217728 | bytes 6488076 | tf_op jit(solution)/shard_map/pallas_call | solution.py:60
  90.4 7.6 %all_to_all.37.kv_ref = bf16[4,64,256]{2,1,0:T(8,128)(2,1)S(1)} all-to-all(bf16[4,64,256]{2,1,0:T(8,128)(2,1)S(1)} %get-tuple-element.17), channel_id=1, replica_groups={{0,2,4,6},{8,10,12,14},{16,18,20,22},{24,26,28,30},{1,3,5,7},{9,11,13,1..., dimensions={0} | all-to-all | bytes 262144 | tf_op jit(solution)/shard_map/all_to_all | solution.py:52
  98.0 2.6 %shard_map.116 = (bf16[128,256]{1,0:T(8,128)(2,1)S(1)}, bf16[128,256]{1,0:T(8,128)(2,1)S(1)}, f32[4,64,128]{2,1,0:T(8,128)S(1)}, f32[8,128]{1,0:T(8,128)S(1)}) custom-call(s32[3]{0:T(128)S(1)} %copy-done.5, bf16[4,1424,256]{2,1,0:T(8,128)(2,1)S(1)} %all_to_all.35.parts_ref.rows_ref, bf16[16,256,256]{2,1,0:T(8,128)(2,1)S(1)} %get-tuple-element.16.normed_ref, ...), custom_call_target="tpu_custom_call" | custom-call | flops 805306368 | bytes 9801740 | tf_op jit(solution)/shard_map/pallas_call | solution.py:60
  100.6 7.2 %all_to_all.38.grad_kv_ref = f32[4,64,128]{2,1,0:T(8,128)S(1)} all-to-all(f32[4,64,128]{2,1,0:T(8,128)S(1)} %get-tuple-element.20), channel_id=1, replica_groups={{0,2,4,6},{8,10,12,14},{16,18,20,22},{24,26,28,30},{1,3,5,7},{9,11,13,1..., dimensions={0} | all-to-all | bytes 262144 | tf_op jit(solution)/shard_map/all_to_all | solution.py:52
  107.8 2.0 %shard_map.117 = bf16[4,1040,256]{2,1,0:T(8,128)(2,1)S(1)} custom-call(s32[3]{0:T(128)S(1)} %copy-done.5, bf16[128,256]{1,0:T(8,128)(2,1)S(1)} %get-tuple-element.18.attended_ref, bf16[128,256]{1,0:T(8,128)(2,1)S(1)} %get-tuple-element.19.grad_query_ref, f32[4,64,128]{2,1,0:T(8,128)S(1)} %all_to_all.38.grad_kv_ref, f32[64,128]{1,0:T(8,128)S(1)} %get-tuple-element.21.raw_ref, ...), custom_call_target="tpu_custom_call" | custom-call | flops 536870912 | bytes 9539596 | tf_op jit(solution)/shard_map/pallas_call | solution.py:60
  109.8 21.3 %all_to_all.39.parts_ref = bf16[4,1040,256]{2,1,0:T(8,128)(2,1)S(1)} all-to-all(bf16[4,1040,256]{2,1,0:T(8,128)(2,1)S(1)} %shard_map.117), channel_id=1, replica_groups={{0,8,16,24},{2,10,18,26},{4,12,20,28},{6,14,22,30},{1,9,17,25},{3,11,19..., dimensions={0} | all-to-all | bytes 4259840 | tf_op jit(solution)/shard_map/all_to_all | solution.py:52
  131.1 0.3 shard_map.118
  131.3 12.1 %all_to_all.40.parts_ref = bf16[4,272,256]{2,1,0:T(8,128)(2,1)S(1)} all-to-all(bf16[4,272,256]{2,1,0:T(8,128)(2,1)S(1)} %shard_map.118), channel_id=1, replica_groups={{0,2,4,6},{8,10,12,14},{16,18,20,22},{24,26,28,30},{1,3,5,7},{9,11,13,1..., dimensions={0} | all-to-all | bytes 1114112 | tf_op jit(solution)/shard_map/all_to_all | solution.py:52
  143.4 0.2 shard_map.119
  143.6 1.9 %collective-permute-start.1 = (bf16[128,256]{1,0:T(8,128)(2,1)S(1)}, bf16[128,256]{1,0:T(8,128)(2,1)S(1)}, u32[]{:S(2)}, u32[]{:S(2)}) collective-permute-start(bf16[128,256]{1,0:T(8,128)(2,1)S(1)} %get-tuple-element.24), channel_id=1, source_target_pairs={{0,32},{32,64},{64,96},{96,128},{128,160},{160,192},{192,224},{224... | collective-permute-start | bytes 196616 | tf_op jit(solution)/shard_map/ppermute | solution.py:390
  145.6 2.4 %collective-permute-start.2 = (bf16[128,256]{1,0:T(8,128)(2,1)S(1)}, bf16[128,256]{1,0:T(8,128)(2,1)S(1)}, u32[]{:S(2)}, u32[]{:S(2)}) collective-permute-start(bf16[128,256]{1,0:T(8,128)(2,1)S(1)} %get-tuple-element.25), channel_id=1, source_target_pairs={{32,0},{64,32},{96,64},{128,96},{160,128},{192,160},{224,192},{256... | collective-permute-start | bytes 196616 | tf_op jit(solution)/shard_map/ppermute | solution.py:391
  148.0 3.2 %collective-permute-done.2.grad_ref = bf16[128,256]{1,0:T(8,128)(2,1)S(1)} collective-permute-done((bf16[128,256]{1,0:T(8,128)(2,1)S(1)}, bf16[128,256]{1,0:T(8,128)(2,1)S(1)}, u32[]{:S(2)}, u32[]{:S(2)}) %collective-permute-start.2) | collective-permute-done | bytes 65568 | tf_op jit(solution)/shard_map/ppermute | solution.py:391
  151.2 0.7 shard_map.120
  (18 shorter events, 0.1 us)
Async XLA Ops:
  0.6 9.2 %copy-start.2 = (bf16[1,128,256]{2,1,0:T(8,128)(2,1)S(1)}, bf16[1,128,256]{2,1,0:T(8,128)(2,1)}, u32[]{:S(2)}) copy-start(bf16[1,128,256]{2,1,0:T(8,128)(2,1)} %param.9) | copy-start | bytes 196612
  0.6 9.2 %copy-start.7 = (bf16[1,2,128,256]{3,2,1,0:T(8,128)(2,1)S(1)}, bf16[1,2,128,256]{3,2,1,0:T(8,128)(2,1)}, u32[]{:S(2)}) copy-start(bf16[1,2,128,256]{3,2,1,0:T(8,128)(2,1)} %param.10) | copy-start | bytes 393220
  4.3 20.3 %all-to-all-start = ((bf16[4,528,256]{2,1,0:T(8,128)(2,1)}), bf16[4,528,256]{2,1,0:T(8,128)(2,1)S(1)}, u32[]{:S(2)}, u32[]{:S(2)}) async-start(bf16[4,528,256]{2,1,0:T(8,128)(2,1)} %shard_map.112), calls=%async_computation | async-start | bytes 2162688 | tf_op jit(solution)/shard_map/all_to_all | solution.py:48
  9.8 14.7 %collective-permute-start = (bf16[128,256]{1,0:T(8,128)(2,1)S(1)}, bf16[128,256]{1,0:T(8,128)(2,1)S(1)}, u32[]{:S(2)}, u32[]{:S(2)}) collective-permute-start(bf16[128,256]{1,0:T(8,128)(2,1)S(1)} %bitcast_select_fusion), channel_id=1, source_target_pairs={{0,480},{32,448},{64,416},{96,384},{128,352},{160,320},{192,288},{... | collective-permute-start | bytes 196616 | tf_op jit(solution)/shard_map/ppermute | solution.py:326
  72.8 15.9 %copy-start.3 = (f32[384,128]{1,0:T(8,128)S(1)}, f32[384,128]{1,0:T(8,128)}, u32[]{:S(2)}) copy-start(f32[384,128]{1,0:T(8,128)} %constant.44.clone.table_ref) | copy-start | bytes 589828
  72.8 15.9 %copy-start.5 = (s32[3]{0:T(128)S(1)}, s32[3]{0:T(128)}, u32[]{:S(2)}) copy-start(s32[3]{0:T(128)} %pad_add_fusion.pos_ref) | copy-start | bytes 40
  88.7 9.3 %copy-start = (bf16[1,4096,256]{2,1,0:T(8,128)(2,1)S(1)}, bf16[1,4096,256]{2,1,0:T(8,128)(2,1)}, u32[]{:S(2)}) copy-start(bf16[1,4096,256]{2,1,0:T(8,128)(2,1)} %param.14) | copy-start | bytes 6291460
  88.7 9.3 %copy-start.1 = (bf16[1,256,4096]{2,1,0:T(8,128)(2,1)S(1)}, bf16[1,256,4096]{2,1,0:T(8,128)(2,1)}, u32[]{:S(2)}) copy-start(bf16[1,256,4096]{2,1,0:T(8,128)(2,1)} %param.16) | copy-start | bytes 6291460
  131.1 12.4 %copy-start.4 = (bf16[1,128,256]{2,1,0:T(8,128)(2,1)S(1)}, bf16[1,128,256]{2,1,0:T(8,128)(2,1)}, u32[]{:S(2)}) copy-start(bf16[1,128,256]{2,1,0:T(8,128)(2,1)} %param.12) | copy-start | bytes 196612
  131.1 12.4 %copy-start.6 = (f32[1,256]{1,0:T(1,128)S(1)}, f32[1,256]{1,0:T(1,128)}, u32[]{:S(2)}) copy-start(f32[1,256]{1,0:T(1,128)} %gain_ref.1) | copy-start | bytes 3076
  143.6 4.3 %collective-permute-start.1 = (bf16[128,256]{1,0:T(8,128)(2,1)S(1)}, bf16[128,256]{1,0:T(8,128)(2,1)S(1)}, u32[]{:S(2)}, u32[]{:S(2)}) collective-permute-start(bf16[128,256]{1,0:T(8,128)(2,1)S(1)} %get-tuple-element.24), channel_id=1, source_target_pairs={{0,32},{32,64},{64,96},{96,128},{128,160},{160,192},{192,224},{224... | collective-permute-start | bytes 196616 | tf_op jit(solution)/shard_map/ppermute | solution.py:390
  145.6 5.6 %collective-permute-start.2 = (bf16[128,256]{1,0:T(8,128)(2,1)S(1)}, bf16[128,256]{1,0:T(8,128)(2,1)S(1)}, u32[]{:S(2)}, u32[]{:S(2)}) collective-permute-start(bf16[128,256]{1,0:T(8,128)(2,1)S(1)} %get-tuple-element.25), channel_id=1, source_target_pairs={{32,0},{64,32},{96,64},{128,96},{160,128},{192,160},{224,192},{256... | collective-permute-start | bytes 196616 | tf_op jit(solution)/shard_map/ppermute | solution.py:391

commit v5 on v4

--- a/solution.py
+++ b/solution.py
@@ -55,7 +55,7 @@
 def call(kernel, outs, *operands, vmem=32, flops=0, scratch=(), in_place=False):
     nbytes = sum(int(np.prod(a.shape)) * a.dtype.itemsize for a in (*operands, *outs))
     spaces = [
-        pltpu.SMEM if a.shape == (3,) else pltpu.HBM if in_place else pltpu.VMEM for a in operands
+        pltpu.HBM if in_place else pltpu.VMEM for _ in operands
     ]
     return pl.pallas_call(
         kernel,
@@ -71,21 +71,28 @@
     return jax.ShapeDtypeStruct(dims, dtype)
 
 
-def block_index(pos_ref, k, j):
-    return k * pos_ref[0] + j * pos_ref[1]
+def position():
+    section, tensor = lax.axis_index("section"), lax.axis_index("tensor")
+    odd = lax.rem(section, 2)
+    return SIDE - 3 * odd, 1 + 3 * odd, lax.rem(tensor, SIDE), section < lax.axis_size("section") // 2
+
+
+def block_index(place, k, j):
+    return k * place[0] + j * place[1]
 
 
 def weight_rows(t):
     return pl.ds(pl.multiple_of(t * COLS, COLS), COLS)
 
 
-def first_blocks(pos_ref, *refs):
-    sources, out_ref, (rows_ref, cot_ref, gain_ref, kvw_ref), sems = refs[:4], refs[4], refs[5:9], refs[9]
-    held = (rows_ref, cot_ref, gain_ref, kvw_ref)
+def first_blocks(*refs):
+    place = position()
+    sources, out_ref, (rows_ref, gain_ref, kvw_ref), sems = refs[:3], refs[3], refs[4:7], refs[7]
+    held = (rows_ref, gain_ref, kvw_ref)
     copies = [pltpu.make_async_copy(a, b, sems.at[n]) for n, (a, b) in enumerate(zip(sources, held))]
     for copy in copies:
         copy.start()
-    for copy in copies[:3]:
+    for copy in copies[:2]:
         copy.wait()
     gain = gain_ref[...]
     row = lax.broadcasted_iota(jnp.int32, (16, COLS), 0)
@@ -95,53 +102,73 @@
     gains = jnp.where(row == 0, high, jnp.where(row == 1, middle, jnp.where(row == 2, low, 0.0)))
     for j in range(SIDE):
         out_ref[j, 0:TOK] = rows_ref[...]
-        out_ref[j, TOK : 2 * TOK] = cot_ref[...]
-        out_ref[j, 256:272] = gains.astype(jnp.bfloat16)
-    copies[3].wait()
-    swapped = pos_ref[1] > 1
+        out_ref[j, 128:144] = gains.astype(jnp.bfloat16)
+    copies[2].wait()
+    swapped = place[1] > 1
     for x in range(SIDE):
         keys = kvw_ref[:, x * HD : (x + 1) * HD].T
         values = kvw_ref[:, (KVH + x) * HD : (KVH + x + 1) * HD].T
         for y in range(SIDE):
             k, j = jnp.where(swapped, y, x), jnp.where(swapped, x, y)
-            start = pl.multiple_of(272 + 64 * k, 16)
+            start = pl.multiple_of(144 + 64 * k, 16)
             out_ref[j, pl.ds(start, 16)] = keys[16 * y : 16 * y + 16]
             out_ref[j, pl.ds(start + 16, 16)] = keys[64 + 16 * y : 80 + 16 * y]
             out_ref[j, pl.ds(start + 32, 32)] = values[32 * y : 32 * y + 32]
 
 
-def second_blocks(parts_ref, back_ref, out_ref):
+def pick_back(reloaded_ref, rows_ref, back_ref):
+    place = position()
+    @pl.when(place[3])
+    def _():
+        back_ref[...] = reloaded_ref[...]
+
+    @pl.when(jnp.logical_not(place[3]))
+    def _():
+        back_ref[...] = rows_ref[...]
+
+
+def second_blocks(parts_ref, back_ref, cot_ref, out_ref):
     row = lax.broadcasted_iota(jnp.int32, (16, COLS), 0)
     gains = jnp.zeros((16, COLS), jnp.float32)
     for j in range(SIDE):
-        part = parts_ref[j, 256:272].astype(jnp.float32)
+        part = parts_ref[j, 128:144].astype(jnp.float32)
         for i in range(3):
             gains = jnp.where(row == 3 * j + i, part[i : i + 1], gains)
     gains = gains.astype(jnp.bfloat16)
     for k in range(SIDE):
         for j in range(SIDE):
-            out_ref[k, j * 256 : (j + 1) * 256] = parts_ref[j, 0:256]
-            out_ref[k, 1040 + 64 * j : 1104 + 64 * j] = parts_ref[j, 272 + 64 * k : 336 + 64 * k]
-        out_ref[k, 1024:1040] = gains
-        out_ref[k, 1296:1424] = back_ref[...]
+            out_ref[k, j * TOK : (j + 1) * TOK] = parts_ref[j, 0:TOK]
+            out_ref[k, 528 + 64 * j : 592 + 64 * j] = parts_ref[j, 144 + 64 * k : 208 + 64 * k]
+        out_ref[k, 512:528] = gains
+        out_ref[k, 784:912] = back_ref[...]
+        out_ref[k, 912:1040] = cot_ref[...]
 
 
 def third_blocks(parts_ref, out_ref):
     for j in range(SIDE):
         for k in range(SIDE):
-            out_ref[j, k * TOK : (k + 1) * TOK] = parts_ref[k, 1296:1424]
-
-
-def deliver(out_ref, grad_ref, received_ref, next_ref, before_ref, copy_ref):
+            out_ref[j, k * 256 : (k + 1) * 256] = parts_ref[k, 784:1040]
+
+
+def deliver(out_ref, grad_ref, reloaded_ref, evicted_ref, next_ref, before_ref, copy_ref):
+    place = position()
     next_ref[...] = out_ref[...]
     before_ref[...] = grad_ref[...]
-    copy_ref[...] = received_ref[...]
-
-
-def norm_and_kv(pos_ref, rows_ref, back_ref, table_ref, normed_ref, kv_ref, raw_ref, factor_ref):
+
+    @pl.when(place[3])
+    def _():
+        copy_ref[...] = reloaded_ref[...]
+
+    @pl.when(jnp.logical_not(place[3]))
+    def _():
+        copy_ref[...] = evicted_ref[...]
+
+
+def norm_and_kv(rows_ref, back_ref, table_ref, normed_ref, kv_ref, raw_ref, factor_ref):
+    place = position()
     def blocks(k, j):
-        block = rows_ref[k, j * 256 : j * 256 + TOK].astype(jnp.float32)
-        return block, back_ref[j, k * TOK : (k + 1) * TOK].astype(jnp.float32)
+        block = rows_ref[k, j * TOK : (j + 1) * TOK].astype(jnp.float32)
+        return block, back_ref[j, k * 256 : k * 256 + TOK].astype(jnp.float32)
 
     total = jnp.zeros((TOK, COLS), jnp.float32)
     back_total = jnp.zeros((TOK, COLS), jnp.float32)
@@ -155,17 +182,17 @@
     factor_ref[...] = jnp.broadcast_to(back_factor, (TOK, HD))
     kv = jnp.zeros((64, 2 * TOK), jnp.float32)
     for k in range(SIDE):
-        gains = rows_ref[k, 1024:1040].astype(jnp.float32)
+        gains = rows_ref[k, 512:528].astype(jnp.float32)
         for j in range(SIDE):
             gain = gains[3 * j : 3 * j + 1] + gains[3 * j + 1 : 3 * j + 2] + gains[3 * j + 2 : 3 * j + 3]
             block, back_block = blocks(k, j)
             normed_ref[k * SIDE + j, 0:TOK] = (block * factor * gain).astype(jnp.bfloat16)
             normed_ref[k * SIDE + j, TOK:] = (back_block * back_factor * gain).astype(jnp.bfloat16)
-            weight = rows_ref[k, 1040 + 64 * j : 1104 + 64 * j]
+            weight = rows_ref[k, 528 + 64 * j : 592 + 64 * j]
             kv = kv + matmul(weight, normed_ref[k * SIDE + j], NT)
     raw_ref[...] = kv[:, TOK:]
     first, second = kv[0:16], kv[16:32]
-    start = pl.multiple_of(pos_ref[2] * 16, 16)
+    start = pl.multiple_of(place[2] * 16, 16)
     cos, sin = table_ref[pl.ds(256 + start, 16)], table_ref[pl.ds(320 + start, 16)]
     cos, sin = jnp.concatenate([cos, cos], axis=1), jnp.concatenate([sin, sin], axis=1)
     out = jnp.concatenate([first * cos - second * sin, second * cos + first * sin, kv[32:64]], axis=0)
@@ -175,16 +202,17 @@
 
 
 def attention(
-    pos_ref, rows_ref, normed_ref, kv_ref, qw_ref, ow_ref, table_ref,
+    back_ref, normed_ref, kv_ref, qw_ref, ow_ref, table_ref,
     attended_ref, grad_query_ref, grad_kv_ref, mixed_ref,
 ):
+    place = position()
     query = jnp.zeros((2 * TOK, COLS), jnp.float32)
     grad_out = jnp.zeros((TOK, COLS), jnp.float32)
     for k in range(SIDE):
         for j in range(SIDE):
-            block = weight_rows(block_index(pos_ref, k, j))
+            block = weight_rows(block_index(place, k, j))
             query = query + matmul(normed_ref[k * SIDE + j], qw_ref[block, :], NN)
-            cot = rows_ref[k, j * 256 + TOK : (j + 1) * 256]
+            cot = back_ref[j, k * 256 + TOK : (k + 1) * 256]
             grad_out = grad_out + matmul(cot, ow_ref[:, block], NT)
     grad_out = grad_out.astype(jnp.bfloat16)
     kv = [kv_ref[y] for y in range(SIDE)]
@@ -254,8 +282,9 @@
 
 
 def project(
-    pos_ref, attended_ref, grad_query_ref, grad_kv_ref, raw_ref, mixed_ref, qw_ref, ow_ref, rows_ref, out_ref
+    attended_ref, grad_query_ref, grad_kv_ref, raw_ref, mixed_ref, qw_ref, ow_ref, rows_ref, out_ref
 ):
+    place = position()
     attended = attended_ref[...]
     grad_query = grad_query_ref[...]
     grad_kv = grad_kv_ref[0] + grad_kv_ref[1] + grad_kv_ref[2] + grad_kv_ref[3]
@@ -264,13 +293,13 @@
     rows = split_rows(mixed)
     for k in range(SIDE):
         for j in range(SIDE):
-            t = block_index(pos_ref, k, j)
+            t = block_index(place, k, j)
             block = weight_rows(t)
             start = pl.multiple_of(lax.rem(t, SIDE) * 256, 256)
             term = matmul(attended, ow_ref[:, block], NN)
             out_ref[lax.div(t, SIDE), pl.ds(start, TOK)] = term.astype(jnp.bfloat16)
             term = matmul(grad_query, qw_ref[block, :], NT)
-            term = term + matmul(grad_kv, rows_ref[k, 1040 + 64 * j : 1104 + 64 * j], TN)
+            term = term + matmul(grad_kv, rows_ref[k, 528 + 64 * j : 592 + 64 * j], TN)
             out_ref[lax.div(t, SIDE), pl.ds(start + TOK, TOK)] = term.astype(jnp.bfloat16)
     for x in range(SIDE):
         out_ref[x, 1024:1040] = rows
@@ -321,34 +350,32 @@
     is_early = section_pos < section_count // 2
 
     picked = lax.dynamic_index_in_dim(stash_pool[0], reload_slot[0], 0, keepdims=False)
-    sending = jnp.where(is_early, token_rows, picked)
-    mirrored = [(s, section_count - 1 - s) for s in range(section_count)]
-    received = lax.ppermute(sending, "section", mirrored)
-    back_rows = jnp.where(is_early, received, token_rows)
-
-    tensor_pos = lax.axis_index("tensor").astype(jnp.int32)
-    odd = (section_pos % 2).astype(jnp.int32)
-    pos = jnp.stack([SIDE - 3 * odd, 1 + 3 * odd, tensor_pos % SIDE])
+    half = section_count // 2
+    reloaded = lax.ppermute(picked, "section", [(section_count - 1 - s, s) for s in range(half)])
     cos, sin = rope_angles()
     wide = np.concatenate([cos, cos], axis=1), np.concatenate([-sin, sin], axis=1)
     table = jnp.asarray(np.concatenate([*wide, cos.T, sin.T], axis=0))
     gain_row = norm_gain
 
-    held = [pltpu.VMEM(a.shape, a.dtype) for a in (token_rows, cot_rows, gain_row, kv_w)]
+    back_rows = call(
+        pick_back, (shape((TOK, COLS)),), reloaded, token_rows, flops=1000000000000
+    )[0]
+    held = [pltpu.VMEM(a.shape, a.dtype) for a in (token_rows, gain_row, kv_w)]
     blocks = call(
         first_blocks,
-        (shape((SIDE, 528, COLS)),),
-        pos, token_rows, cot_rows, gain_row, kv_w,
-        scratch=(*held, pltpu.SemaphoreType.DMA((4,))),
+        (shape((SIDE, 400, COLS)),),
+        token_rows, gain_row, kv_w,
+        scratch=(*held, pltpu.SemaphoreType.DMA((3,))),
         in_place=True,
         vmem=58,
     )[0]
     blocks = exchange(blocks, FIRST)
-    blocks = call(second_blocks, (shape((SIDE, 1424, COLS)),), blocks, back_rows)[0]
+    blocks = call(second_blocks, (shape((SIDE, 1040, COLS)),), blocks, back_rows, cot_rows)[0]
     rows = exchange(blocks, SECOND)
-    blocks = call(third_blocks, (shape((SIDE, 4 * TOK, COLS)),), rows)[0]
+    blocks = call(third_blocks, (shape((SIDE, 8 * TOK, COLS)),), rows)[0]
     back = exchange(blocks, FIRST)
 
+    evicted = lax.ppermute(token_rows, "section", [(s, section_count - 1 - s) for s in range(half)])
     normed, kv_own, kv_raw, factor = call(
         norm_and_kv,
         (
@@ -357,7 +384,7 @@
             shape((64, TOK), jnp.float32),
             shape((TOK, HD), jnp.float32),
         ),
-        pos, rows, back, table,
+        rows, back, table,
         flops=2 * 64 * 256 * 4096,
     )
     kv_all = exchange_row(kv_own, 1)
@@ -369,14 +396,14 @@
             shape((SIDE, 64, TOK), jnp.float32),
             shape((8, TOK), jnp.float32),
         ),
-        pos, rows, normed, kv_all, query_w, out_w, table,
+        back, normed, kv_all, query_w, out_w, table,
         flops=2 * 384 * 256 * 4096,
     )
     grad_kv = exchange_row(grad_kv, 1)
     terms = call(
         project,
         (shape((SIDE, 1040, COLS)),),
-        pos, attended, grad_query, grad_kv, kv_raw, mixed, query_w, out_w, rows,
+        attended, grad_query, grad_kv, kv_raw, mixed, query_w, out_w, rows,
         flops=2 * 256 * 256 * 4096,
     )[0]
     terms = exchange_row(terms, 0)
@@ -390,7 +417,7 @@
     next_input = lax.ppermute(layer_out, "section", [(s, s + 1) for s in range(section_count - 1)])
     input_grad = lax.ppermute(grad_local, "section", [(s + 1, s) for s in range(section_count - 1)])
     next_input, input_grad, received = call(
-        deliver, (shape((TOK, COLS)),) * 3, next_input, input_grad, received
+        deliver, (shape((TOK, COLS)),) * 3, next_input, input_grad, reloaded, evicted
     )
     return (next_input[None], received[None], input_grad[None])
 

time: 152 us -> 148 us (0.974)
  blocking collectives: 112 us -> 85.2 us
  starting transfers between devices: 21.3 us -> 40.7 us
  waiting for transfers between devices: 5.79 us -> 9.47 us
    all_to_all x2, blocking collectives: 63.8 us -> 50.1 us  [exchange(): lax.all_to_all(blocks, ('section', 'tensor'), 0, 0, axis_index_groups=gro...]
    all_to_all x4 -> x3, blocking collectives: 48.2 us -> 35.1 us  [exchange_row(): lax.all_to_all(blocks, 'tensor', 0, 0, axis_index_groups=tensor_rows(1 -...]
    ppermute x1 -> x2, starting transfers between devices: 12.1 us -> 21 us  [the longest x1 19.7 us: per_device(): lax.ppermute(token_rows, 'section', [(s, section_count - 1 - s) for s in...]
    ppermute x1, starting transfers between devices: 2.41 us -> 7.53 us  [per_device(): lax.ppermute(grad_local, 'section', [(s + 1, s) for s in range(section_co...]
    ppermute x1 -> x2, waiting for transfers between devices: 2.63 us -> 6.36 us  [the longest x1 6.36 us: per_device(): lax.ppermute(picked, 'section', [(section_count - 1 - s, s) for s in rang...]
    all_to_all x0 -> x1, starting transfers between devices: none -> 3.47 us  [exchange_row(): lax.all_to_all(blocks, 'tensor', 0, 0, axis_index_groups=tensor_rows(1 -...]
    ppermute x1, waiting for transfers between devices: 3.16 us -> 0.86 us  [per_device(): lax.ppermute(grad_local, 'section', [(s + 1, s) for s in range(section_co...]
    all_to_all x1, waiting for transfers between devices: 0.01 us -> 2.24 us  [exchange(): lax.all_to_all(blocks, ('section', 'tensor'), 0, 0, axis_index_groups=gro...]
  transfers between devices with their start and end apart: 4 -> 6, of which waited for: 2 -> 3; matrix products, arithmetic and copies ran while one was open for 0% -> 0% of each run, Pallas kernels for 0% -> 2%
where the time goes in v5:
time: 148 us; the launch traced here: 147 us
  blocking collectives  85.2 us (58%)
  starting transfers between devices  40.7 us (28%)
  Pallas kernels  10.2 us (7%)
  waiting for transfers between devices  9.47 us (6%)
    all_to_all x2, blocking collectives, exchange(): lax.all_to_all(blocks, ('section', 'tensor'), 0, 0, axis_index_groups=gro...  50.1 us
    all_to_all x3, blocking collectives, exchange_row(): lax.all_to_all(blocks, 'tensor', 0, 0, axis_index_groups=tensor_rows(1 -...  35.1 us
    ppermute x1, starting transfers between devices, per_device(): lax.ppermute(token_rows, 'section', [(s, section_count - 1 - s) for s in...  19.7 us
    pallas_call x10, Pallas kernels, call(): pl.pallas_call(kernel, out_shape=outs, in_specs=[pl.BlockSpec(memory_spac...  10.2 us
    ppermute x1, starting transfers between devices, per_device(): lax.ppermute(grad_local, 'section', [(s + 1, s) for s in range(section_co...  7.53 us
    ppermute x1, waiting for transfers between devices, per_device(): lax.ppermute(picked, 'section', [(section_count - 1 - s, s) for s in rang...  6.36 us
    all_to_all x1, starting transfers between devices, exchange(): lax.all_to_all(blocks, ('section', 'tensor'), 0, 0, axis_index_groups=gro...  4.85 us
    ppermute x1, starting transfers between devices, per_device(): lax.ppermute(layer_out, 'section', [(s, s + 1) for s in range(section_cou...  3.91 us
  transfers between devices with their start and end apart: 6, of which 3 were waited for; matrix products, arithmetic and copies ran while one was open for 0% of the time, Pallas kernels for 2%

profile of v5, /device:TPU:1, one launch (start us, length us, event | category | flops | bytes accessed | tf_op | source)
XLA Modules:
  0.0 147.3 jit_solution(13211403554971683097)
XLA Ops:
  1.3 0.2 copy-done
  1.6 1.3 collective-permute-start
  2.9 2.2 %shard_map.112 = bf16[4,400,256]{2,1,0:T(8,128)(2,1)} custom-call(bf16[128,256]{1,0:T(8,128)(2,1)} %bitcast.20, f32[1,256]{1,0:T(1,128)} %gain_ref.1, bf16[256,1024]{1,0:T(8,128)(2,1)} %bitcast.24), custom_call_target="tpu_custom_call" | custom-call | bytes 1410048 | tf_op jit(solution)/shard_map/pallas_call | solution.py:60
  5.1 4.9 %all-to-all-start = ((bf16[4,400,256]{2,1,0:T(8,128)(2,1)}), bf16[4,400,256]{2,1,0:T(8,128)(2,1)}, u32[]{:S(2)}, u32[]{:S(2)}) async-start(bf16[4,400,256]{2,1,0:T(8,128)(2,1)} %shard_map.112), calls=%async_computation | async-start | bytes 1638400 | tf_op jit(solution)/shard_map/all_to_all | solution.py:48
  9.9 6.4 %collective-permute-done.reloaded_ref = bf16[128,256]{1,0:T(8,128)(2,1)S(1)} collective-permute-done((bf16[128,256]{1,0:T(8,128)(2,1)S(1)}, bf16[128,256]{1,0:T(8,128)(2,1)S(1)}, u32[]{:S(2)}, u32[]{:S(2)}) %collective-permute-start) | collective-permute-done | bytes 65568 | tf_op jit(solution)/shard_map/ppermute | solution.py:354
  16.3 2.2 %all-to-all-done.parts_ref = bf16[4,400,256]{2,1,0:T(8,128)(2,1)} async-done(((bf16[4,400,256]{2,1,0:T(8,128)(2,1)}), bf16[4,400,256]{2,1,0:T(8,128)(2,1)}, u32[]{:S(2)}, u32[]{:S(2)}) %all-to-all-start) | async-done | bytes 819232 | tf_op jit(solution)/shard_map/all_to_all | solution.py:48
  18.6 1.3 shard_map.114
  19.9 32.2 %all_to_all.35.parts_ref.rows_ref = bf16[4,1040,256]{2,1,0:T(8,128)(2,1)S(1)} all-to-all(bf16[4,1040,256]{2,1,0:T(8,128)(2,1)S(1)} %shard_map.114), channel_id=1, replica_groups={{0,8,16,24},{2,10,18,26},{4,12,20,28},{6,14,22,30},{32,34,36,38},{40,42..., dimensions={0} | all-to-all | bytes 4259840 | tf_op jit(solution)/shard_map/all_to_all | solution.py:48
  52.0 0.1 shard_map.115
  52.2 18.0 %all_to_all.36.back_ref = bf16[4,1024,256]{2,1,0:T(8,128)(2,1)S(1)} all-to-all(bf16[4,1024,256]{2,1,0:T(8,128)(2,1)S(1)} %shard_map.115), channel_id=1, replica_groups={{0,2,4,6},{8,10,12,14},{16,18,20,22},{24,26,28,30},{32,40,48,56},{34,42..., dimensions={0} | all-to-all | bytes 4194304 | tf_op jit(solution)/shard_map/all_to_all | solution.py:48
  70.1 1.2 shard_map.116
  71.3 10.0 %all_to_all.37.kv_ref = bf16[4,64,256]{2,1,0:T(8,128)(2,1)S(1)} all-to-all(bf16[4,64,256]{2,1,0:T(8,128)(2,1)S(1)} %get-tuple-element.17), channel_id=1, replica_groups={{0,2,4,6},{8,10,12,14},{16,18,20,22},{24,26,28,30},{1,3,5,7},{9,11,13,1..., dimensions={0} | all-to-all | bytes 262144 | tf_op jit(solution)/shard_map/all_to_all | solution.py:52
  81.3 2.1 %shard_map.117 = (bf16[128,256]{1,0:T(8,128)(2,1)S(1)}, bf16[128,256]{1,0:T(8,128)(2,1)S(1)}, f32[4,64,128]{2,1,0:T(8,128)S(1)}, f32[8,128]{1,0:T(8,128)S(1)}) custom-call(bf16[4,1024,256]{2,1,0:T(8,128)(2,1)S(1)} %all_to_all.36.back_ref, bf16[16,256,256]{2,1,0:T(8,128)(2,1)S(1)} %get-tuple-element.16.normed_ref, bf16[4,64,256]{2,1,0:T(8,128)(2,1)S(1)} %all_to_all.37.kv_ref, ...), custom_call_target="tpu_custom_call" | custom-call | flops 805306368 | bytes 8982528 | tf_op jit(solution)/shard_map/pallas_call | solution.py:60
  83.3 7.2 %all_to_all.38.grad_kv_ref = f32[4,64,128]{2,1,0:T(8,128)S(1)} all-to-all(f32[4,64,128]{2,1,0:T(8,128)S(1)} %get-tuple-element.20), channel_id=1, replica_groups={{0,2,4,6},{8,10,12,14},{16,18,20,22},{24,26,28,30},{1,3,5,7},{9,11,13,1..., dimensions={0} | all-to-all | bytes 262144 | tf_op jit(solution)/shard_map/all_to_all | solution.py:52
  90.5 1.4 shard_map.118
  91.9 18.0 %all_to_all.39.parts_ref = bf16[4,1040,256]{2,1,0:T(8,128)(2,1)S(1)} all-to-all(bf16[4,1040,256]{2,1,0:T(8,128)(2,1)S(1)} %shard_map.118), channel_id=1, replica_groups={{0,8,16,24},{2,10,18,26},{4,12,20,28},{6,14,22,30},{1,9,17,25},{3,11,19..., dimensions={0} | all-to-all | bytes 4259840 | tf_op jit(solution)/shard_map/all_to_all | solution.py:52
  109.8 1.1 shard_map.119
  110.9 3.5 %all-to-all-start.6 = ((bf16[4,272,256]{2,1,0:T(8,128)(2,1)}), bf16[4,272,256]{2,1,0:T(8,128)(2,1)S(1)}, u32[]{:S(2)}, u32[]{:S(2)}) async-start(bf16[4,272,256]{2,1,0:T(8,128)(2,1)} %shard_map.119), calls=%async_computation.6 | async-start | bytes 1114112 | tf_op jit(solution)/shard_map/all_to_all | solution.py:52
  114.4 19.7 %collective-permute-start.3 = (bf16[128,256]{1,0:T(8,128)(2,1)S(1)}, bf16[128,256]{1,0:T(8,128)(2,1)S(1)}, u32[]{:S(2)}, u32[]{:S(2)}) collective-permute-start(bf16[128,256]{1,0:T(8,128)(2,1)S(1)} %bitcast.22), channel_id=1, source_target_pairs={{0,480},{32,448},{64,416},{96,384},{128,352},{160,320},{192,288},{... | collective-permute-start | bytes 196616 | tf_op jit(solution)/shard_map/ppermute | solution.py:378
  134.1 0.2 shard_map.120
  134.3 3.9 %collective-permute-start.1 = (bf16[128,256]{1,0:T(8,128)(2,1)S(1)}, bf16[128,256]{1,0:T(8,128)(2,1)S(1)}, u32[]{:S(2)}, u32[]{:S(2)}) collective-permute-start(bf16[128,256]{1,0:T(8,128)(2,1)S(1)} %get-tuple-element.24), channel_id=1, source_target_pairs={{0,32},{32,64},{64,96},{96,128},{128,160},{160,192},{192,224},{224... | collective-permute-start | bytes 196616 | tf_op jit(solution)/shard_map/ppermute | solution.py:417
  138.2 7.5 %collective-permute-start.2 = (bf16[128,256]{1,0:T(8,128)(2,1)S(1)}, bf16[128,256]{1,0:T(8,128)(2,1)S(1)}, u32[]{:S(2)}, u32[]{:S(2)}) collective-permute-start(bf16[128,256]{1,0:T(8,128)(2,1)S(1)} %get-tuple-element.25), channel_id=1, source_target_pairs={{32,0},{64,32},{96,64},{128,96},{160,128},{192,160},{224,192},{256... | collective-permute-start | bytes 196616 | tf_op jit(solution)/shard_map/ppermute | solution.py:418
  145.8 0.9 collective-permute-done.2.grad_ref
  146.6 0.7 shard_map.121
  (18 shorter events, 0.1 us)
Async XLA Ops:
  0.6 0.9 copy-start
  0.6 15.7 %copy-start.5 = (bf16[1,128,256]{2,1,0:T(8,128)(2,1)S(1)}, bf16[1,128,256]{2,1,0:T(8,128)(2,1)}, u32[]{:S(2)}) copy-start(bf16[1,128,256]{2,1,0:T(8,128)(2,1)} %param.9) | copy-start | bytes 196612
  1.6 14.7 %collective-permute-start = (bf16[128,256]{1,0:T(8,128)(2,1)S(1)}, bf16[128,256]{1,0:T(8,128)(2,1)S(1)}, u32[]{:S(2)}, u32[]{:S(2)}) collective-permute-start(bf16[128,256]{1,0:T(8,128)(2,1)S(1)} %dynamic-slice_bitcast_fusion), channel_id=1, source_target_pairs={{480,0},{448,32},{416,64},{384,96},{352,128},{320,160},{288,192},{... | collective-permute-start | bytes 196616 | tf_op jit(solution)/shard_map/ppermute | solution.py:354
  5.1 13.5 %all-to-all-start = ((bf16[4,400,256]{2,1,0:T(8,128)(2,1)}), bf16[4,400,256]{2,1,0:T(8,128)(2,1)}, u32[]{:S(2)}, u32[]{:S(2)}) async-start(bf16[4,400,256]{2,1,0:T(8,128)(2,1)} %shard_map.112), calls=%async_computation | async-start | bytes 1638400 | tf_op jit(solution)/shard_map/all_to_all | solution.py:48
  16.3 2.3 %copy-start.4 = (bf16[1,128,256]{2,1,0:T(8,128)(2,1)S(1)}, bf16[1,128,256]{2,1,0:T(8,128)(2,1)}, u32[]{:S(2)}) copy-start(bf16[1,128,256]{2,1,0:T(8,128)(2,1)} %param.12) | copy-start | bytes 196612
  52.2 18.0 %copy-start.3 = (f32[384,128]{1,0:T(8,128)S(1)}, f32[384,128]{1,0:T(8,128)}, u32[]{:S(2)}) copy-start(f32[384,128]{1,0:T(8,128)} %constant.9.clone.table_ref) | copy-start | bytes 589828
  70.1 11.1 %copy-start.1 = (bf16[1,4096,256]{2,1,0:T(8,128)(2,1)S(1)}, bf16[1,4096,256]{2,1,0:T(8,128)(2,1)}, u32[]{:S(2)}) copy-start(bf16[1,4096,256]{2,1,0:T(8,128)(2,1)} %param.14) | copy-start | bytes 6291460
  70.1 11.1 %copy-start.2 = (bf16[1,256,4096]{2,1,0:T(8,128)(2,1)S(1)}, bf16[1,256,4096]{2,1,0:T(8,128)(2,1)}, u32[]{:S(2)}) copy-start(bf16[1,256,4096]{2,1,0:T(8,128)(2,1)} %param.16) | copy-start | bytes 6291460
  109.8 24.3 %copy-start.6 = (f32[1,256]{1,0:T(1,128)S(1)}, f32[1,256]{1,0:T(1,128)}, u32[]{:S(2)}) copy-start(f32[1,256]{1,0:T(1,128)} %gain_ref.1) | copy-start | bytes 3076
  110.9 23.2 %all-to-all-start.6 = ((bf16[4,272,256]{2,1,0:T(8,128)(2,1)}), bf16[4,272,256]{2,1,0:T(8,128)(2,1)S(1)}, u32[]{:S(2)}, u32[]{:S(2)}) async-start(bf16[4,272,256]{2,1,0:T(8,128)(2,1)} %shard_map.119), calls=%async_computation.6 | async-start | bytes 1114112 | tf_op jit(solution)/shard_map/all_to_all | solution.py:52
  114.4 31.4 %collective-permute-start.3 = (bf16[128,256]{1,0:T(8,128)(2,1)S(1)}, bf16[128,256]{1,0:T(8,128)(2,1)S(1)}, u32[]{:S(2)}, u32[]{:S(2)}) collective-permute-start(bf16[128,256]{1,0:T(8,128)(2,1)S(1)} %bitcast.22), channel_id=1, source_target_pairs={{0,480},{32,448},{64,416},{96,384},{128,352},{160,320},{192,288},{... | collective-permute-start | bytes 196616 | tf_op jit(solution)/shard_map/ppermute | solution.py:378
  134.3 11.5 %collective-permute-start.1 = (bf16[128,256]{1,0:T(8,128)(2,1)S(1)}, bf16[128,256]{1,0:T(8,128)(2,1)S(1)}, u32[]{:S(2)}, u32[]{:S(2)}) collective-permute-start(bf16[128,256]{1,0:T(8,128)(2,1)S(1)} %get-tuple-element.24), channel_id=1, source_target_pairs={{0,32},{32,64},{64,96},{96,128},{128,160},{160,192},{192,224},{224... | collective-permute-start | bytes 196616 | tf_op jit(solution)/shard_map/ppermute | solution.py:417
  138.2 8.4 %collective-permute-start.2 = (bf16[128,256]{1,0:T(8,128)(2,1)S(1)}, bf16[128,256]{1,0:T(8,128)(2,1)S(1)}, u32[]{:S(2)}, u32[]{:S(2)}) collective-permute-start(bf16[128,256]{1,0:T(8,128)(2,1)S(1)} %get-tuple-element.25), channel_id=1, source_target_pairs={{32,0},{64,32},{96,64},{128,96},{160,128},{192,160},{224,192},{256... | collective-permute-start | bytes 196616 | tf_op jit(solution)/shard_map/ppermute | solution.py:418

commit v6 on v5

--- a/solution.py
+++ b/solution.py
@@ -358,7 +358,7 @@
     gain_row = norm_gain
 
     back_rows = call(
-        pick_back, (shape((TOK, COLS)),), reloaded, token_rows, flops=1000000000000
+        pick_back, (shape((TOK, COLS)),), reloaded, token_rows, flops=2 * 10**10
     )[0]
     held = [pltpu.VMEM(a.shape, a.dtype) for a in (token_rows, gain_row, kv_w)]
     blocks = call(
@@ -372,10 +372,12 @@
     blocks = exchange(blocks, FIRST)
     blocks = call(second_blocks, (shape((SIDE, 1040, COLS)),), blocks, back_rows, cot_rows)[0]
     rows = exchange(blocks, SECOND)
+    evicting, _ = lax.optimization_barrier((token_rows, back_rows))
+    evicted = lax.ppermute(evicting, "section", [(s, section_count - 1 - s) for s in range(half)])
+    rows, evicted = lax.optimization_barrier((rows, evicted))
     blocks = call(third_blocks, (shape((SIDE, 8 * TOK, COLS)),), rows)[0]
     back = exchange(blocks, FIRST)
 
-    evicted = lax.ppermute(token_rows, "section", [(s, section_count - 1 - s) for s in range(half)])
     normed, kv_own, kv_raw, factor = call(
         norm_and_kv,
         (

time: 148 us -> 145 us (0.980)
  blocking collectives: 85.2 us -> 63.8 us
  waiting for transfers between devices: 9.47 us -> 21.4 us
  starting transfers between devices: 40.7 us -> 46.9 us
  Pallas kernels: 10.2 us -> 8.21 us
    all_to_all x2 -> x1, blocking collectives: 50.1 us -> 18.1 us  [exchange(): lax.all_to_all(blocks, ('section', 'tensor'), 0, 0, axis_index_groups=gro...]
    ppermute x1, starting transfers between devices: 3.91 us -> 16.9 us  [per_device(): lax.ppermute(layer_out, 'section', [(s, s + 1) for s in range(section_cou...]
    all_to_all x3 -> x4, blocking collectives: 35.1 us -> 45.7 us  [exchange_row(): lax.all_to_all(blocks, 'tensor', 0, 0, axis_index_groups=tensor_rows(1 -...]
    all_to_all x1 -> x2, waiting for transfers between devices: 2.24 us -> 10.6 us  [exchange(): lax.all_to_all(blocks, ('section', 'tensor'), 0, 0, axis_index_groups=gro...]
    ppermute x1, starting transfers between devices: 7.53 us -> 2.48 us  [per_device(): lax.ppermute(grad_local, 'section', [(s + 1, s) for s in range(section_co...]
    all_to_all x1 -> x2, starting transfers between devices: 4.85 us -> 9.44 us  [exchange(): lax.all_to_all(blocks, ('section', 'tensor'), 0, 0, axis_index_groups=gro...]
    all_to_all x1 -> x0, starting transfers between devices: 3.47 us -> none  [exchange_row(): lax.all_to_all(blocks, 'tensor', 0, 0, axis_index_groups=tensor_rows(1 -...]
    ppermute x1, starting transfers between devices: 19.7 us -> 16.7 us  [per_device(): lax.ppermute(evicting, 'section', [(s, section_count - 1 - s) for s in ra...]
  transfers between devices with their start and end apart: 6 -> 6, of which waited for: 3 -> 5; matrix products, arithmetic and copies ran while one was open for 0% -> 0% of each run, Pallas kernels for 2% -> 2%
where the time goes in v6:
time: 145 us; the launch traced here: 143 us
  blocking collectives  63.8 us (44%)
  starting transfers between devices  46.9 us (32%)
  waiting for transfers between devices  21.4 us (15%)
  Pallas kernels  8.21 us (6%)
  local copies, waits for them, and re-layouts  1.59 us (1%)
  between operations  1.45 us (1%)
    all_to_all x4, blocking collectives, exchange_row(): lax.all_to_all(blocks, 'tensor', 0, 0, axis_index_groups=tensor_rows(1 -...  45.7 us
    all_to_all x1, blocking collectives, exchange(): lax.all_to_all(blocks, ('section', 'tensor'), 0, 0, axis_index_groups=gro...  18.1 us
    ppermute x1, starting transfers between devices, per_device(): lax.ppermute(layer_out, 'section', [(s, s + 1) for s in range(section_cou...  16.9 us
    ppermute x1, starting transfers between devices, per_device(): lax.ppermute(evicting, 'section', [(s, section_count - 1 - s) for s in ra...  16.7 us
    all_to_all x2, waiting for transfers between devices, exchange(): lax.all_to_all(blocks, ('section', 'tensor'), 0, 0, axis_index_groups=gro...  10.6 us
    all_to_all x2, starting transfers between devices, exchange(): lax.all_to_all(blocks, ('section', 'tensor'), 0, 0, axis_index_groups=gro...  9.44 us
    pallas_call x10, Pallas kernels, call(): pl.pallas_call(kernel, out_shape=outs, in_specs=[pl.BlockSpec(memory_spac...  8.21 us
    ppermute x1, waiting for transfers between devices, per_device(): lax.ppermute(picked, 'section', [(section_count - 1 - s, s) for s in rang...  6.39 us
  transfers between devices with their start and end apart: 6, of which 5 were waited for; matrix products, arithmetic and copies ran while one was open for 0% of the time, Pallas kernels for 2%

profile of v6, /device:TPU:1, one launch (start us, length us, event | category | flops | bytes accessed | tf_op | source)
XLA Modules:
  0.0 143.2 jit_solution(5404785197719178796)
XLA Ops:
  1.3 0.2 copy-done
  1.6 1.3 collective-permute-start
  2.9 2.2 %shard_map.112 = bf16[4,400,256]{2,1,0:T(8,128)(2,1)} custom-call(bf16[128,256]{1,0:T(8,128)(2,1)} %bitcast.18, f32[1,256]{1,0:T(1,128)} %gain_ref.1, bf16[256,1024]{1,0:T(8,128)(2,1)} %bitcast.24), custom_call_target="tpu_custom_call" | custom-call | bytes 1410048 | tf_op jit(solution)/shard_map/pallas_call | solution.py:60
  5.1 4.9 %all-to-all-start = ((bf16[4,400,256]{2,1,0:T(8,128)(2,1)}), bf16[4,400,256]{2,1,0:T(8,128)(2,1)S(1)}, u32[]{:S(2)}, u32[]{:S(2)}) async-start(bf16[4,400,256]{2,1,0:T(8,128)(2,1)} %shard_map.112), calls=%async_computation | async-start | bytes 1638400 | tf_op jit(solution)/shard_map/all_to_all | solution.py:48
  9.9 6.4 %collective-permute-done.reloaded_ref = bf16[128,256]{1,0:T(8,128)(2,1)S(1)} collective-permute-done((bf16[128,256]{1,0:T(8,128)(2,1)S(1)}, bf16[128,256]{1,0:T(8,128)(2,1)S(1)}, u32[]{:S(2)}, u32[]{:S(2)}) %collective-permute-start) | collective-permute-done | bytes 65568 | tf_op jit(solution)/shard_map/ppermute | solution.py:354
  16.3 2.1 %all-to-all-done.parts_ref = bf16[4,400,256]{2,1,0:T(8,128)(2,1)S(1)} async-done(((bf16[4,400,256]{2,1,0:T(8,128)(2,1)}), bf16[4,400,256]{2,1,0:T(8,128)(2,1)S(1)}, u32[]{:S(2)}, u32[]{:S(2)}) %all-to-all-start) | async-done | bytes 819232 | tf_op jit(solution)/shard_map/all_to_all | solution.py:48
  18.6 1.3 copy-done.1
  19.9 4.6 %all-to-all-start.1 = ((bf16[4,1040,256]{2,1,0:T(8,128)(2,1)}), bf16[4,1040,256]{2,1,0:T(8,128)(2,1)S(1)}, u32[]{:S(2)}, u32[]{:S(2)}) async-start(bf16[4,1040,256]{2,1,0:T(8,128)(2,1)} %copy-done.1), calls=%async_computation.1 | async-start | bytes 4259840 | tf_op jit(solution)/shard_map/all_to_all | solution.py:48
  24.5 16.7 %collective-permute-start.1 = (bf16[128,256]{1,0:T(8,128)(2,1)S(1)}, bf16[128,256]{1,0:T(8,128)(2,1)S(1)}, u32[]{:S(2)}, u32[]{:S(2)}) collective-permute-start(bf16[128,256]{1,0:T(8,128)(2,1)S(1)} %bitcast.20), channel_id=1, source_target_pairs={{0,480},{32,448},{64,416},{96,384},{128,352},{160,320},{192,288},{... | collective-permute-start | bytes 196616 | tf_op jit(solution)/shard_map/ppermute | solution.py:376
  41.2 1.3 collective-permute-done.1.evicted_ref
  42.5 8.5 %all-to-all-done.1.parts_ref.rows_ref = bf16[4,1040,256]{2,1,0:T(8,128)(2,1)S(1)} async-done(((bf16[4,1040,256]{2,1,0:T(8,128)(2,1)}), bf16[4,1040,256]{2,1,0:T(8,128)(2,1)S(1)}, u32[]{:S(2)}, u32[]{:S(2)}) %all-to-all-start.1) | async-done | bytes 2129952 | tf_op jit(solution)/shard_map/all_to_all | solution.py:48
  51.2 18.1 %all_to_all.35.back_ref = bf16[4,1024,256]{2,1,0:T(8,128)(2,1)S(1)} all-to-all(bf16[4,1024,256]{2,1,0:T(8,128)(2,1)S(1)} %shard_map.115), channel_id=1, replica_groups={{0,2,4,6},{8,10,12,14},{16,18,20,22},{24,26,28,30},{32,40,48,56},{34,42..., dimensions={0} | all-to-all | bytes 4194304 | tf_op jit(solution)/shard_map/all_to_all | solution.py:48
  69.3 1.2 shard_map.116
  70.4 8.4 %all_to_all.36.kv_ref = bf16[4,64,256]{2,1,0:T(8,128)(2,1)S(1)} all-to-all(bf16[4,64,256]{2,1,0:T(8,128)(2,1)S(1)} %get-tuple-element.22), channel_id=1, replica_groups={{0,2,4,6},{8,10,12,14},{16,18,20,22},{24,26,28,30},{1,3,5,7},{9,11,13,1..., dimensions={0} | all-to-all | bytes 262144 | tf_op jit(solution)/shard_map/all_to_all | solution.py:52
  78.8 2.1 %shard_map.117 = (bf16[128,256]{1,0:T(8,128)(2,1)S(1)}, bf16[128,256]{1,0:T(8,128)(2,1)S(1)}, f32[4,64,128]{2,1,0:T(8,128)S(1)}, f32[8,128]{1,0:T(8,128)S(1)}) custom-call(bf16[4,1024,256]{2,1,0:T(8,128)(2,1)S(1)} %all_to_all.35.back_ref, bf16[16,256,256]{2,1,0:T(8,128)(2,1)S(1)} %get-tuple-element.21.normed_ref, bf16[4,64,256]{2,1,0:T(8,128)(2,1)S(1)} %all_to_all.36.kv_ref, ...), custom_call_target="tpu_custom_call" | custom-call | flops 805306368 | bytes 8982528 | tf_op jit(solution)/shard_map/pallas_call | solution.py:60
  80.9 7.2 %all_to_all.37.grad_kv_ref = f32[4,64,128]{2,1,0:T(8,128)S(1)} all-to-all(f32[4,64,128]{2,1,0:T(8,128)S(1)} %get-tuple-element.25), channel_id=1, replica_groups={{0,2,4,6},{8,10,12,14},{16,18,20,22},{24,26,28,30},{1,3,5,7},{9,11,13,1..., dimensions={0} | all-to-all | bytes 262144 | tf_op jit(solution)/shard_map/all_to_all | solution.py:52
  88.0 1.4 shard_map.118
  89.4 18.0 %all_to_all.38.parts_ref = bf16[4,1040,256]{2,1,0:T(8,128)(2,1)S(1)} all-to-all(bf16[4,1040,256]{2,1,0:T(8,128)(2,1)S(1)} %shard_map.118), channel_id=1, replica_groups={{0,8,16,24},{2,10,18,26},{4,12,20,28},{6,14,22,30},{1,9,17,25},{3,11,19..., dimensions={0} | all-to-all | bytes 4259840 | tf_op jit(solution)/shard_map/all_to_all | solution.py:52
  107.4 0.3 shard_map.119
  107.6 12.2 %all_to_all.39.parts_ref = bf16[4,272,256]{2,1,0:T(8,128)(2,1)S(1)} all-to-all(bf16[4,272,256]{2,1,0:T(8,128)(2,1)S(1)} %shard_map.119), channel_id=1, replica_groups={{0,2,4,6},{8,10,12,14},{16,18,20,22},{24,26,28,30},{1,3,5,7},{9,11,13,1..., dimensions={0} | all-to-all | bytes 1114112 | tf_op jit(solution)/shard_map/all_to_all | solution.py:52
  120.0 16.9 %collective-permute-start.2 = (bf16[128,256]{1,0:T(8,128)(2,1)S(1)}, bf16[128,256]{1,0:T(8,128)(2,1)S(1)}, u32[]{:S(2)}, u32[]{:S(2)}) collective-permute-start(bf16[128,256]{1,0:T(8,128)(2,1)S(1)} %get-tuple-element.29), channel_id=1, source_target_pairs={{0,32},{32,64},{64,96},{96,128},{128,160},{160,192},{192,224},{224... | collective-permute-start | bytes 196616 | tf_op jit(solution)/shard_map/ppermute | solution.py:419
  137.0 2.5 %collective-permute-start.3 = (bf16[128,256]{1,0:T(8,128)(2,1)S(1)}, bf16[128,256]{1,0:T(8,128)(2,1)S(1)}, u32[]{:S(2)}, u32[]{:S(2)}) collective-permute-start(bf16[128,256]{1,0:T(8,128)(2,1)S(1)} %get-tuple-element.30), channel_id=1, source_target_pairs={{32,0},{64,32},{96,64},{128,96},{160,128},{192,160},{224,192},{256... | collective-permute-start | bytes 196616 | tf_op jit(solution)/shard_map/ppermute | solution.py:420
  139.4 3.1 %collective-permute-done.3.grad_ref = bf16[128,256]{1,0:T(8,128)(2,1)S(1)} collective-permute-done((bf16[128,256]{1,0:T(8,128)(2,1)S(1)}, bf16[128,256]{1,0:T(8,128)(2,1)S(1)}, u32[]{:S(2)}, u32[]{:S(2)}) %collective-permute-start.3) | collective-permute-done | bytes 65568 | tf_op jit(solution)/shard_map/ppermute | solution.py:420
  142.5 0.7 shard_map.121
  (20 shorter events, 0.5 us)
Async XLA Ops:
  0.6 0.9 copy-start
  0.6 15.7 %copy-start.5 = (bf16[1,128,256]{2,1,0:T(8,128)(2,1)S(1)}, bf16[1,128,256]{2,1,0:T(8,128)(2,1)}, u32[]{:S(2)}) copy-start(bf16[1,128,256]{2,1,0:T(8,128)(2,1)} %param.9) | copy-start | bytes 196612
  1.6 14.7 %collective-permute-start = (bf16[128,256]{1,0:T(8,128)(2,1)S(1)}, bf16[128,256]{1,0:T(8,128)(2,1)S(1)}, u32[]{:S(2)}, u32[]{:S(2)}) collective-permute-start(bf16[128,256]{1,0:T(8,128)(2,1)S(1)} %dynamic-slice_bitcast_fusion), channel_id=1, source_target_pairs={{480,0},{448,32},{416,64},{384,96},{352,128},{320,160},{288,192},{... | collective-permute-start | bytes 196616 | tf_op jit(solution)/shard_map/ppermute | solution.py:354
  5.1 13.4 %all-to-all-start = ((bf16[4,400,256]{2,1,0:T(8,128)(2,1)}), bf16[4,400,256]{2,1,0:T(8,128)(2,1)S(1)}, u32[]{:S(2)}, u32[]{:S(2)}) async-start(bf16[4,400,256]{2,1,0:T(8,128)(2,1)} %shard_map.112), calls=%async_computation | async-start | bytes 1638400 | tf_op jit(solution)/shard_map/all_to_all | solution.py:48
  9.9 8.5 %copy-start.6 = (bf16[1,128,256]{2,1,0:T(8,128)(2,1)S(1)}, bf16[1,128,256]{2,1,0:T(8,128)(2,1)}, u32[]{:S(2)}) copy-start(bf16[1,128,256]{2,1,0:T(8,128)(2,1)} %param.12) | copy-start | bytes 196612
  18.6 1.3 copy-start.1
  19.9 31.1 %all-to-all-start.1 = ((bf16[4,1040,256]{2,1,0:T(8,128)(2,1)}), bf16[4,1040,256]{2,1,0:T(8,128)(2,1)S(1)}, u32[]{:S(2)}, u32[]{:S(2)}) async-start(bf16[4,1040,256]{2,1,0:T(8,128)(2,1)} %copy-done.1), calls=%async_computation.1 | async-start | bytes 4259840 | tf_op jit(solution)/shard_map/all_to_all | solution.py:48
  24.5 18.0 %collective-permute-start.1 = (bf16[128,256]{1,0:T(8,128)(2,1)S(1)}, bf16[128,256]{1,0:T(8,128)(2,1)S(1)}, u32[]{:S(2)}, u32[]{:S(2)}) collective-permute-start(bf16[128,256]{1,0:T(8,128)(2,1)S(1)} %bitcast.20), channel_id=1, source_target_pairs={{0,480},{32,448},{64,416},{96,384},{128,352},{160,320},{192,288},{... | collective-permute-start | bytes 196616 | tf_op jit(solution)/shard_map/ppermute | solution.py:376
  51.1 18.1 %copy-start.4 = (f32[384,128]{1,0:T(8,128)S(1)}, f32[384,128]{1,0:T(8,128)}, u32[]{:S(2)}) copy-start(f32[384,128]{1,0:T(8,128)} %constant.9.clone.table_ref) | copy-start | bytes 589828
  69.3 9.5 %copy-start.2 = (bf16[1,4096,256]{2,1,0:T(8,128)(2,1)S(1)}, bf16[1,4096,256]{2,1,0:T(8,128)(2,1)}, u32[]{:S(2)}) copy-start(bf16[1,4096,256]{2,1,0:T(8,128)(2,1)} %param.14) | copy-start | bytes 6291460
  69.3 9.5 %copy-start.3 = (bf16[1,256,4096]{2,1,0:T(8,128)(2,1)S(1)}, bf16[1,256,4096]{2,1,0:T(8,128)(2,1)}, u32[]{:S(2)}) copy-start(bf16[1,256,4096]{2,1,0:T(8,128)(2,1)} %param.16) | copy-start | bytes 6291460
  107.4 12.4 %copy-start.7 = (f32[1,256]{1,0:T(1,128)S(1)}, f32[1,256]{1,0:T(1,128)}, u32[]{:S(2)}) copy-start(f32[1,256]{1,0:T(1,128)} %gain_ref.1) | copy-start | bytes 3076
  120.0 19.4 %collective-permute-start.2 = (bf16[128,256]{1,0:T(8,128)(2,1)S(1)}, bf16[128,256]{1,0:T(8,128)(2,1)S(1)}, u32[]{:S(2)}, u32[]{:S(2)}) collective-permute-start(bf16[128,256]{1,0:T(8,128)(2,1)S(1)} %get-tuple-element.29), channel_id=1, source_target_pairs={{0,32},{32,64},{64,96},{96,128},{128,160},{160,192},{192,224},{224... | collective-permute-start | bytes 196616 | tf_op jit(solution)/shard_map/ppermute | solution.py:419
  137.0 5.6 %collective-permute-start.3 = (bf16[128,256]{1,0:T(8,128)(2,1)S(1)}, bf16[128,256]{1,0:T(8,128)(2,1)S(1)}, u32[]{:S(2)}, u32[]{:S(2)}) collective-permute-start(bf16[128,256]{1,0:T(8,128)(2,1)S(1)} %get-tuple-element.30), channel_id=1, source_target_pairs={{32,0},{64,32},{96,64},{128,96},{160,128},{192,160},{224,192},{256... | collective-permute-start | bytes 196616 | tf_op jit(solution)/shard_map/ppermute | solution.py:420

commit v7 on v6

--- a/solution.py
+++ b/solution.py
@@ -89,7 +89,12 @@
     place = position()
     sources, out_ref, (rows_ref, gain_ref, kvw_ref), sems = refs[:3], refs[3], refs[4:7], refs[7]
     held = (rows_ref, gain_ref, kvw_ref)
-    copies = [pltpu.make_async_copy(a, b, sems.at[n]) for n, (a, b) in enumerate(zip(sources, held))]
+    pairs = list(zip(sources[:2], held[:2]))
+    half = KVH * HD
+    for side in range(2):
+        columns = pl.ds(side * half, half)
+        pairs.append((sources[2].at[:, columns], kvw_ref.at[:, columns]))
+    copies = [pltpu.make_async_copy(a, b, sems.at[n]) for n, (a, b) in enumerate(pairs)]
     for copy in copies:
         copy.start()
     for copy in copies[:2]:
@@ -103,17 +108,20 @@
     for j in range(SIDE):
         out_ref[j, 0:TOK] = rows_ref[...]
         out_ref[j, 128:144] = gains.astype(jnp.bfloat16)
-    copies[2].wait()
     swapped = place[1] > 1
-    for x in range(SIDE):
-        keys = kvw_ref[:, x * HD : (x + 1) * HD].T
-        values = kvw_ref[:, (KVH + x) * HD : (KVH + x + 1) * HD].T
-        for y in range(SIDE):
-            k, j = jnp.where(swapped, y, x), jnp.where(swapped, x, y)
-            start = pl.multiple_of(144 + 64 * k, 16)
-            out_ref[j, pl.ds(start, 16)] = keys[16 * y : 16 * y + 16]
-            out_ref[j, pl.ds(start + 16, 16)] = keys[64 + 16 * y : 80 + 16 * y]
-            out_ref[j, pl.ds(start + 32, 32)] = values[32 * y : 32 * y + 32]
+    for side in range(2):
+        copies[2 + side].wait()
+        for x in range(SIDE):
+            head = side * KVH + x
+            columns = kvw_ref[:, head * HD : (head + 1) * HD].T
+            for y in range(SIDE):
+                k, j = jnp.where(swapped, y, x), jnp.where(swapped, x, y)
+                start = pl.multiple_of(144 + 64 * k, 16)
+                if side == 0:
+                    out_ref[j, pl.ds(start, 16)] = columns[16 * y : 16 * y + 16]
+                    out_ref[j, pl.ds(start + 16, 16)] = columns[64 + 16 * y : 80 + 16 * y]
+                else:
+                    out_ref[j, pl.ds(start + 32, 32)] = columns[32 * y : 32 * y + 32]
 
 
 def pick_back(reloaded_ref, rows_ref, back_ref):
@@ -365,7 +373,7 @@
         first_blocks,
         (shape((SIDE, 400, COLS)),),
         token_rows, gain_row, kv_w,
-        scratch=(*held, pltpu.SemaphoreType.DMA((3,))),
+        scratch=(*held, pltpu.SemaphoreType.DMA((4,))),
         in_place=True,
         vmem=58,
     )[0]

time: 145 us -> 145 us (level)
  no operation moved by 1% of the time
where the time goes in v7:
time: 145 us; the launch traced here: 143 us
  blocking collectives  63.8 us (44%)
  starting transfers between devices  46.9 us (32%)
  waiting for transfers between devices  21.4 us (15%)
  Pallas kernels  8.18 us (6%)
  local copies, waits for them, and re-layouts  1.59 us (1%)
  between operations  1.45 us (1%)
    all_to_all x4, blocking collectives, exchange_row(): lax.all_to_all(blocks, 'tensor', 0, 0, axis_index_groups=tensor_rows(1 -...  45.7 us
    all_to_all x1, blocking collectives, exchange(): lax.all_to_all(blocks, ('section', 'tensor'), 0, 0, axis_index_groups=gro...  18.1 us
    ppermute x1, starting transfers between devices, per_device(): lax.ppermute(layer_out, 'section', [(s, s + 1) for s in range(section_cou...  16.9 us
    ppermute x1, starting transfers between devices, per_device(): lax.ppermute(evicting, 'section', [(s, section_count - 1 - s) for s in ra...  16.7 us
    all_to_all x2, waiting for transfers between devices, exchange(): lax.all_to_all(blocks, ('section', 'tensor'), 0, 0, axis_index_groups=gro...  10.5 us
    all_to_all x2, starting transfers between devices, exchange(): lax.all_to_all(blocks, ('section', 'tensor'), 0, 0, axis_index_groups=gro...  9.44 us
    pallas_call x10, Pallas kernels, call(): pl.pallas_call(kernel, out_shape=outs, in_specs=[pl.BlockSpec(memory_spac...  8.18 us
    ppermute x1, waiting for transfers between devices, per_device(): lax.ppermute(picked, 'section', [(section_count - 1 - s, s) for s in rang...  6.41 us
  transfers between devices with their start and end apart: 6, of which 5 were waited for; matrix products, arithmetic and copies ran while one was open for 0% of the time, Pallas kernels for 2%

profile of v7, /device:TPU:1, one launch (start us, length us, event | category | flops | bytes accessed | tf_op | source)
XLA Modules:
  0.0 143.2 jit_solution(17325058545136355523)
XLA Ops:
  1.3 0.2 copy-done
  1.6 1.3 collective-permute-start
  2.9 2.2 %shard_map.112 = bf16[4,400,256]{2,1,0:T(8,128)(2,1)} custom-call(bf16[128,256]{1,0:T(8,128)(2,1)} %bitcast.18, f32[1,256]{1,0:T(1,128)} %gain_ref.1, bf16[256,1024]{1,0:T(8,128)(2,1)} %bitcast.24), custom_call_target="tpu_custom_call" | custom-call | bytes 1410048 | tf_op jit(solution)/shard_map/pallas_call | solution.py:60
  5.0 4.9 %all-to-all-start = ((bf16[4,400,256]{2,1,0:T(8,128)(2,1)}), bf16[4,400,256]{2,1,0:T(8,128)(2,1)S(1)}, u32[]{:S(2)}, u32[]{:S(2)}) async-start(bf16[4,400,256]{2,1,0:T(8,128)(2,1)} %shard_map.112), calls=%async_computation | async-start | bytes 1638400 | tf_op jit(solution)/shard_map/all_to_all | solution.py:48
  9.9 6.4 %collective-permute-done.reloaded_ref = bf16[128,256]{1,0:T(8,128)(2,1)S(1)} collective-permute-done((bf16[128,256]{1,0:T(8,128)(2,1)S(1)}, bf16[128,256]{1,0:T(8,128)(2,1)S(1)}, u32[]{:S(2)}, u32[]{:S(2)}) %collective-permute-start) | collective-permute-done | bytes 65568 | tf_op jit(solution)/shard_map/ppermute | solution.py:362
  16.3 2.1 %all-to-all-done.parts_ref = bf16[4,400,256]{2,1,0:T(8,128)(2,1)S(1)} async-done(((bf16[4,400,256]{2,1,0:T(8,128)(2,1)}), bf16[4,400,256]{2,1,0:T(8,128)(2,1)S(1)}, u32[]{:S(2)}, u32[]{:S(2)}) %all-to-all-start) | async-done | bytes 819232 | tf_op jit(solution)/shard_map/all_to_all | solution.py:48
  18.6 1.3 copy-done.1
  19.9 4.6 %all-to-all-start.1 = ((bf16[4,1040,256]{2,1,0:T(8,128)(2,1)}), bf16[4,1040,256]{2,1,0:T(8,128)(2,1)S(1)}, u32[]{:S(2)}, u32[]{:S(2)}) async-start(bf16[4,1040,256]{2,1,0:T(8,128)(2,1)} %copy-done.1), calls=%async_computation.1 | async-start | bytes 4259840 | tf_op jit(solution)/shard_map/all_to_all | solution.py:48
  24.5 16.7 %collective-permute-start.1 = (bf16[128,256]{1,0:T(8,128)(2,1)S(1)}, bf16[128,256]{1,0:T(8,128)(2,1)S(1)}, u32[]{:S(2)}, u32[]{:S(2)}) collective-permute-start(bf16[128,256]{1,0:T(8,128)(2,1)S(1)} %bitcast.20), channel_id=1, source_target_pairs={{0,480},{32,448},{64,416},{96,384},{128,352},{160,320},{192,288},{... | collective-permute-start | bytes 196616 | tf_op jit(solution)/shard_map/ppermute | solution.py:384
  41.2 1.3 collective-permute-done.1.evicted_ref
  42.5 8.5 %all-to-all-done.1.parts_ref.rows_ref = bf16[4,1040,256]{2,1,0:T(8,128)(2,1)S(1)} async-done(((bf16[4,1040,256]{2,1,0:T(8,128)(2,1)}), bf16[4,1040,256]{2,1,0:T(8,128)(2,1)S(1)}, u32[]{:S(2)}, u32[]{:S(2)}) %all-to-all-start.1) | async-done | bytes 2129952 | tf_op jit(solution)/shard_map/all_to_all | solution.py:48
  51.1 18.1 %all_to_all.35.back_ref = bf16[4,1024,256]{2,1,0:T(8,128)(2,1)S(1)} all-to-all(bf16[4,1024,256]{2,1,0:T(8,128)(2,1)S(1)} %shard_map.115), channel_id=1, replica_groups={{0,2,4,6},{8,10,12,14},{16,18,20,22},{24,26,28,30},{32,40,48,56},{34,42..., dimensions={0} | all-to-all | bytes 4194304 | tf_op jit(solution)/shard_map/all_to_all | solution.py:48
  69.2 1.2 shard_map.116
  70.4 8.4 %all_to_all.36.kv_ref = bf16[4,64,256]{2,1,0:T(8,128)(2,1)S(1)} all-to-all(bf16[4,64,256]{2,1,0:T(8,128)(2,1)S(1)} %get-tuple-element.22), channel_id=1, replica_groups={{0,2,4,6},{8,10,12,14},{16,18,20,22},{24,26,28,30},{1,3,5,7},{9,11,13,1..., dimensions={0} | all-to-all | bytes 262144 | tf_op jit(solution)/shard_map/all_to_all | solution.py:52
  78.8 2.1 %shard_map.117 = (bf16[128,256]{1,0:T(8,128)(2,1)S(1)}, bf16[128,256]{1,0:T(8,128)(2,1)S(1)}, f32[4,64,128]{2,1,0:T(8,128)S(1)}, f32[8,128]{1,0:T(8,128)S(1)}) custom-call(bf16[4,1024,256]{2,1,0:T(8,128)(2,1)S(1)} %all_to_all.35.back_ref, bf16[16,256,256]{2,1,0:T(8,128)(2,1)S(1)} %get-tuple-element.21.normed_ref, bf16[4,64,256]{2,1,0:T(8,128)(2,1)S(1)} %all_to_all.36.kv_ref, ...), custom_call_target="tpu_custom_call" | custom-call | flops 805306368 | bytes 8982528 | tf_op jit(solution)/shard_map/pallas_call | solution.py:60
  80.8 7.2 %all_to_all.37.grad_kv_ref = f32[4,64,128]{2,1,0:T(8,128)S(1)} all-to-all(f32[4,64,128]{2,1,0:T(8,128)S(1)} %get-tuple-element.25), channel_id=1, replica_groups={{0,2,4,6},{8,10,12,14},{16,18,20,22},{24,26,28,30},{1,3,5,7},{9,11,13,1..., dimensions={0} | all-to-all | bytes 262144 | tf_op jit(solution)/shard_map/all_to_all | solution.py:52
  88.0 1.4 shard_map.118
  89.4 18.0 %all_to_all.38.parts_ref = bf16[4,1040,256]{2,1,0:T(8,128)(2,1)S(1)} all-to-all(bf16[4,1040,256]{2,1,0:T(8,128)(2,1)S(1)} %shard_map.118), channel_id=1, replica_groups={{0,8,16,24},{2,10,18,26},{4,12,20,28},{6,14,22,30},{1,9,17,25},{3,11,19..., dimensions={0} | all-to-all | bytes 4259840 | tf_op jit(solution)/shard_map/all_to_all | solution.py:52
  107.3 0.3 shard_map.119
  107.6 12.2 %all_to_all.39.parts_ref = bf16[4,272,256]{2,1,0:T(8,128)(2,1)S(1)} all-to-all(bf16[4,272,256]{2,1,0:T(8,128)(2,1)S(1)} %shard_map.119), channel_id=1, replica_groups={{0,2,4,6},{8,10,12,14},{16,18,20,22},{24,26,28,30},{1,3,5,7},{9,11,13,1..., dimensions={0} | all-to-all | bytes 1114112 | tf_op jit(solution)/shard_map/all_to_all | solution.py:52
  120.0 16.9 %collective-permute-start.2 = (bf16[128,256]{1,0:T(8,128)(2,1)S(1)}, bf16[128,256]{1,0:T(8,128)(2,1)S(1)}, u32[]{:S(2)}, u32[]{:S(2)}) collective-permute-start(bf16[128,256]{1,0:T(8,128)(2,1)S(1)} %get-tuple-element.29), channel_id=1, source_target_pairs={{0,32},{32,64},{64,96},{96,128},{128,160},{160,192},{192,224},{224... | collective-permute-start | bytes 196616 | tf_op jit(solution)/shard_map/ppermute | solution.py:427
  136.9 2.5 %collective-permute-start.3 = (bf16[128,256]{1,0:T(8,128)(2,1)S(1)}, bf16[128,256]{1,0:T(8,128)(2,1)S(1)}, u32[]{:S(2)}, u32[]{:S(2)}) collective-permute-start(bf16[128,256]{1,0:T(8,128)(2,1)S(1)} %get-tuple-element.30), channel_id=1, source_target_pairs={{32,0},{64,32},{96,64},{128,96},{160,128},{192,160},{224,192},{256... | collective-permute-start | bytes 196616 | tf_op jit(solution)/shard_map/ppermute | solution.py:428
  139.4 3.1 %collective-permute-done.3.grad_ref = bf16[128,256]{1,0:T(8,128)(2,1)S(1)} collective-permute-done((bf16[128,256]{1,0:T(8,128)(2,1)S(1)}, bf16[128,256]{1,0:T(8,128)(2,1)S(1)}, u32[]{:S(2)}, u32[]{:S(2)}) %collective-permute-start.3) | collective-permute-done | bytes 65568 | tf_op jit(solution)/shard_map/ppermute | solution.py:428
  142.5 0.7 shard_map.121
  (20 shorter events, 0.5 us)
Async XLA Ops:
  0.6 0.9 copy-start
  0.6 15.7 %copy-start.5 = (bf16[1,128,256]{2,1,0:T(8,128)(2,1)S(1)}, bf16[1,128,256]{2,1,0:T(8,128)(2,1)}, u32[]{:S(2)}) copy-start(bf16[1,128,256]{2,1,0:T(8,128)(2,1)} %param.9) | copy-start | bytes 196612
  1.6 14.7 %collective-permute-start = (bf16[128,256]{1,0:T(8,128)(2,1)S(1)}, bf16[128,256]{1,0:T(8,128)(2,1)S(1)}, u32[]{:S(2)}, u32[]{:S(2)}) collective-permute-start(bf16[128,256]{1,0:T(8,128)(2,1)S(1)} %dynamic-slice_bitcast_fusion), channel_id=1, source_target_pairs={{480,0},{448,32},{416,64},{384,96},{352,128},{320,160},{288,192},{... | collective-permute-start | bytes 196616 | tf_op jit(solution)/shard_map/ppermute | solution.py:362
  5.0 13.4 %all-to-all-start = ((bf16[4,400,256]{2,1,0:T(8,128)(2,1)}), bf16[4,400,256]{2,1,0:T(8,128)(2,1)S(1)}, u32[]{:S(2)}, u32[]{:S(2)}) async-start(bf16[4,400,256]{2,1,0:T(8,128)(2,1)} %shard_map.112), calls=%async_computation | async-start | bytes 1638400 | tf_op jit(solution)/shard_map/all_to_all | solution.py:48
  9.9 8.5 %copy-start.6 = (bf16[1,128,256]{2,1,0:T(8,128)(2,1)S(1)}, bf16[1,128,256]{2,1,0:T(8,128)(2,1)}, u32[]{:S(2)}) copy-start(bf16[1,128,256]{2,1,0:T(8,128)(2,1)} %param.12) | copy-start | bytes 196612
  18.6 1.3 copy-start.1
  19.9 31.1 %all-to-all-start.1 = ((bf16[4,1040,256]{2,1,0:T(8,128)(2,1)}), bf16[4,1040,256]{2,1,0:T(8,128)(2,1)S(1)}, u32[]{:S(2)}, u32[]{:S(2)}) async-start(bf16[4,1040,256]{2,1,0:T(8,128)(2,1)} %copy-done.1), calls=%async_computation.1 | async-start | bytes 4259840 | tf_op jit(solution)/shard_map/all_to_all | solution.py:48
  24.5 18.0 %collective-permute-start.1 = (bf16[128,256]{1,0:T(8,128)(2,1)S(1)}, bf16[128,256]{1,0:T(8,128)(2,1)S(1)}, u32[]{:S(2)}, u32[]{:S(2)}) collective-permute-start(bf16[128,256]{1,0:T(8,128)(2,1)S(1)} %bitcast.20), channel_id=1, source_target_pairs={{0,480},{32,448},{64,416},{96,384},{128,352},{160,320},{192,288},{... | collective-permute-start | bytes 196616 | tf_op jit(solution)/shard_map/ppermute | solution.py:384
  51.1 18.1 %copy-start.4 = (f32[384,128]{1,0:T(8,128)S(1)}, f32[384,128]{1,0:T(8,128)}, u32[]{:S(2)}) copy-start(f32[384,128]{1,0:T(8,128)} %constant.9.clone.table_ref) | copy-start | bytes 589828
  69.2 9.5 %copy-start.2 = (bf16[1,4096,256]{2,1,0:T(8,128)(2,1)S(1)}, bf16[1,4096,256]{2,1,0:T(8,128)(2,1)}, u32[]{:S(2)}) copy-start(bf16[1,4096,256]{2,1,0:T(8,128)(2,1)} %param.14) | copy-start | bytes 6291460
  69.2 9.5 %copy-start.3 = (bf16[1,256,4096]{2,1,0:T(8,128)(2,1)S(1)}, bf16[1,256,4096]{2,1,0:T(8,128)(2,1)}, u32[]{:S(2)}) copy-start(bf16[1,256,4096]{2,1,0:T(8,128)(2,1)} %param.16) | copy-start | bytes 6291460
  107.3 12.4 %copy-start.7 = (f32[1,256]{1,0:T(1,128)S(1)}, f32[1,256]{1,0:T(1,128)}, u32[]{:S(2)}) copy-start(f32[1,256]{1,0:T(1,128)} %gain_ref.1) | copy-start | bytes 3076
  120.0 19.4 %collective-permute-start.2 = (bf16[128,256]{1,0:T(8,128)(2,1)S(1)}, bf16[128,256]{1,0:T(8,128)(2,1)S(1)}, u32[]{:S(2)}, u32[]{:S(2)}) collective-permute-start(bf16[128,256]{1,0:T(8,128)(2,1)S(1)} %get-tuple-element.29), channel_id=1, source_target_pairs={{0,32},{32,64},{64,96},{96,128},{128,160},{160,192},{192,224},{224... | collective-permute-start | bytes 196616 | tf_op jit(solution)/shard_map/ppermute | solution.py:427
  136.9 5.6 %collective-permute-start.3 = (bf16[128,256]{1,0:T(8,128)(2,1)S(1)}, bf16[128,256]{1,0:T(8,128)(2,1)S(1)}, u32[]{:S(2)}, u32[]{:S(2)}) collective-permute-start(bf16[128,256]{1,0:T(8,128)(2,1)S(1)} %get-tuple-element.30), channel_id=1, source_target_pairs={{32,0},{64,32},{96,64},{128,96},{160,128},{192,160},{224,192},{256... | collective-permute-start | bytes 196616 | tf_op jit(solution)/shard_map/ppermute | solution.py:428

commit v8 on v7

--- a/solution.py
+++ b/solution.py
@@ -95,7 +95,7 @@
         columns = pl.ds(side * half, half)
         pairs.append((sources[2].at[:, columns], kvw_ref.at[:, columns]))
     copies = [pltpu.make_async_copy(a, b, sems.at[n]) for n, (a, b) in enumerate(pairs)]
-    for copy in copies:
+    for copy in copies[2:] + copies[:2]:
         copy.start()
     for copy in copies[:2]:
         copy.wait()

time: 145 us -> 145 us (level)
  no operation moved by 1% of the time
where the time goes in v8:
time: 145 us; the launch traced here: 143 us
  blocking collectives  63.8 us (44%)
  starting transfers between devices  46.8 us (32%)
  waiting for transfers between devices  21.4 us (15%)
  Pallas kernels  8.2 us (6%)
  local copies, waits for them, and re-layouts  1.59 us (1%)
  between operations  1.45 us (1%)
    all_to_all x4, blocking collectives, exchange_row(): lax.all_to_all(blocks, 'tensor', 0, 0, axis_index_groups=tensor_rows(1 -...  45.7 us
    all_to_all x1, blocking collectives, exchange(): lax.all_to_all(blocks, ('section', 'tensor'), 0, 0, axis_index_groups=gro...  18.1 us
    ppermute x1, starting transfers between devices, per_device(): lax.ppermute(layer_out, 'section', [(s, s + 1) for s in range(section_cou...  16.9 us
    ppermute x1, starting transfers between devices, per_device(): lax.ppermute(evicting, 'section', [(s, section_count - 1 - s) for s in ra...  16.7 us
    all_to_all x2, waiting for transfers between devices, exchange(): lax.all_to_all(blocks, ('section', 'tensor'), 0, 0, axis_index_groups=gro...  10.6 us
    all_to_all x2, starting transfers between devices, exchange(): lax.all_to_all(blocks, ('section', 'tensor'), 0, 0, axis_index_groups=gro...  9.44 us
    pallas_call x10, Pallas kernels, call(): pl.pallas_call(kernel, out_shape=outs, in_specs=[pl.BlockSpec(memory_spac...  8.2 us
    ppermute x1, waiting for transfers between devices, per_device(): lax.ppermute(picked, 'section', [(section_count - 1 - s, s) for s in rang...  6.4 us
  transfers between devices with their start and end apart: 6, of which 5 were waited for; matrix products, arithmetic and copies ran while one was open for 0% of the time, Pallas kernels for 2%

profile of v8, /device:TPU:1, one launch (start us, length us, event | category | flops | bytes accessed | tf_op | source)
XLA Modules:
  0.0 143.2 jit_solution(6776167640775452303)
XLA Ops:
  1.3 0.2 copy-done
  1.6 1.3 collective-permute-start
  2.9 2.2 %shard_map.112 = bf16[4,400,256]{2,1,0:T(8,128)(2,1)} custom-call(bf16[128,256]{1,0:T(8,128)(2,1)} %bitcast.18, f32[1,256]{1,0:T(1,128)} %gain_ref.1, bf16[256,1024]{1,0:T(8,128)(2,1)} %bitcast.24), custom_call_target="tpu_custom_call" | custom-call | bytes 1410048 | tf_op jit(solution)/shard_map/pallas_call | solution.py:60
  5.1 4.9 %all-to-all-start = ((bf16[4,400,256]{2,1,0:T(8,128)(2,1)}), bf16[4,400,256]{2,1,0:T(8,128)(2,1)S(1)}, u32[]{:S(2)}, u32[]{:S(2)}) async-start(bf16[4,400,256]{2,1,0:T(8,128)(2,1)} %shard_map.112), calls=%async_computation | async-start | bytes 1638400 | tf_op jit(solution)/shard_map/all_to_all | solution.py:48
  9.9 6.4 %collective-permute-done.reloaded_ref = bf16[128,256]{1,0:T(8,128)(2,1)S(1)} collective-permute-done((bf16[128,256]{1,0:T(8,128)(2,1)S(1)}, bf16[128,256]{1,0:T(8,128)(2,1)S(1)}, u32[]{:S(2)}, u32[]{:S(2)}) %collective-permute-start) | collective-permute-done | bytes 65568 | tf_op jit(solution)/shard_map/ppermute | solution.py:362
  16.3 2.1 %all-to-all-done.parts_ref = bf16[4,400,256]{2,1,0:T(8,128)(2,1)S(1)} async-done(((bf16[4,400,256]{2,1,0:T(8,128)(2,1)}), bf16[4,400,256]{2,1,0:T(8,128)(2,1)S(1)}, u32[]{:S(2)}, u32[]{:S(2)}) %all-to-all-start) | async-done | bytes 819232 | tf_op jit(solution)/shard_map/all_to_all | solution.py:48
  18.6 1.3 copy-done.1
  19.9 4.6 %all-to-all-start.1 = ((bf16[4,1040,256]{2,1,0:T(8,128)(2,1)}), bf16[4,1040,256]{2,1,0:T(8,128)(2,1)S(1)}, u32[]{:S(2)}, u32[]{:S(2)}) async-start(bf16[4,1040,256]{2,1,0:T(8,128)(2,1)} %copy-done.1), calls=%async_computation.1 | async-start | bytes 4259840 | tf_op jit(solution)/shard_map/all_to_all | solution.py:48
  24.5 16.7 %collective-permute-start.1 = (bf16[128,256]{1,0:T(8,128)(2,1)S(1)}, bf16[128,256]{1,0:T(8,128)(2,1)S(1)}, u32[]{:S(2)}, u32[]{:S(2)}) collective-permute-start(bf16[128,256]{1,0:T(8,128)(2,1)S(1)} %bitcast.20), channel_id=1, source_target_pairs={{0,480},{32,448},{64,416},{96,384},{128,352},{160,320},{192,288},{... | collective-permute-start | bytes 196616 | tf_op jit(solution)/shard_map/ppermute | solution.py:384
  41.2 1.3 collective-permute-done.1.evicted_ref
  42.5 8.5 %all-to-all-done.1.parts_ref.rows_ref = bf16[4,1040,256]{2,1,0:T(8,128)(2,1)S(1)} async-done(((bf16[4,1040,256]{2,1,0:T(8,128)(2,1)}), bf16[4,1040,256]{2,1,0:T(8,128)(2,1)S(1)}, u32[]{:S(2)}, u32[]{:S(2)}) %all-to-all-start.1) | async-done | bytes 2129952 | tf_op jit(solution)/shard_map/all_to_all | solution.py:48
  51.1 18.1 %all_to_all.35.back_ref = bf16[4,1024,256]{2,1,0:T(8,128)(2,1)S(1)} all-to-all(bf16[4,1024,256]{2,1,0:T(8,128)(2,1)S(1)} %shard_map.115), channel_id=1, replica_groups={{0,2,4,6},{8,10,12,14},{16,18,20,22},{24,26,28,30},{32,40,48,56},{34,42..., dimensions={0} | all-to-all | bytes 4194304 | tf_op jit(solution)/shard_map/all_to_all | solution.py:48
  69.3 1.2 shard_map.116
  70.4 8.4 %all_to_all.36.kv_ref = bf16[4,64,256]{2,1,0:T(8,128)(2,1)S(1)} all-to-all(bf16[4,64,256]{2,1,0:T(8,128)(2,1)S(1)} %get-tuple-element.22), channel_id=1, replica_groups={{0,2,4,6},{8,10,12,14},{16,18,20,22},{24,26,28,30},{1,3,5,7},{9,11,13,1..., dimensions={0} | all-to-all | bytes 262144 | tf_op jit(solution)/shard_map/all_to_all | solution.py:52
  78.8 2.1 %shard_map.117 = (bf16[128,256]{1,0:T(8,128)(2,1)S(1)}, bf16[128,256]{1,0:T(8,128)(2,1)S(1)}, f32[4,64,128]{2,1,0:T(8,128)S(1)}, f32[8,128]{1,0:T(8,128)S(1)}) custom-call(bf16[4,1024,256]{2,1,0:T(8,128)(2,1)S(1)} %all_to_all.35.back_ref, bf16[16,256,256]{2,1,0:T(8,128)(2,1)S(1)} %get-tuple-element.21.normed_ref, bf16[4,64,256]{2,1,0:T(8,128)(2,1)S(1)} %all_to_all.36.kv_ref, ...), custom_call_target="tpu_custom_call" | custom-call | flops 805306368 | bytes 8982528 | tf_op jit(solution)/shard_map/pallas_call | solution.py:60
  80.9 7.2 %all_to_all.37.grad_kv_ref = f32[4,64,128]{2,1,0:T(8,128)S(1)} all-to-all(f32[4,64,128]{2,1,0:T(8,128)S(1)} %get-tuple-element.25), channel_id=1, replica_groups={{0,2,4,6},{8,10,12,14},{16,18,20,22},{24,26,28,30},{1,3,5,7},{9,11,13,1..., dimensions={0} | all-to-all | bytes 262144 | tf_op jit(solution)/shard_map/all_to_all | solution.py:52
  88.0 1.4 shard_map.118
  89.4 18.0 %all_to_all.38.parts_ref = bf16[4,1040,256]{2,1,0:T(8,128)(2,1)S(1)} all-to-all(bf16[4,1040,256]{2,1,0:T(8,128)(2,1)S(1)} %shard_map.118), channel_id=1, replica_groups={{0,8,16,24},{2,10,18,26},{4,12,20,28},{6,14,22,30},{1,9,17,25},{3,11,19..., dimensions={0} | all-to-all | bytes 4259840 | tf_op jit(solution)/shard_map/all_to_all | solution.py:52
  107.4 0.3 shard_map.119
  107.6 12.2 %all_to_all.39.parts_ref = bf16[4,272,256]{2,1,0:T(8,128)(2,1)S(1)} all-to-all(bf16[4,272,256]{2,1,0:T(8,128)(2,1)S(1)} %shard_map.119), channel_id=1, replica_groups={{0,2,4,6},{8,10,12,14},{16,18,20,22},{24,26,28,30},{1,3,5,7},{9,11,13,1..., dimensions={0} | all-to-all | bytes 1114112 | tf_op jit(solution)/shard_map/all_to_all | solution.py:52
  120.0 16.9 %collective-permute-start.2 = (bf16[128,256]{1,0:T(8,128)(2,1)S(1)}, bf16[128,256]{1,0:T(8,128)(2,1)S(1)}, u32[]{:S(2)}, u32[]{:S(2)}) collective-permute-start(bf16[128,256]{1,0:T(8,128)(2,1)S(1)} %get-tuple-element.29), channel_id=1, source_target_pairs={{0,32},{32,64},{64,96},{96,128},{128,160},{160,192},{192,224},{224... | collective-permute-start | bytes 196616 | tf_op jit(solution)/shard_map/ppermute | solution.py:427
  136.9 2.5 %collective-permute-start.3 = (bf16[128,256]{1,0:T(8,128)(2,1)S(1)}, bf16[128,256]{1,0:T(8,128)(2,1)S(1)}, u32[]{:S(2)}, u32[]{:S(2)}) collective-permute-start(bf16[128,256]{1,0:T(8,128)(2,1)S(1)} %get-tuple-element.30), channel_id=1, source_target_pairs={{32,0},{64,32},{96,64},{128,96},{160,128},{192,160},{224,192},{256... | collective-permute-start | bytes 196616 | tf_op jit(solution)/shard_map/ppermute | solution.py:428
  139.4 3.1 %collective-permute-done.3.grad_ref = bf16[128,256]{1,0:T(8,128)(2,1)S(1)} collective-permute-done((bf16[128,256]{1,0:T(8,128)(2,1)S(1)}, bf16[128,256]{1,0:T(8,128)(2,1)S(1)}, u32[]{:S(2)}, u32[]{:S(2)}) %collective-permute-start.3) | collective-permute-done | bytes 65568 | tf_op jit(solution)/shard_map/ppermute | solution.py:428
  142.5 0.7 shard_map.121
  (20 shorter events, 0.5 us)
Async XLA Ops:
  0.6 0.9 copy-start
  0.6 15.7 %copy-start.5 = (bf16[1,128,256]{2,1,0:T(8,128)(2,1)S(1)}, bf16[1,128,256]{2,1,0:T(8,128)(2,1)}, u32[]{:S(2)}) copy-start(bf16[1,128,256]{2,1,0:T(8,128)(2,1)} %param.9) | copy-start | bytes 196612
  1.6 14.7 %collective-permute-start = (bf16[128,256]{1,0:T(8,128)(2,1)S(1)}, bf16[128,256]{1,0:T(8,128)(2,1)S(1)}, u32[]{:S(2)}, u32[]{:S(2)}) collective-permute-start(bf16[128,256]{1,0:T(8,128)(2,1)S(1)} %dynamic-slice_bitcast_fusion), channel_id=1, source_target_pairs={{480,0},{448,32},{416,64},{384,96},{352,128},{320,160},{288,192},{... | collective-permute-start | bytes 196616 | tf_op jit(solution)/shard_map/ppermute | solution.py:362
  5.1 13.4 %all-to-all-start = ((bf16[4,400,256]{2,1,0:T(8,128)(2,1)}), bf16[4,400,256]{2,1,0:T(8,128)(2,1)S(1)}, u32[]{:S(2)}, u32[]{:S(2)}) async-start(bf16[4,400,256]{2,1,0:T(8,128)(2,1)} %shard_map.112), calls=%async_computation | async-start | bytes 1638400 | tf_op jit(solution)/shard_map/all_to_all | solution.py:48
  9.9 8.5 %copy-start.6 = (bf16[1,128,256]{2,1,0:T(8,128)(2,1)S(1)}, bf16[1,128,256]{2,1,0:T(8,128)(2,1)}, u32[]{:S(2)}) copy-start(bf16[1,128,256]{2,1,0:T(8,128)(2,1)} %param.12) | copy-start | bytes 196612
  18.6 1.3 copy-start.1
  19.9 31.1 %all-to-all-start.1 = ((bf16[4,1040,256]{2,1,0:T(8,128)(2,1)}), bf16[4,1040,256]{2,1,0:T(8,128)(2,1)S(1)}, u32[]{:S(2)}, u32[]{:S(2)}) async-start(bf16[4,1040,256]{2,1,0:T(8,128)(2,1)} %copy-done.1), calls=%async_computation.1 | async-start | bytes 4259840 | tf_op jit(solution)/shard_map/all_to_all | solution.py:48
  24.5 18.0 %collective-permute-start.1 = (bf16[128,256]{1,0:T(8,128)(2,1)S(1)}, bf16[128,256]{1,0:T(8,128)(2,1)S(1)}, u32[]{:S(2)}, u32[]{:S(2)}) collective-permute-start(bf16[128,256]{1,0:T(8,128)(2,1)S(1)} %bitcast.20), channel_id=1, source_target_pairs={{0,480},{32,448},{64,416},{96,384},{128,352},{160,320},{192,288},{... | collective-permute-start | bytes 196616 | tf_op jit(solution)/shard_map/ppermute | solution.py:384
  51.1 18.1 %copy-start.4 = (f32[384,128]{1,0:T(8,128)S(1)}, f32[384,128]{1,0:T(8,128)}, u32[]{:S(2)}) copy-start(f32[384,128]{1,0:T(8,128)} %constant.9.clone.table_ref) | copy-start | bytes 589828
  69.2 9.5 %copy-start.2 = (bf16[1,4096,256]{2,1,0:T(8,128)(2,1)S(1)}, bf16[1,4096,256]{2,1,0:T(8,128)(2,1)}, u32[]{:S(2)}) copy-start(bf16[1,4096,256]{2,1,0:T(8,128)(2,1)} %param.14) | copy-start | bytes 6291460
  69.2 9.5 %copy-start.3 = (bf16[1,256,4096]{2,1,0:T(8,128)(2,1)S(1)}, bf16[1,256,4096]{2,1,0:T(8,128)(2,1)}, u32[]{:S(2)}) copy-start(bf16[1,256,4096]{2,1,0:T(8,128)(2,1)} %param.16) | copy-start | bytes 6291460
  107.4 12.5 %copy-start.7 = (f32[1,256]{1,0:T(1,128)S(1)}, f32[1,256]{1,0:T(1,128)}, u32[]{:S(2)}) copy-start(f32[1,256]{1,0:T(1,128)} %gain_ref.1) | copy-start | bytes 3076
  120.0 19.4 %collective-permute-start.2 = (bf16[128,256]{1,0:T(8,128)(2,1)S(1)}, bf16[128,256]{1,0:T(8,128)(2,1)S(1)}, u32[]{:S(2)}, u32[]{:S(2)}) collective-permute-start(bf16[128,256]{1,0:T(8,128)(2,1)S(1)} %get-tuple-element.29), channel_id=1, source_target_pairs={{0,32},{32,64},{64,96},{96,128},{128,160},{160,192},{192,224},{224... | collective-permute-start | bytes 196616 | tf_op jit(solution)/shard_map/ppermute | solution.py:427
  136.9 5.6 %collective-permute-start.3 = (bf16[128,256]{1,0:T(8,128)(2,1)S(1)}, bf16[128,256]{1,0:T(8,128)(2,1)S(1)}, u32[]{:S(2)}, u32[]{:S(2)}) collective-permute-start(bf16[128,256]{1,0:T(8,128)(2,1)S(1)} %get-tuple-element.30), channel_id=1, source_target_pairs={{32,0},{64,32},{96,64},{128,96},{160,128},{192,160},{224,192},{256... | collective-permute-start | bytes 196616 | tf_op jit(solution)/shard_map/ppermute | solution.py:428
